TPU v7x, 256 devices: a whole 4x4x8 slice. The times are simulated.
256 devices in a mesh: leaf: 128 (over z, y, x), sub: 2 (over core).
Axes of the slice: x: 4, y: 4, z: 8, core: 2. Of those that a mesh axis runs over, the one named last changes fastest.
Arguments:
- points: bfloat16 [8, 65536], P(None, ('leaf', 'sub')), may hold values from 0 to 1
- omega: bfloat16 [128, 65536], P(None, ('leaf', 'sub')), may hold values from -6 to 6
- tree_order: int32 [65536], P(('leaf', 'sub')), may hold values from 0 to 65535, as said below
- sibling_blocks: int32 [128, 16], P('leaf'), may hold values from 0 to 127, as said below
- cousin_blocks: int32 [128, 32], P('leaf'), may hold values from 0 to 127, as said below
- skeleton: int32 [4, 256], replicated, may hold values from 0 to 65535, as said below
Outputs:
- node_basis: float32 [65536, 256], P(('leaf', 'sub'))
- coupling: float32 [2, 256, 256], replicated
Inputs may be any that keep to these rules, and one draw needn't show every extreme that they name: tree_order maps each aligned group of 256 rows onto itself, a permutation inside each group. `sibling_blocks`: row b holds 16 different blocks of the sibling of b's node of 32 blocks, whose index is (b // 32) xor 1. `cousin_blocks`: row b holds 32 different blocks of the half of the blocks that does not hold b. `skeleton`: row c holds 256 different tree rows of node c.
All inputs are finite; a program needn't handle non-finite values.
Results may differ from a plain program's by a relative error of at most 0.0043.
Values may be sent and summed in bfloat16 or wider, within the bound.
A program may use at most 128 MiB of HBM per device.

v0:
```python
import math

import jax
import jax.numpy as jnp
from jax import lax
from jax.sharding import PartitionSpec as P

SPREAD = 2.0
SHIFT = 0.01
HIGHEST = lax.Precision.HIGHEST


def kernel_values(row_points, col_points):
    inner_products = lax.dot_general(
        row_points, col_points, (((0,), (0,)), ((), ())), precision=HIGHEST
    )
    distance = (
        jnp.sum(row_points * row_points, axis=0)[:, None]
        + jnp.sum(col_points * col_points, axis=0)[None, :]
        - 2.0 * inner_products
    )
    return jnp.exp(-SPREAD * distance)


def cholesky_factor(gram_matrix):
    shifted = gram_matrix + SHIFT * jnp.trace(gram_matrix) * jnp.eye(
        gram_matrix.shape[0], dtype=jnp.float32
    )
    return jnp.linalg.cholesky(shifted)


def right_solve(lower_part, values, factor):
    return factor * jax.scipy.linalg.solve_triangular(lower_part, values.T, lower=True).T


def sample_fold(row_points, block_span, sibling, cousin, totals, shard_piece):
    piece_points, piece_omega = shard_piece
    length = piece_points.shape[1]
    stride = 2048

    def add_block(number, running):
        offset = number * stride
        col_points = lax.dynamic_slice_in_dim(piece_points, offset, stride, 1).astype(jnp.float32)
        col_omega = lax.dynamic_slice_in_dim(piece_omega, offset, stride, 1)
        owners = (offset + lax.iota(jnp.int32, stride)) // block_span
        near_hit = jnp.sum((owners[None, :] == sibling[:, None]).astype(jnp.int32), axis=0).astype(
            jnp.bfloat16
        )
        far_hit = jnp.sum((owners[None, :] == cousin[:, None]).astype(jnp.int32), axis=0).astype(
            jnp.bfloat16
        )
        weighted = jnp.concatenate(
            [col_omega * near_hit[None, :], col_omega * far_hit[None, :]], axis=0
        )
        kernel_block = kernel_values(row_points, col_points).astype(jnp.bfloat16)
        return running + lax.dot_general(
            kernel_block, weighted, (((1,), (1,)), ((), ())), preferred_element_type=jnp.float32
        )

    return lax.fori_loop(0, length // stride, add_block, totals)


def body(points, omega, tree_order, sibling_blocks, cousin_blocks, skeleton):
    local_rows = points.shape[1]
    leaf_count = lax.axis_size("leaf")
    core_count = lax.axis_size("sub")
    local_order = tree_order % local_rows
    tree_points = jnp.take(points, local_order, axis=1)
    tree_omega = jnp.take(omega, local_order, axis=1)
    sibling = sibling_blocks[0]
    cousin = cousin_blocks[0]
    columns_out = 2 * omega.shape[0]
    leaf_index = lax.axis_index("leaf")
    core_index = lax.axis_index("sub")
    own_points = tree_points.astype(jnp.float32)
    zero_start = jnp.zeros((local_rows, columns_out), jnp.float32)
    samples = sample_fold(
        own_points,
        local_rows * core_count,
        sibling,
        cousin,
        zero_start,
        (
            lax.all_gather(tree_points, ("leaf", "sub"), axis=1, tiled=True),
            lax.all_gather(tree_omega, ("leaf", "sub"), axis=1, tiled=True),
        ),
    )
    rank_width = samples.shape[1]
    group_blocks = leaf_count // 4
    node_index = leaf_index // group_blocks
    factor = math.sqrt(leaf_count * core_count * local_rows // 4)
    row_ids = (leaf_index * core_count + core_index) * local_rows + lax.iota(jnp.int32, local_rows)
    selector = (skeleton.reshape(-1)[:, None] == row_ids[None, :]).astype(jnp.float32)
    skel_local = lax.dot_general(
        tree_points.astype(jnp.float32), selector, (((1,), (1,)), ((), ())), precision=HIGHEST
    )
    gram_local = lax.dot_general(samples, samples, (((0,), (0,)), ((), ())), precision=HIGHEST)
    slots = (jnp.arange(4) == node_index).astype(jnp.float32)[:, None, None] * gram_local[None]
    skel_samples = jnp.dot(selector, samples, precision=HIGHEST)
    tables, skel_rows, skel_points = lax.psum((slots, skel_samples, skel_local), ("leaf", "sub"))
    lowers = [cholesky_factor(tables[member]) for member in range(4)]
    stacked = jnp.stack(lowers)
    node_basis = right_solve(stacked[node_index], samples, factor)
    reduced = [
        right_solve(
            lowers[member], skel_rows[member * rank_width : (member + 1) * rank_width], factor
        )
        for member in range(4)
    ]
    couplings = []
    for couple in range(2):
        left_points = skel_points[:, 2 * couple * rank_width : (2 * couple + 1) * rank_width]
        right_points = skel_points[:, (2 * couple + 1) * rank_width : (2 * couple + 2) * rank_width]
        kernel_skel = kernel_values(left_points, right_points)
        middle = jnp.dot(kernel_skel, reduced[2 * couple + 1], precision=HIGHEST)
        couplings.append(
            jnp.dot(reduced[2 * couple].T, middle, precision=HIGHEST) / math.sqrt(rank_width)
        )
    return (node_basis, jnp.stack(couplings))


def solution(mesh):
    return jax.shard_map(
        body,
        mesh=mesh,
        in_specs=(
            P(None, ("leaf", "sub")),
            P(None, ("leaf", "sub")),
            P(("leaf", "sub")),
            P("leaf", None),
            P("leaf", None),
            P(),
        ),
        out_specs=(P(("leaf", "sub"), None), P()),
        check_vma=False,
    )
```

profile of v0, /device:TPU:1, one launch (start us, length us, event | category | flops | bytes accessed | tf_op | source)
XLA Modules:
  0.0 1003.6 jit_solution(16535030341943430783)
XLA Ops:
  14.7 126.6 %all-gather.3.cloned.1.call-done = bf16[8,65536]{0,1:T(8,128)(2,1)} async-done(((bf16[8,256]{0,1:T(8,128)(2,1)}), bf16[8,65536]{0,1:T(8,128)(2,1)}) %all-gather.3.cloned.1.call-update) | async-done | bytes 1048592 | tf_op jit(solution)/shard_map/all_gather | solution.py:84
  141.3 12.2 %copy.21 = bf16[8,65536]{1,0:T(8,128)(2,1)S(1)} copy(bf16[8,65536]{0,1:T(8,128)(2,1)} %all-gather.3.cloned.1.call-done) | data formatting | bytes 2097152
  153.5 114.1 %all-gather.5.cloned.1.call-done = bf16[128,65536]{0,1:T(8,128)(2,1)} async-done(((bf16[128,256]{0,1:T(8,128)(2,1)}), bf16[128,65536]{0,1:T(8,128)(2,1)}) %all-gather.5.cloned.1.call-update) | async-done | bytes 16777232 | tf_op jit(solution)/shard_map/all_gather | solution.py:85
  267.6 187.3 %while.26 = (s32[]{:T(128)}, f32[256,256]{1,0:T(8,128)S(1)}, f32[256]{0:T(256)S(1)}, bf16[8,65536]{1,0:T(8,128)(2,1)S(1)}, f32[8,256]{1,0:T(8,128)S(1)}, /*index...) while((s32[]{:T(128)}, f32[256,256]{1,0:T(8,128)S(1)}, ...), condition=%wide.region_5.6_spmd.clone, body=%wide.region_1.5_spmd.clone.sunk | while | flops 324515840 | bytes 7505285 | solution.py:60
  267.6 2.4 fusion.161
  273.5 2.4 fusion.161
  277.5 1.8 convolution_add_fusion.2
  279.3 2.4 fusion.161
  285.2 2.4 fusion.161
  289.2 1.8 convolution_add_fusion.2
  291.0 2.4 fusion.161
  295.1 1.8 convolution_add_fusion.2
  296.9 2.4 fusion.161
  302.7 2.4 fusion.161
  308.6 2.4 fusion.161
  314.4 2.4 fusion.161
  320.3 2.4 fusion.161
  326.1 2.4 fusion.161
  332.0 2.4 fusion.161
  337.9 2.4 fusion.161
  343.7 2.4 fusion.161
  349.6 2.4 fusion.161
  355.4 2.4 fusion.161
  361.3 2.4 fusion.161
  367.1 2.4 fusion.161
  373.0 2.4 fusion.161
  378.8 2.4 fusion.161
  384.7 2.4 fusion.161
  390.5 2.4 fusion.161
  396.4 2.4 fusion.161
  402.2 2.4 fusion.161
  408.1 2.4 fusion.161
  413.9 2.4 fusion.161
  419.8 2.4 fusion.161
  425.6 2.4 fusion.161
  431.5 2.4 fusion.161
  437.3 2.4 fusion.161
  443.2 2.4 fusion.161
  449.1 2.4 fusion.161
  458.7 74.9 %psum.23 = f32[8,1024]{1,0:T(8,128)S(1)} all-reduce(f32[8,1024]{1,0:T(8,128)S(1)} %fusion.14), channel_id=1, replica_groups=mesh['leaf'=128,'sub'=2] {'leaf','sub'}, use_global_device_ids=true, to_apply=%region_16.19 | all-reduce | flops 8192 | bytes 65536 | tf_op jit(solution)/shard_map/psum | solution.py:100
  535.9 179.8 %all-reduce.4.cloned.1.call-done = (f32[4,256,256]{1,2,0:T(8,128)}, f32[1024,256]{1,0:T(8,128)}) async-done(((f32[4,256,256]{1,2,0:T(8,128)}, f32[1024,256]{1,0:T(8,128)}), (f32[4,256,256]{1,2,0:T(8,128)}, f32[1024,256]{1,0:T(8,128)})) %all-reduce.4.cloned.1.call-update) | async-done | bytes 2097168 | tf_op jit(solution)/shard_map/psum | solution.py:100
  715.7 1.9 select_reduce_fusion
  721.8 11.7 %cholesky.214 = f32[128,128]{1,0:T(8,128)S(1)} custom-call(f32[128,128]{1,0:T(8,128)S(1)} %cholesky.346), custom_call_target="Cholesky" | custom-call | tf_op jit(solution)/shard_map/jit(cholesky)/cholesky | solution.py:29
  733.5 9.8 custom-call.19
  743.8 11.7 %cholesky.231 = f32[128,128]{1,0:T(8,128)S(1)} custom-call(f32[128,128]{1,0:T(8,128)S(1)} %convolution_subtract_fusion.8), custom_call_target="Cholesky" | custom-call | tf_op jit(solution)/shard_map/jit(cholesky)/cholesky | solution.py:29
  756.9 12.1 %cholesky.248 = f32[128,128]{1,0:T(8,128)S(1)} custom-call(f32[128,128]{1,0:T(8,128)S(1)} %cholesky.349), custom_call_target="Cholesky" | custom-call | tf_op jit(solution)/shard_map/jit(cholesky)/cholesky | solution.py:29
  769.1 9.8 custom-call.20
  779.4 11.7 %cholesky.265 = f32[128,128]{1,0:T(8,128)S(1)} custom-call(f32[128,128]{1,0:T(8,128)S(1)} %convolution_subtract_fusion.7), custom_call_target="Cholesky" | custom-call | tf_op jit(solution)/shard_map/jit(cholesky)/cholesky | solution.py:29
  792.8 11.9 %cholesky.282 = f32[128,128]{1,0:T(8,128)S(1)} custom-call(f32[128,128]{1,0:T(8,128)S(1)} %cholesky.352), custom_call_target="Cholesky" | custom-call | tf_op jit(solution)/shard_map/jit(cholesky)/cholesky | solution.py:29
  804.7 9.8 custom-call.21
  815.0 11.7 %cholesky.299 = f32[128,128]{1,0:T(8,128)S(1)} custom-call(f32[128,128]{1,0:T(8,128)S(1)} %convolution_subtract_fusion.6), custom_call_target="Cholesky" | custom-call | tf_op jit(solution)/shard_map/jit(cholesky)/cholesky | solution.py:29
  828.1 11.7 %cholesky.316 = f32[128,128]{1,0:T(8,128)S(1)} custom-call(f32[128,128]{1,0:T(8,128)S(1)} %cholesky.355), custom_call_target="Cholesky" | custom-call | tf_op jit(solution)/shard_map/jit(cholesky)/cholesky | solution.py:29
  839.9 10.0 custom-call.22
  850.3 11.7 %cholesky.333 = f32[128,128]{1,0:T(8,128)S(1)} custom-call(f32[128,128]{1,0:T(8,128)S(1)} %convolution_subtract_fusion.5), custom_call_target="Cholesky" | custom-call | tf_op jit(solution)/shard_map/jit(cholesky)/cholesky | solution.py:29
  868.9 4.1 while.27
  873.0 19.7 %custom-call.23 = f32[2,128,128]{1,2,0:T(8,128)S(1)} custom-call(f32[2,128,128]{2,1,0:T(8,128)S(1)} %get-tuple-element.248), custom_call_target="InvertDiagBlocksLowerTriangular" | custom-call | tf_op jit(solution)/shard_map/jit(_solve_triangular)/triangular_solve | solution.py:33
  894.7 4.1 while.31
  898.8 19.9 %custom-call.27 = f32[2,128,128]{1,2,0:T(8,128)S(1)} custom-call(f32[2,128,128]{2,1,0:T(8,128)S(1)} %get-tuple-element.252), custom_call_target="InvertDiagBlocksLowerTriangular" | custom-call | tf_op jit(solution)/shard_map/jit(_solve_triangular)/triangular_solve | solution.py:33
  919.8 4.1 while.30
  923.8 19.7 %custom-call.26 = f32[2,128,128]{1,2,0:T(8,128)S(1)} custom-call(f32[2,128,128]{2,1,0:T(8,128)S(1)} %get-tuple-element.251), custom_call_target="InvertDiagBlocksLowerTriangular" | custom-call | tf_op jit(solution)/shard_map/jit(_solve_triangular)/triangular_solve | solution.py:33
  944.6 4.1 while.29
  948.7 19.7 %custom-call.25 = f32[2,128,128]{1,2,0:T(8,128)S(1)} custom-call(f32[2,128,128]{2,1,0:T(8,128)S(1)} %get-tuple-element.250), custom_call_target="InvertDiagBlocksLowerTriangular" | custom-call | tf_op jit(solution)/shard_map/jit(_solve_triangular)/triangular_solve | solution.py:33
  969.4 4.1 while.28
  973.5 19.7 %custom-call.24 = f32[2,128,128]{1,2,0:T(8,128)S(1)} custom-call(f32[2,128,128]{2,1,0:T(8,128)S(1)} %get-tuple-element.249), custom_call_target="InvertDiagBlocksLowerTriangular" | custom-call | tf_op jit(solution)/shard_map/jit(_solve_triangular)/triangular_solve | solution.py:33
  (457 shorter events, 154.8 us)
Async XLA Ops:
  7.2 134.1 %all-gather.3.cloned.1.call-start = ((), (), s32[]{:S(2)}) async-start(), calls=%async_computation | async-start | bytes 16842752 | tf_op jit(solution)/shard_map/all_gather | solution.py:84
  10.3 257.2 %all-gather.5.cloned.1.call-start = ((), (), s32[]{:S(2)}) async-start(), calls=%async_computation.1 | async-start | bytes 16842752 | tf_op jit(solution)/shard_map/all_gather | solution.py:85
  13.0 702.8 %all-reduce.4.cloned.1.call-start = ((), (), s32[]{:S(2)}) async-start(), calls=%async_computation.2 | async-start | bytes 4194304 | tf_op jit(solution)/shard_map/psum | solution.py:100
  14.6 253.0 %copy-start.3 = (s32[1,16]{1,0:T(1,128)S(1)}, s32[1,16]{1,0:T(1,128)}, u32[]{:S(2)}) copy-start(s32[1,16]{1,0:T(1,128)} %param.14) | copy-start | bytes 196
  14.6 252.9 %copy-start.4 = (s32[1,32]{1,0:T(1,128)S(1)}, s32[1,32]{1,0:T(1,128)}, u32[]{:S(2)}) copy-start(s32[1,32]{1,0:T(1,128)} %param.15) | copy-start | bytes 388
  868.7 25.9 %copy-start = (f32[1024,256]{1,0:T(8,128)S(1)}, f32[1024,256]{1,0:T(8,128)}, u32[]{:S(2)}) copy-start(f32[1024,256]{1,0:T(8,128)} %get-tuple-element.338) | copy-start | bytes 3145732
  944.6 49.7 %copy-start.2 = (f32[256,256]{1,0:T(8,128)S(1)}, f32[256,256]{1,0:T(8,128)}, u32[]{:S(2)}) copy-start(f32[256,256]{1,0:T(8,128)} %fusion.22) | copy-start | bytes 786436
  969.1 26.0 %copy-start.1 = (f32[256,256]{1,0:T(8,128)S(1)}, f32[256,256]{1,0:T(8,128)}, u32[]{:S(2)}) copy-start(f32[256,256]{1,0:T(8,128)} %fusion.25) | copy-start | bytes 786436
Sparse Core Ops, SparseCore 0:
  12.2 129.0 all-gather.2
  145.4 122.1 all-gather.4
  458.4 257.3 all-reduce.3
where the time goes:
time: 1010 us; the launch traced here: 1000 us
  waiting for transfers between devices  421 us (42%)
  other arithmetic  256 us (25%)
  matrix products  146 us (14%)
  local copies, waits for them, and re-layouts  80.3 us (8%)
  blocking collectives  74.9 us (7%)
  between operations  22.3 us (2%)
    psum x1, waiting for transfers between devices, body(): lax.psum((slots, skel_samples, skel_local), ('leaf', 'sub'))  180 us
    another operation x28, other arithmetic, cholesky_factor(): return jnp.linalg.cholesky(shifted)  139 us
    all_gather x1, waiting for transfers between devices, body(): lax.all_gather(tree_points, ('leaf', 'sub'), axis=1, tiled=True)  127 us
    all_gather x1, waiting for transfers between devices, body(): lax.all_gather(tree_omega, ('leaf', 'sub'), axis=1, tiled=True)  114 us
    another operation x11, other arithmetic, right_solve(): jax.scipy.linalg.solve_triangular(lower_part, values.T, lower=True)  98.9 us
    dot_general x34, matrix products, kernel_values(): lax.dot_general(row_points, col_points, (((0,), (0,)), ((), ())), precisi...  78.7 us
    psum x1, blocking collectives, body(): lax.psum((slots, skel_samples, skel_local), ('leaf', 'sub'))  74.9 us
    dot_general x32, matrix products, add_block(): lax.dot_general(kernel_block, weighted, (((1,), (1,)), ((), ())), preferr...  56.2 us
  transfers between devices with their start and end apart: 3, of which 3 were waited for; matrix products, arithmetic and copies ran while one was open for 2% of the time, Pallas kernels for 0%

commit v1 on v0

v1 whole, which is shorter than its diff:
```python
import functools
import math

import jax
import jax.numpy as jnp
from jax import lax
from jax.experimental import pallas as pl
from jax.experimental.pallas import tpu as pltpu
from jax.sharding import PartitionSpec as P

MESH = pl.DeviceIdType.MESH
HIGH = lax.Precision.HIGH
HIGHEST = lax.Precision.HIGHEST
F32 = jnp.float32
BF16 = jnp.bfloat16
VMEM = pl.BlockSpec(memory_space=pltpu.VMEM)
SMEM = pl.BlockSpec(memory_space=pltpu.SMEM)

ROWS = 256
FEATS = 8
SAMPLES = 128
RANK = 256
SPAN = 288
LINK = F32


def place():
    leaf = lax.axis_index("leaf")
    core = lax.axis_index("sub")
    return leaf % 4, (leaf // 4) % 4, leaf // 16, core


def device(x, y, z, core):
    return (z * 16 + y * 4 + x, core)


def greet(partners):
    barrier = pltpu.get_barrier_semaphore()
    for partner in partners:
        pl.semaphore_signal(barrier, inc=1, device_id=partner, device_id_type=MESH)
    pl.semaphore_wait(barrier, len(partners))


def send(src, dst, send_sem, recv_sem, target):
    copy = pltpu.make_async_remote_copy(
        src_ref=src,
        dst_ref=dst,
        send_sem=send_sem,
        recv_sem=recv_sem,
        device_id=target,
        device_id_type=MESH,
    )
    copy.start()
    return copy


def features(coordinates, scale, ones_first):
    norm = -2.0 * jnp.sum(coordinates * coordinates, axis=0, keepdims=True)
    first = norm.astype(BF16).astype(F32)
    second = (norm - first).astype(BF16).astype(F32)
    third = norm - first - second
    row = lax.broadcasted_iota(jnp.int32, coordinates.shape, 0)
    start = 3 if ones_first else 0
    other = 0 if ones_first else 3
    tail = jnp.where((row >= other) & (row < other + 3), 1.0, 0.0)
    tail = jnp.where(row == start, first, tail)
    tail = jnp.where(row == start + 1, second, tail)
    tail = jnp.where(row == start + 2, third, tail)
    return jnp.concatenate([scale * coordinates, tail], axis=0)


def gather_kernel(
    points, omega, order, siblings, cousins,
    blocks, row_points, lists, tree_points,
    own, own_rows, own_lists,
    z_send, z_recv, up_send, up_recv, down_send, down_recv, far_send, far_recv,
    rows_send, rows_recv, list_send, list_recv,
):
    x, y, z, core = place()
    mate = 7 - 6 * (z % 2)
    offsets = [mate, 2, 6, 3, 5, 4]
    z_partners = [device(x, y, (z + offset) % 8, core) for offset in offsets]
    up = device(x, (y + 1) % 4, z, core)
    down = device(x, (y + 3) % 4, z, core)
    near = [
        (dx, dc, device((x + dx) % 4, y, z, (core + dc) % 2))
        for dx in range(4)
        for dc in range(2)
        if dx or dc
    ]
    greet(z_partners + [up, down] + [who for _, _, who in near])

    own[0:ROWS, :] = omega[...].astype(F32).T.astype(BF16)
    columns = features(points[...].astype(F32), 1.0, False).astype(BF16)
    own[256:272, :] = columns[:, :128]
    own[272:288, :] = columns[:, 128:]
    pending = []
    z_copies = []
    for k, offset in enumerate(offsets):
        back = (8 - offset) % 8
        z_copies.append(
            send(own, blocks.at[back], z_send.at[k], z_recv.at[back], z_partners[k])
        )

    local = order[...] % ROWS
    lane = lax.broadcasted_iota(jnp.int32, (ROWS, ROWS), 0)
    pick = jnp.where(lane == local, 1.0, 0.0).astype(BF16)
    mine = jnp.dot(points[...], pick, preferred_element_type=F32)
    tree_points[...] = mine
    own_rows[...] = features(mine, 4.0, True).astype(BF16)
    own_lists[...] = jnp.zeros_like(own_lists)
    own_lists[0:1, 0:16] = siblings[...]
    own_lists[1:2, 0:32] = cousins[...]
    row_points[x * 2 + core] = own_rows[...]
    lists[x] = own_lists[...]
    small = []
    for k, (dx, dc, who) in enumerate(near):
        small.append(
            send(own_rows, row_points.at[x * 2 + core], rows_send.at[k], rows_recv.at[k], who)
        )
        if not dc:
            small.append(
                send(own_lists, lists.at[x], list_send.at[dx], list_recv.at[dx], who)
            )

    far = []

    def relay(k):
        offset = offsets[k]
        if k % 2:
            down_copies[k].wait_recv()
            far.append(
                send(blocks.at[24 + offset], blocks.at[16 + offset], far_send.at[k], far_recv.at[k], up)
            )
        else:
            up_copies[k].wait_recv()
            far.append(
                send(blocks.at[8 + offset], blocks.at[16 + offset], far_send.at[k], far_recv.at[k], down)
            )

    up_copies, down_copies = [], []
    for k, offset in enumerate(offsets):
        pltpu.make_async_remote_copy(
            src_ref=own, dst_ref=blocks.at[offset], send_sem=z_send.at[k],
            recv_sem=z_recv.at[offset], device_id=up, device_id_type=MESH,
        ).wait_recv()
        down_copies.append(
            send(blocks.at[offset], blocks.at[24 + offset], up_send.at[k], down_recv.at[k], up)
        )
        up_copies.append(
            send(blocks.at[offset], blocks.at[8 + offset], down_send.at[k], up_recv.at[k], down)
        )
        if k:
            relay(k - 1)
    relay(5)
    for k in range(6):
        if k % 2:
            up_copies[k].wait_recv()
        else:
            down_copies[k].wait_recv()
    for copy in far:
        copy.wait()
    for copy in small:
        copy.wait()
    for copy in z_copies + up_copies + down_copies:
        copy.wait_send()


def gather(points, omega, order, siblings, cousins):
    dma = pltpu.SemaphoreType.DMA
    return pl.pallas_call(
        gather_kernel,
        out_shape=(
            jax.ShapeDtypeStruct((32, SPAN, 128), BF16),
            jax.ShapeDtypeStruct((8, 16, ROWS), BF16),
            jax.ShapeDtypeStruct((4, 8, 128), jnp.int32),
            jax.ShapeDtypeStruct((FEATS, ROWS), F32),
        ),
        in_specs=[VMEM] * 5,
        out_specs=(VMEM,) * 4,
        scratch_shapes=[
            pltpu.VMEM((SPAN, 128), BF16),
            pltpu.VMEM((16, ROWS), BF16),
            pltpu.VMEM((8, 128), jnp.int32),
            dma((6,)), dma((8,)), dma((6,)), dma((6,)), dma((6,)), dma((6,)), dma((6,)), dma((6,)),
            dma((7,)), dma((7,)), dma((4,)), dma((4,)),
        ],
        compiler_params=pltpu.CompilerParams(
            collective_id=0, has_side_effects=True, vmem_limit_bytes=32 << 20
        ),
        name="gather",
    )(points, omega, order, siblings, cousins)


def sample_kernel(blocks, row_points, lists, out, total, rows):
    x, y, z, _ = place()
    for row_block in range(4):
        for half in range(2):
            rows[half * ROWS : (half + 1) * ROWS, :] = (
                row_points[2 * row_block + half].astype(F32).T.astype(BF16)
            )
        total[...] = jnp.zeros_like(total)
        for side, count in ((0, 16), (1, 32)):

            def add_block(entry, carry, side=side, row_block=row_block):
                block = lists[row_block, side, entry]

                @pl.when(block % 4 == x)
                def _():
                    slot = ((block // 4 + 4 - y) % 4) * 8 + (block // 16 + 8 - z) % 8
                    weights = blocks[slot, 0:ROWS, :]
                    columns = jnp.concatenate(
                        [blocks[slot, 256:272, :], blocks[slot, 272:288, :]], axis=1
                    )
                    for part in range(2):
                        span = pl.ds(part * ROWS, ROWS)
                        exponent = jnp.dot(rows[span, :], columns, preferred_element_type=F32)
                        tile = jnp.exp(exponent).astype(BF16)
                        total[side, span, :] += jnp.dot(tile, weights, preferred_element_type=F32)

                return carry

            lax.fori_loop(0, count, add_block, 0)
        for half in range(2):
            for side in range(2):
                out[half, row_block, :, side * SAMPLES : (side + 1) * SAMPLES] = total[
                    side, half * ROWS : (half + 1) * ROWS, :
                ]


def sample(blocks, row_points, lists):
    return pl.pallas_call(
        sample_kernel,
        out_shape=jax.ShapeDtypeStruct((2, 4, ROWS, RANK), F32),
        in_specs=[VMEM, VMEM, SMEM],
        out_specs=VMEM,
        scratch_shapes=[pltpu.VMEM((2, 2 * ROWS, SAMPLES), F32), pltpu.VMEM((2 * ROWS, 16), BF16)],
        compiler_params=pltpu.CompilerParams(vmem_limit_bytes=32 << 20),
        name="sample",
    )(blocks, row_points, lists)


def collect_kernel(
    parts, skeleton, tree_points,
    samples, full,
    other_core, relay_out, relay_in, near_out, near_in, table, other_table, piece, pieces,
    core_sems, relay_sems, near_sems, table_sems, piece_send, piece_recv,
    z_send, z_recv, y_sems, x_sems, swap_send, swap_recv,
):
    x, y, z, core = place()
    leaf = z * 16 + y * 4 + x
    node = z // 2
    other = device(x, y, z, 1 - core)
    mates = []
    for dz in range(2):
        for dy in range(4):
            for dx in range(4):
                if dz or dy or dx:
                    where = ((x + dx) % 4, (y + dy) % 4, node * 2 + (z + dz) % 2)
                    mates.append((dz * 16 + dy * 4 + dx, where, device(*where, core)))
    column = [device(x, y, (z + dz) % 8, core) for dz in range(1, 8)]
    strangers = [device(x, y, ((node + dn) % 4) * 2 + dz, core) for dn in range(1, 4) for dz in range(2)]
    greet([other] + [who for _, _, who in mates] + strangers)
    right, left = device((x + 1) % 4, y, z, core), device((x + 3) % 4, y, z, core)
    above, below = device(x, (y + 1) % 4, z, core), device(x, (y + 3) % 4, z, core)

    swap = send(parts.at[1 - core], other_core, core_sems.at[0], core_sems.at[1], other)
    swap.wait()

    def partial(place_x):
        return parts[core, place_x] + other_core[place_x]

    ahead, behind, across = (x + 1) % 4, (x + 3) % 4, (x + 2) % 4
    farthest = partial(across)
    relay_out[...] = farthest.astype(LINK)
    relays = [
        send(relay_out.at[0:128], relay_in.at[0], relay_sems.at[0], relay_sems.at[1], right),
        send(relay_out.at[128:256], relay_in.at[1], relay_sems.at[2], relay_sems.at[3], left),
    ]
    to_right, to_left = partial(ahead), partial(behind)
    near_out[0, 128:256, :] = to_right[128:256].astype(LINK)
    near_out[1, 0:128, :] = to_left[0:128].astype(LINK)
    nears = [
        send(near_out.at[0, 128:256], near_in.at[0, 128:256], near_sems.at[0], near_sems.at[1], right),
        send(near_out.at[1, 0:128], near_in.at[1, 0:128], near_sems.at[2], near_sems.at[3], left),
    ]
    relays[0].wait_recv()
    near_out[0, 0:128, :] = (to_right[0:128] + relay_in[0].astype(F32)).astype(LINK)
    nears.append(
        send(near_out.at[0, 0:128], near_in.at[0, 0:128], near_sems.at[4], near_sems.at[5], right)
    )
    relays[1].wait_recv()
    near_out[1, 128:256, :] = (to_left[128:256] + relay_in[1].astype(F32)).astype(LINK)
    nears.append(
        send(near_out.at[1, 128:256], near_in.at[1, 128:256], near_sems.at[6], near_sems.at[7], left)
    )
    mine = partial(x)
    first_row = (leaf * 2 + core) * ROWS
    row = lax.broadcasted_iota(jnp.int32, (ROWS, RANK), 0) + first_row
    chosen = jnp.where(row == skeleton[pl.ds(node, 1), :], 1.0, 0.0)
    skeleton_points = jnp.dot(
        tree_points[...].astype(BF16), chosen.astype(BF16), preferred_element_type=F32
    )
    for copy in nears:
        copy.wait_recv()
    rows = mine + (near_in[0].astype(F32) + near_in[1].astype(F32))
    samples[...] = rows

    table[0:256, :] = lax.dot_general(
        rows, rows, (((0,), (0,)), ((), ())), precision=HIGHEST, preferred_element_type=F32
    )
    table[128:256, 0:128] = jnp.zeros((128, 128), F32)
    table[128:136, 0:128] = skeleton_points[:, 0:128]
    table[136:144, 0:128] = skeleton_points[:, 128:256]
    table[256:512, :] = lax.dot_general(
        chosen, rows, (((0,), (0,)), ((), ())), precision=HIGHEST, preferred_element_type=F32
    )
    start = pl.multiple_of((1 - core) * 256, 256)
    swap_table = send(
        table.at[pl.ds(start, 256)], other_table, table_sems.at[0], table_sems.at[1], other
    )
    swap_table.wait()
    keep = pl.multiple_of(core * 256, 256)
    other_table[...] += table[pl.ds(keep, 256), :]

    def chunk(where):
        first = (where[0] * 8 + where[1] * 2 + where[2] % 2) * 8
        return other_table.at[pl.ds(pl.multiple_of(first, 8), 8)]

    spreads = []
    for slot, where, who in mates:
        spreads.append(
            send(chunk(where), pieces.at[slot], piece_send.at[slot], piece_recv.at[slot], who)
        )
    sums = chunk((x, y, z))[...]
    for copy in spreads:
        copy.wait_recv()
    for slot, _, _ in mates:
        sums = sums + pieces[slot]
    piece[...] = sums
    full[core, x, y, z] = sums
    for copy in spreads:
        copy.wait_send()

    stages = [
        send(piece, full.at[core, x, y, z], z_send.at[k], z_recv.at[k], who)
        for k, who in enumerate(column)
    ]
    for copy in stages:
        copy.wait()

    def ring(mine_at, sems, plus, minus, before, after, cut):
        mine_ref = full.at[mine_at]
        out = [
            send(mine_ref, mine_ref, sems.at[0], sems.at[1], plus),
            send(mine_ref, mine_ref, sems.at[2], sems.at[3], minus),
        ]
        out[0].wait_recv()
        first_half = full.at[before + (pl.ds(0, cut),)]
        out.append(send(first_half, first_half, sems.at[4], sems.at[5], plus))
        out[1].wait_recv()
        second_half = full.at[after + (pl.ds(cut, cut),)]
        out.append(send(second_half, second_half, sems.at[6], sems.at[7], minus))
        return out

    hops = ring((core, x, y), y_sems, above, below, (core, x, (y + 3) % 4), (core, x, (y + 1) % 4), 4)
    for copy in hops[2:]:
        copy.wait_recv()
    for copy in hops:
        copy.wait_send()

    hops = ring((core, x), x_sems, right, left, (core, behind), (core, ahead), 2)
    swaps = []

    def hand(place_x):
        ref = full.at[core, place_x]
        swaps.append(send(ref, ref, swap_send.at[len(swaps)], swap_recv.at[len(swaps)], other))

    hand(x)
    hand(behind)
    hand(ahead)
    for copy in hops[2:]:
        copy.wait_recv()
    hand(across)
    for copy in hops:
        copy.wait_send()
    for copy in swaps:
        copy.wait()
    for copy in relays + nears:
        copy.wait_send()


def collect(parts, skeleton, tree_points):
    dma = pltpu.SemaphoreType.DMA
    return pl.pallas_call(
        collect_kernel,
        out_shape=(
            jax.ShapeDtypeStruct((ROWS, RANK), F32),
            jax.ShapeDtypeStruct((2, 4, 4, 8, 8, RANK), F32),
        ),
        in_specs=[VMEM] * 3,
        out_specs=(VMEM,) * 2,
        scratch_shapes=[
            pltpu.VMEM((4, ROWS, RANK), F32),
            pltpu.VMEM((ROWS, RANK), LINK),
            pltpu.VMEM((2, 128, RANK), LINK),
            pltpu.VMEM((2, ROWS, RANK), LINK),
            pltpu.VMEM((2, ROWS, RANK), LINK),
            pltpu.VMEM((512, RANK), F32),
            pltpu.VMEM((256, RANK), F32),
            pltpu.VMEM((8, RANK), F32),
            pltpu.VMEM((32, 8, RANK), F32),
            dma((2,)), dma((4,)), dma((8,)), dma((2,)), dma((32,)), dma((32,)),
            dma((7,)), dma((7,)), dma((8,)), dma((8,)), dma((4,)), dma((4,)),
        ],
        compiler_params=pltpu.CompilerParams(
            collective_id=1, has_side_effects=True, vmem_limit_bytes=32 << 20
        ),
        name="collect",
    )(parts, skeleton, tree_points)


def finish_kernel(full, samples, basis, coupling, work, chosen):
    node = lax.axis_index("leaf") // 32
    row = lax.broadcasted_iota(jnp.int32, (RANK, RANK), 0)
    col = lax.broadcasted_iota(jnp.int32, (RANK, RANK), 1)
    skeleton_points = []
    for n in range(4):
        for at_x in range(4):
            for at_y in range(4):
                span = pl.ds(at_x * 64 + at_y * 16, 16)
                work[n, span, :] = full[0, at_x, at_y, 2 * n : 2 * n + 2].reshape(16, RANK)
                chosen[n, span, :] = full[1, at_x, at_y, 2 * n : 2 * n + 2].reshape(16, RANK)
        skeleton_points.append(
            jnp.concatenate([work[n, 128:136, 0:128], work[n, 136:144, 0:128]], axis=1)
        )
        gram = work[n]
        on_diagonal = jnp.where(row == col, gram, 0.0)
        trace = jnp.sum(jnp.sum(on_diagonal, axis=0, keepdims=True), axis=1, keepdims=True)
        work[n] = gram + jnp.where(row == col, 0.01 * trace, 0.0)

    middles = []
    for k in range(2):
        row_side = features(skeleton_points[2 * k], 4.0, True).T.astype(BF16)
        col_side = features(skeleton_points[2 * k + 1], 1.0, False).astype(BF16)
        kernel_skel = jnp.exp(jnp.dot(row_side, col_side, preferred_element_type=F32))
        right = jnp.dot(kernel_skel, chosen[2 * k + 1], precision=HIGH, preferred_element_type=F32)
        middles.append(
            lax.dot_general(
                chosen[2 * k], right, (((0,), (0,)), ((), ())),
                precision=HIGH, preferred_element_type=F32,
            )
        )

    lane8 = lax.broadcasted_iota(jnp.int32, (8, 128), 1)
    row8 = lax.broadcasted_iota(jnp.int32, (8, 128), 0)
    group8 = (lane8 // 32) * 32
    lane = lax.broadcasted_iota(jnp.int32, (32, 128), 1)
    for p in range(8):
        top = 32 * p
        aligned = (top // 128) * 128
        packed = jnp.zeros((32, 128), F32)
        for n in range(4):
            block = work[n, top : top + 32, aligned : aligned + 128]
            turn = (32 * n - (top - aligned)) % 128
            if turn:
                block = pltpu.roll(block, turn, 1)
            packed = jnp.where(lane // 32 == n, block, packed)
        left = [packed[8 * g : 8 * g + 8] for g in range(4)]
        inverse = [jnp.where(lane8 - group8 == row8 + 8 * g, 1.0, 0.0) for g in range(4)]
        for j in range(32):
            own, inner = j // 8, j % 8
            index = group8 + j
            spread = {
                g: jnp.take_along_axis(left[g], index, axis=1, mode="promise_in_bounds")
                for g in range(own, 4)
            }
            scale = lax.rsqrt(spread[own][inner : inner + 1, :])
            left_row = left[own][inner : inner + 1, :] * scale
            inverse_row = inverse[own][inner : inner + 1, :] * scale
            for g in range(own, 4):
                factor = spread[g] * scale
                if g == own:
                    factor = jnp.where(row8 > inner, factor, 0.0)
                left[g] = left[g] - factor * left_row
                inverse[g] = inverse[g] - factor * inverse_row
                if g == own:
                    inverse[g] = jnp.where(row8 == inner, inverse_row, inverse[g])
        packed = jnp.concatenate(inverse, axis=0)
        diagonal = jnp.concatenate([jnp.where(lane // 32 == n, packed, 0.0) for n in range(4)], axis=0)
        stacked = jnp.concatenate([work[n, top : top + 32, :] for n in range(4)], axis=0)
        srow = lax.broadcasted_iota(jnp.int32, (128, RANK), 0)
        scol = lax.broadcasted_iota(jnp.int32, (128, RANK), 1)
        identity = jnp.where(srow % 32 == scol % 32, 1.0, 0.0)
        stacked = jnp.where(scol // 32 == p, identity, stacked)
        solved = jnp.dot(diagonal, stacked, precision=HIGHEST, preferred_element_type=F32)
        done = jnp.where(scol < top + 32, solved, 0.0)
        for n in range(4):
            work[n, top : top + 32, :] = done[32 * n : 32 * n + 32]
        rest = RANK - top - 32
        if rest:
            turned = solved.T[top + 32 :, :]
            tlane = lax.broadcasted_iota(jnp.int32, (rest, 128), 1)
            tcol = lax.broadcasted_iota(jnp.int32, (rest, RANK), 1)
            for n in range(4):
                update = jnp.dot(
                    jnp.where(tlane // 32 == n, turned, 0.0), solved,
                    precision=HIGHEST, preferred_element_type=F32,
                )
                work[n, top + 32 :, :] = jnp.where(tcol // 32 == p, 0.0, work[n, top + 32 :, :]) - update

    last = (((1,), (1,)), ((), ()))
    basis[...] = 128.0 * lax.dot_general(
        samples[...], work[node], last, precision=HIGH, preferred_element_type=F32
    )
    for k in range(2):
        half = jnp.dot(work[2 * k], middles[k], precision=HIGH, preferred_element_type=F32)
        coupling[k] = (16384.0 / math.sqrt(RANK)) * lax.dot_general(
            half, work[2 * k + 1], last, precision=HIGH, preferred_element_type=F32
        )


def finish(full, samples):
    return pl.pallas_call(
        finish_kernel,
        out_shape=(
            jax.ShapeDtypeStruct((ROWS, RANK), F32),
            jax.ShapeDtypeStruct((2, RANK, RANK), F32),
        ),
        in_specs=[VMEM] * 2,
        out_specs=(VMEM,) * 2,
        scratch_shapes=[pltpu.VMEM((4, RANK, RANK), F32), pltpu.VMEM((4, RANK, RANK), F32)],
        compiler_params=pltpu.CompilerParams(vmem_limit_bytes=32 << 20),
        name="finish",
    )(full, samples)


def body(points, omega, tree_order, sibling_blocks, cousin_blocks, skeleton):
    blocks, row_points, lists, tree_points = gather(
        points, omega, tree_order.reshape(1, ROWS), sibling_blocks, cousin_blocks
    )
    parts = sample(blocks, row_points, lists)
    samples, full = collect(parts, skeleton, tree_points)
    return finish(full, samples)


def solution(mesh):
    return jax.shard_map(
        body,
        mesh=mesh,
        in_specs=(
            P(None, ("leaf", "sub")),
            P(None, ("leaf", "sub")),
            P(("leaf", "sub")),
            P("leaf", None),
            P("leaf", None),
            P(),
        ),
        out_specs=(P(("leaf", "sub"), None), P()),
        check_vma=False,
    )
```

time: 1010 us -> 159 us (0.16)
  waiting for transfers between devices: 421 us -> 0 us
  other arithmetic: 256 us -> 0 us
  Pallas kernels: 0 us -> 155 us
  matrix products: 146 us -> 0 us
  local copies, waits for them, and re-layouts: 80.3 us -> 3.51 us
  blocking collectives: 74.9 us -> 0 us
  between operations: 22.3 us -> 0.68 us
    all_gather x2 -> x0, waiting for transfers between devices: 241 us -> none  [the longest x1 127 us: body(): lax.all_gather(tree_points, ('leaf', 'sub'), axis=1, tiled=True)]
    another operation x40 -> x0, other arithmetic: 239 us -> none  [the longest x28 139 us: cholesky_factor(): return jnp.linalg.cholesky(shifted)]
    psum x1 -> x0, waiting for transfers between devices: 180 us -> none  [body(): lax.psum((slots, skel_samples, skel_local), ('leaf', 'sub'))]
    pallas_call x0 -> x4, Pallas kernels: none -> 155 us  [the longest x1 64.7 us: collect(): pl.pallas_call(collect_kernel, out_shape=(jax.ShapeDtypeStruct((ROWS, RAN...]
    dot_general x73 -> x0, matrix products: 139 us -> none  [the longest x34 78.7 us: kernel_values(): lax.dot_general(row_points, col_points, (((0,), (0,)), ((), ())), precisi...]
    psum x1 -> x0, blocking collectives: 74.9 us -> none  [body(): lax.psum((slots, skel_samples, skel_local), ('leaf', 'sub'))]
    dynamic_slice x64 -> x0, local copies, waits for them, and re-layouts: 41.2 us -> none  [add_block(): col_omega = lax.dynamic_slice_in_dim(piece_omega, offset, stride, 1)]
    another operation x44 -> x0, local copies, waits for them, and re-layouts: 20.4 us -> none  [the longest x36 20.3 us: right_solve(): jax.scipy.linalg.solve_triangular(lower_part, values.T, lower=True)]
  transfers between devices with their start and end apart: 3 -> 0, of which waited for: 3 -> 0; matrix products, arithmetic and copies ran while one was open for 2% -> 0% of each run, Pallas kernels for 0% -> 0%
where the time goes in v1:
time: 159 us
  Pallas kernels  155 us (97%)
  local copies, waits for them, and re-layouts  3.51 us (2%)
    pallas_call x1, Pallas kernels, collect(): pl.pallas_call(collect_kernel, out_shape=(jax.ShapeDtypeStruct((ROWS, RAN...  64.7 us
    pallas_call x1, Pallas kernels, gather(): pl.pallas_call(gather_kernel, out_shape=(jax.ShapeDtypeStruct((32, SPAN,...  34.7 us
    pallas_call x1, Pallas kernels, finish(): pl.pallas_call(finish_kernel, out_shape=(jax.ShapeDtypeStruct((ROWS, RANK...  30.4 us
    pallas_call x1, Pallas kernels, sample(): pl.pallas_call(sample_kernel, out_shape=jax.ShapeDtypeStruct((2, 4, ROWS,...  24.9 us
    unnamed x12, local copies, waits for them, and re-layouts  3.51 us

profile of v1, /device:TPU:1, one launch (start us, length us, event | category | flops | bytes accessed | tf_op | source)
XLA Modules:
  0.0 158.9 jit_solution(2083434100338324249)
XLA Ops:
  0.6 0.0 copy-start
  0.6 0.8 copy-done
  1.5 0.0 copy-start.2
  1.5 0.7 copy-done.2
  2.2 0.0 copy-start.3
  2.2 0.7 copy-done.3
  2.8 0.0 copy-start.4
  2.8 0.7 copy-done.4
  3.5 0.0 copy-start.5
  3.5 0.7 copy-done.5
  4.2 34.7 %gather.1 = (bf16[32,288,128]{2,1,0:T(8,128)(2,1)S(1)}, bf16[8,16,256]{2,1,0:T(8,128)(2,1)S(1)}, s32[4,8,128]{2,1,0:T(8,128)S(1)}, f32[8,256]{1,0:T(8,128)S(1)}) custom-call(bf16[8,256]{1,0:T(8,128)(2,1)S(1)} %copy-done.2, bf16[128,256]{1,0:T(8,128)(2,1)S(1)} %copy-done, s32[1,256]{1,0:T(1,128)S(1)} %bitcast.1, s32[1,16]{1,0:T(1,128)S(1)} %copy-done.4, ...), custom_call_target="tpu_custom_call" | custom-call | tf_op jit(solution)/shard_map/gather/pallas_call | solution.py:171
  38.9 0.0 copy-start.1
  38.9 24.9 %sample.1.parts = f32[2,4,256,256]{3,2,1,0:T(8,128)S(1)} custom-call(bf16[32,288,128]{2,1,0:T(8,128)(2,1)S(1)} %get-tuple-element.8.blocks, bf16[8,16,256]{2,1,0:T(8,128)(2,1)S(1)} %get-tuple-element.9.row_points, s32[4,8,128]{2,1,0:T(8,128)S(1)} %get-tuple-element.10.lists), custom_call_target="tpu_custom_call" | custom-call | tf_op jit(solution)/shard_map/sample/pallas_call | solution.py:232
  63.8 0.0 copy-done.1
  63.8 64.7 %collect.1 = (f32[256,256]{1,0:T(8,128)S(1)}, f32[2,4,4,8,8,256]{5,4,3,2,1,0:T(8,128)S(1)}) custom-call(f32[2,4,256,256]{3,2,1,0:T(8,128)S(1)} %sample.1.parts, s32[4,256]{1,0:T(4,128)S(1)} %copy-done.1, f32[8,256]{1,0:T(8,128)S(1)} %get-tuple-element.11.tree_points), custom_call_target="tpu_custom_call" | custom-call | tf_op jit(solution)/shard_map/collect/pallas_call | solution.py:395
  128.5 30.4 %finish.1 = (f32[256,256]{1,0:T(8,128)}, f32[2,256,256]{2,1,0:T(8,128)}) custom-call(f32[2,4,4,8,8,256]{5,4,3,2,1,0:T(8,128)S(1)} %get-tuple-element.12.full, f32[256,256]{1,0:T(8,128)S(1)} %get-tuple-element.13.samples), custom_call_target="tpu_custom_call" | custom-call | tf_op jit(solution)/shard_map/finish/pallas_call | solution.py:524
Async XLA Ops:
  0.6 0.8 copy-start
  1.5 0.7 copy-start.2
  2.2 0.7 copy-start.3
  2.8 0.7 copy-start.4
  3.5 0.7 copy-start.5
  38.9 24.9 %copy-start.1 = (s32[4,256]{1,0:T(4,128)S(1)}, s32[4,256]{1,0:T(4,128)}, u32[]{:S(2)}) copy-start(s32[4,256]{1,0:T(4,128)} %skeleton.1) | copy-start | bytes 12292

commit v2 on v1

--- a/solution.py
+++ b/solution.py
@@ -15,6 +15,7 @@
 BF16 = jnp.bfloat16
 VMEM = pl.BlockSpec(memory_space=pltpu.VMEM)
 SMEM = pl.BlockSpec(memory_space=pltpu.SMEM)
+HBM = pl.BlockSpec(memory_space=pltpu.HBM)
 
 ROWS = 256
 FEATS = 8
@@ -70,12 +71,26 @@
 
 
 def gather_kernel(
-    points, omega, order, siblings, cousins,
+    points_in, omega_in, order_in, siblings_in, cousins_in,
     blocks, row_points, lists, tree_points,
-    own, own_rows, own_lists,
+    points, omega, order, siblings, cousins, load_sems, own, own_rows, own_lists,
     z_send, z_recv, up_send, up_recv, down_send, down_recv, far_send, far_recv,
     rows_send, rows_recv, list_send, list_recv,
 ):
+    loads = [
+        pltpu.make_async_copy(source, target, load_sems.at[k])
+        for k, (source, target) in enumerate(
+            [
+                (omega_in, omega),
+                (points_in, points),
+                (order_in, order),
+                (siblings_in, siblings),
+                (cousins_in, cousins),
+            ]
+        )
+    ]
+    for copy in loads:
+        copy.start()
     x, y, z, core = place()
     mate = 7 - 6 * (z % 2)
     offsets = [mate, 2, 6, 3, 5, 4]
@@ -88,13 +103,13 @@
         for dc in range(2)
         if dx or dc
     ]
-    greet(z_partners + [up, down] + [who for _, _, who in near])
-
+    loads[0].wait()
     own[0:ROWS, :] = omega[...].astype(F32).T.astype(BF16)
+    loads[1].wait()
     columns = features(points[...].astype(F32), 1.0, False).astype(BF16)
     own[256:272, :] = columns[:, :128]
     own[272:288, :] = columns[:, 128:]
-    pending = []
+    greet(z_partners + [up, down] + [who for _, _, who in near])
     z_copies = []
     for k, offset in enumerate(offsets):
         back = (8 - offset) % 8
@@ -102,6 +117,8 @@
             send(own, blocks.at[back], z_send.at[k], z_recv.at[back], z_partners[k])
         )
 
+    for copy in loads[2:]:
+        copy.wait()
     local = order[...] % ROWS
     lane = lax.broadcasted_iota(jnp.int32, (ROWS, ROWS), 0)
     pick = jnp.where(lane == local, 1.0, 0.0).astype(BF16)
@@ -176,9 +193,15 @@
             jax.ShapeDtypeStruct((4, 8, 128), jnp.int32),
             jax.ShapeDtypeStruct((FEATS, ROWS), F32),
         ),
-        in_specs=[VMEM] * 5,
+        in_specs=[HBM] * 5,
         out_specs=(VMEM,) * 4,
         scratch_shapes=[
+            pltpu.VMEM((FEATS, ROWS), BF16),
+            pltpu.VMEM((SAMPLES, ROWS), BF16),
+            pltpu.VMEM((1, ROWS), jnp.int32),
+            pltpu.VMEM((1, 16), jnp.int32),
+            pltpu.VMEM((1, 32), jnp.int32),
+            dma((5,)),
             pltpu.VMEM((SPAN, 128), BF16),
             pltpu.VMEM((16, ROWS), BF16),
             pltpu.VMEM((8, 128), jnp.int32),
@@ -192,39 +215,58 @@
     )(points, omega, order, siblings, cousins)
 
 
-def sample_kernel(blocks, row_points, lists, out, total, rows):
+def sample_kernel(blocks, row_points, lists, out, total, rows, slots):
     x, y, z, _ = place()
+    sides = ((0, 16), (1, 32))
+
+    counts = {}
+    for row_block in range(4):
+        for side, length in sides:
+
+            def pick(entry, count, row_block=row_block, side=side):
+                block = lists[row_block, side, entry]
+                slots[row_block, side, count] = ((block // 4 + 4 - y) % 4) * 8 + (block // 16 + 8 - z) % 8
+                return count + jnp.where(block % 4 == x, 1, 0)
+
+            counts[row_block, side] = lax.fori_loop(0, length, pick, 0, unroll=True)
+
+    total[...] = jnp.zeros_like(total)
     for row_block in range(4):
         for half in range(2):
-            rows[half * ROWS : (half + 1) * ROWS, :] = (
+            rows[row_block, half * ROWS : (half + 1) * ROWS, :] = (
                 row_points[2 * row_block + half].astype(F32).T.astype(BF16)
             )
-        total[...] = jnp.zeros_like(total)
-        for side, count in ((0, 16), (1, 32)):
-
-            def add_block(entry, carry, side=side, row_block=row_block):
-                block = lists[row_block, side, entry]
-
-                @pl.when(block % 4 == x)
-                def _():
-                    slot = ((block // 4 + 4 - y) % 4) * 8 + (block // 16 + 8 - z) % 8
-                    weights = blocks[slot, 0:ROWS, :]
-                    columns = jnp.concatenate(
-                        [blocks[slot, 256:272, :], blocks[slot, 272:288, :]], axis=1
-                    )
-                    for part in range(2):
-                        span = pl.ds(part * ROWS, ROWS)
-                        exponent = jnp.dot(rows[span, :], columns, preferred_element_type=F32)
-                        tile = jnp.exp(exponent).astype(BF16)
-                        total[side, span, :] += jnp.dot(tile, weights, preferred_element_type=F32)
-
+        for side, _ in sides:
+            count = counts[row_block, side]
+
+            def add_pair(step, carry, row_block=row_block, side=side, count=count):
+                first = 2 * step
+                paired = first + 1 < count
+                one = slots[row_block, side, first]
+                two = jnp.where(paired, slots[row_block, side, first + 1], one)
+                weight = jnp.where(paired, 1.0, 0.0).astype(BF16)
+                columns = jnp.concatenate(
+                    [
+                        blocks[one, 256:272, :],
+                        blocks[one, 272:288, :],
+                        blocks[two, 256:272, :],
+                        blocks[two, 272:288, :],
+                    ],
+                    axis=1,
+                )
+                weights = jnp.concatenate(
+                    [blocks[one, 0:ROWS, :], blocks[two, 0:ROWS, :] * weight], axis=0
+                )
+                exponent = jnp.dot(rows[row_block], columns, preferred_element_type=F32)
+                tile = jnp.exp(exponent).astype(BF16)
+                total[row_block, side] += jnp.dot(tile, weights, preferred_element_type=F32)
                 return carry
 
-            lax.fori_loop(0, count, add_block, 0)
+            lax.fori_loop(0, (count + 1) // 2, add_pair, 0)
         for half in range(2):
             for side in range(2):
                 out[half, row_block, :, side * SAMPLES : (side + 1) * SAMPLES] = total[
-                    side, half * ROWS : (half + 1) * ROWS, :
+                    row_block, side, half * ROWS : (half + 1) * ROWS, :
                 ]
 
 
@@ -234,7 +276,11 @@
         out_shape=jax.ShapeDtypeStruct((2, 4, ROWS, RANK), F32),
         in_specs=[VMEM, VMEM, SMEM],
         out_specs=VMEM,
-        scratch_shapes=[pltpu.VMEM((2, 2 * ROWS, SAMPLES), F32), pltpu.VMEM((2 * ROWS, 16), BF16)],
+        scratch_shapes=[
+            pltpu.VMEM((4, 2, 2 * ROWS, SAMPLES), F32),
+            pltpu.VMEM((4, 2 * ROWS, 16), BF16),
+            pltpu.SMEM((4, 2, 40), jnp.int32),
+        ],
         compiler_params=pltpu.CompilerParams(vmem_limit_bytes=32 << 20),
         name="sample",
     )(blocks, row_points, lists)
@@ -245,7 +291,7 @@
     samples, full,
     other_core, relay_out, relay_in, near_out, near_in, table, other_table, piece, pieces,
     core_sems, relay_sems, near_sems, table_sems, piece_send, piece_recv,
-    z_send, z_recv, y_sems, x_sems, swap_send, swap_recv,
+    z_send, z_recv, y_sems, x_sems, swap_sems,
 ):
     x, y, z, core = place()
     leaf = z * 16 + y * 4 + x
@@ -349,40 +395,63 @@
     for copy in stages:
         copy.wait()
 
-    def ring(mine_at, sems, plus, minus, before, after, cut):
-        mine_ref = full.at[mine_at]
-        out = [
-            send(mine_ref, mine_ref, sems.at[0], sems.at[1], plus),
-            send(mine_ref, mine_ref, sems.at[2], sems.at[3], minus),
-        ]
-        out[0].wait_recv()
-        first_half = full.at[before + (pl.ds(0, cut),)]
-        out.append(send(first_half, first_half, sems.at[4], sems.at[5], plus))
-        out[1].wait_recv()
-        second_half = full.at[after + (pl.ds(cut, cut),)]
-        out.append(send(second_half, second_half, sems.at[6], sems.at[7], minus))
-        return out
-
-    hops = ring((core, x, y), y_sems, above, below, (core, x, (y + 3) % 4), (core, x, (y + 1) % 4), 4)
-    for copy in hops[2:]:
+    first_lanes, second_lanes = pl.ds(0, 128), pl.ds(128, 128)
+    every8, every4 = pl.ds(0, 8), pl.ds(0, 4)
+    cuts8, cuts4 = (pl.ds(0, 4), pl.ds(4, 4)), (pl.ds(0, 2), pl.ds(2, 2))
+    next_y, last_y = (y + 1) % 4, (y + 3) % 4
+
+    def push(ref, sems, k, who):
+        return send(ref, ref, sems.at[2 * k], sems.at[2 * k + 1], who)
+
+    def region(at_x, at_y, at_z, lanes):
+        return full.at[core, at_x, at_y, at_z, every8, lanes]
+
+    first = [push(region(x, y, every8, first_lanes), y_sems, 0, above)]
+    first.append(push(region(x, y, every8, first_lanes), y_sems, 1, below))
+    second = [push(region(x, y, every8, second_lanes), x_sems, 0, right)]
+    second.append(push(region(x, y, every8, second_lanes), x_sems, 1, left))
+    first[0].wait_recv()
+    first.append(push(region(x, last_y, cuts8[0], first_lanes), y_sems, 2, above))
+    second[0].wait_recv()
+    second.append(push(region(behind, y, cuts8[0], second_lanes), x_sems, 2, right))
+    first[1].wait_recv()
+    first.append(push(region(x, next_y, cuts8[1], first_lanes), y_sems, 3, below))
+    second[1].wait_recv()
+    second.append(push(region(ahead, y, cuts8[1], second_lanes), x_sems, 3, left))
+    for copy in first[2:]:
         copy.wait_recv()
-    for copy in hops:
-        copy.wait_send()
-
-    hops = ring((core, x), x_sems, right, left, (core, behind), (core, ahead), 2)
+    first.append(push(region(x, every4, every8, first_lanes), x_sems, 4, right))
+    first.append(push(region(x, every4, every8, first_lanes), x_sems, 5, left))
+    for copy in second[2:]:
+        copy.wait_recv()
+    second.append(push(region(every4, y, every8, second_lanes), y_sems, 4, above))
+    second.append(push(region(every4, y, every8, second_lanes), y_sems, 5, below))
     swaps = []
 
-    def hand(place_x):
-        ref = full.at[core, place_x]
-        swaps.append(send(ref, ref, swap_send.at[len(swaps)], swap_recv.at[len(swaps)], other))
-
-    hand(x)
-    hand(behind)
-    hand(ahead)
-    for copy in hops[2:]:
+    def hand(at_x, at_y, lanes):
+        swaps.append(push(region(at_x, at_y, every8, lanes), swap_sems, len(swaps), other))
+
+    hand(x, every4, first_lanes)
+    hand(every4, y, second_lanes)
+    first[4].wait_recv()
+    first.append(push(region(behind, cuts4[0], every8, first_lanes), x_sems, 6, right))
+    second[4].wait_recv()
+    second.append(push(region(cuts4[0], last_y, every8, second_lanes), y_sems, 6, above))
+    first[5].wait_recv()
+    first.append(push(region(ahead, cuts4[1], every8, first_lanes), x_sems, 7, left))
+    second[5].wait_recv()
+    second.append(push(region(cuts4[1], next_y, every8, second_lanes), y_sems, 7, below))
+    hand(behind, every4, first_lanes)
+    hand(every4, last_y, second_lanes)
+    hand(ahead, every4, first_lanes)
+    hand(every4, next_y, second_lanes)
+    for copy in first[6:]:
         copy.wait_recv()
-    hand(across)
-    for copy in hops:
+    hand(across, every4, first_lanes)
+    for copy in second[6:]:
+        copy.wait_recv()
+    hand(every4, (y + 2) % 4, second_lanes)
+    for copy in first + second:
         copy.wait_send()
     for copy in swaps:
         copy.wait()
@@ -411,7 +480,7 @@
             pltpu.VMEM((8, RANK), F32),
             pltpu.VMEM((32, 8, RANK), F32),
             dma((2,)), dma((4,)), dma((8,)), dma((2,)), dma((32,)), dma((32,)),
-            dma((7,)), dma((7,)), dma((8,)), dma((8,)), dma((4,)), dma((4,)),
+            dma((7,)), dma((7,)), dma((16,)), dma((16,)), dma((16,)),
         ],
         compiler_params=pltpu.CompilerParams(
             collective_id=1, has_side_effects=True, vmem_limit_bytes=32 << 20
@@ -420,11 +489,40 @@
     )(parts, skeleton, tree_points)
 
 
+def fold(factors, lines):
+    a, b, c, d = (factor * values for factor, values in zip(factors, lines, strict=True))
+    return (a + b) + (c + d)
+
+
+def pivots(entry):
+    def pair(a, b, c):
+        scale = lax.rsqrt(a)
+        return scale, b * scale, a * lax.rsqrt(a * (a * c - b * b))
+
+    r0, l10, r1 = pair(entry(0, 0), entry(1, 0), entry(1, 1))
+    l20, l30 = entry(2, 0) * r0, entry(3, 0) * r0
+    l21, l31 = (entry(2, 1) - l20 * l10) * r1, (entry(3, 1) - l30 * l10) * r1
+    r2, l32, r3 = pair(
+        entry(2, 2) - (l20 * l20 + l21 * l21),
+        entry(3, 2) - (l30 * l20 + l31 * l21),
+        entry(3, 3) - (l30 * l30 + l31 * l31),
+    )
+
+    def solve(values):
+        v0 = values[0] * r0
+        v1 = (values[1] - v0 * l10) * r1
+        v2 = (values[2] - (v0 * l20 + v1 * l21)) * r2
+        v3 = ((values[3] - (v0 * l30 + v1 * l31)) - v2 * l32) * r3
+        return [v0, v1, v2, v3]
+
+    return solve
+
+
 def finish_kernel(full, samples, basis, coupling, work, chosen):
     node = lax.axis_index("leaf") // 32
     row = lax.broadcasted_iota(jnp.int32, (RANK, RANK), 0)
     col = lax.broadcasted_iota(jnp.int32, (RANK, RANK), 1)
-    skeleton_points = []
+    skeleton_points, sizes = [], []
     for n in range(4):
         for at_x in range(4):
             for at_y in range(4):
@@ -437,7 +535,8 @@
         gram = work[n]
         on_diagonal = jnp.where(row == col, gram, 0.0)
         trace = jnp.sum(jnp.sum(on_diagonal, axis=0, keepdims=True), axis=1, keepdims=True)
-        work[n] = gram + jnp.where(row == col, 0.01 * trace, 0.0)
+        work[n] = gram * (1.0 / trace) + jnp.where(row == col, 0.01, 0.0)
+        sizes.append(lax.rsqrt(trace))
 
     middles = []
     for k in range(2):
@@ -468,24 +567,32 @@
             packed = jnp.where(lane // 32 == n, block, packed)
         left = [packed[8 * g : 8 * g + 8] for g in range(4)]
         inverse = [jnp.where(lane8 - group8 == row8 + 8 * g, 1.0, 0.0) for g in range(4)]
-        for j in range(32):
+        for j in range(0, 32, 4):
             own, inner = j // 8, j % 8
-            index = group8 + j
             spread = {
-                g: jnp.take_along_axis(left[g], index, axis=1, mode="promise_in_bounds")
+                g: [
+                    jnp.take_along_axis(left[g], group8 + (j + t), axis=1, mode="promise_in_bounds")
+                    for t in range(4)
+                ]
                 for g in range(own, 4)
             }
-            scale = lax.rsqrt(spread[own][inner : inner + 1, :])
-            left_row = left[own][inner : inner + 1, :] * scale
-            inverse_row = inverse[own][inner : inner + 1, :] * scale
+
+            def line(tile, t, inner=inner):
+                return jnp.broadcast_to(tile[inner + t : inner + t + 1, :], (8, 128))
+
+            solve = pivots(lambda t, u: line(spread[own][u], t))
+            left_rows = solve([line(left[own], t) for t in range(4)])
+            inverse_rows = solve([line(inverse[own], t) for t in range(4)])
             for g in range(own, 4):
-                factor = spread[g] * scale
+                if g == own and inner == 4:
+                    continue
+                factors = solve(spread[g])
                 if g == own:
-                    factor = jnp.where(row8 > inner, factor, 0.0)
-                left[g] = left[g] - factor * left_row
-                inverse[g] = inverse[g] - factor * inverse_row
-                if g == own:
-                    inverse[g] = jnp.where(row8 == inner, inverse_row, inverse[g])
+                    factors = [jnp.where(row8 > 3, factor, 0.0) for factor in factors]
+                left[g] = left[g] - fold(factors, left_rows)
+                inverse[g] = inverse[g] - fold(factors, inverse_rows)
+            for t in range(4):
+                inverse[own] = jnp.where(row8 == inner + t, inverse_rows[t], inverse[own])
         packed = jnp.concatenate(inverse, axis=0)
         diagonal = jnp.concatenate([jnp.where(lane // 32 == n, packed, 0.0) for n in range(4)], axis=0)
         stacked = jnp.concatenate([work[n, top : top + 32, :] for n in range(4)], axis=0)
@@ -510,12 +617,13 @@
                 work[n, top + 32 :, :] = jnp.where(tcol // 32 == p, 0.0, work[n, top + 32 :, :]) - update
 
     last = (((1,), (1,)), ((), ()))
-    basis[...] = 128.0 * lax.dot_general(
+    size = sum(jnp.where(node == n, sizes[n], 0.0) for n in range(4))
+    basis[...] = (128.0 * size) * lax.dot_general(
         samples[...], work[node], last, precision=HIGH, preferred_element_type=F32
     )
     for k in range(2):
         half = jnp.dot(work[2 * k], middles[k], precision=HIGH, preferred_element_type=F32)
-        coupling[k] = (16384.0 / math.sqrt(RANK)) * lax.dot_general(
+        coupling[k] = ((16384.0 / math.sqrt(RANK)) * sizes[2 * k] * sizes[2 * k + 1]) * lax.dot_general(
             half, work[2 * k + 1], last, precision=HIGH, preferred_element_type=F32
         )
 

time: 159 us -> 127 us (0.80)
  Pallas kernels: 155 us -> 123 us
    pallas_call x1, Pallas kernels: 30.4 us -> 16.1 us  [finish(): pl.pallas_call(finish_kernel, out_shape=(jax.ShapeDtypeStruct((ROWS, RANK...]
    pallas_call x1, Pallas kernels: 64.7 us -> 55.3 us  [collect(): pl.pallas_call(collect_kernel, out_shape=(jax.ShapeDtypeStruct((ROWS, RAN...]
    pallas_call x1, Pallas kernels: 24.9 us -> 16.2 us  [sample(): pl.pallas_call(sample_kernel, out_shape=jax.ShapeDtypeStruct((2, 4, ROWS,...]
where the time goes in v2:
time: 127 us
  Pallas kernels  123 us (97%)
  local copies, waits for them, and re-layouts  3.51 us (3%)
    pallas_call x1, Pallas kernels, collect(): pl.pallas_call(collect_kernel, out_shape=(jax.ShapeDtypeStruct((ROWS, RAN...  55.3 us
    pallas_call x1, Pallas kernels, gather(): pl.pallas_call(gather_kernel, out_shape=(jax.ShapeDtypeStruct((32, SPAN,...  34.9 us
    pallas_call x1, Pallas kernels, sample(): pl.pallas_call(sample_kernel, out_shape=jax.ShapeDtypeStruct((2, 4, ROWS,...  16.2 us
    pallas_call x1, Pallas kernels, finish(): pl.pallas_call(finish_kernel, out_shape=(jax.ShapeDtypeStruct((ROWS, RANK...  16.1 us
    unnamed x12, local copies, waits for them, and re-layouts  3.51 us

profile of v2, /device:TPU:1, one launch (start us, length us, event | category | flops | bytes accessed | tf_op | source)
XLA Modules:
  0.0 126.8 jit_solution(17306406844262300106)
XLA Ops:
  0.6 0.0 copy-start
  0.6 0.8 copy-done
  1.5 0.0 copy-start.2
  1.5 0.7 copy-done.2
  2.2 0.0 copy-start.3
  2.2 0.7 copy-done.3
  2.8 0.0 copy-start.4
  2.8 0.7 copy-done.4
  3.5 0.0 copy-start.5
  3.5 0.7 copy-done.5
  4.2 34.9 %gather.1 = (bf16[32,288,128]{2,1,0:T(8,128)(2,1)S(1)}, bf16[8,16,256]{2,1,0:T(8,128)(2,1)S(1)}, s32[4,8,128]{2,1,0:T(8,128)S(1)}, f32[8,256]{1,0:T(8,128)S(1)}) custom-call(bf16[8,256]{1,0:T(8,128)(2,1)S(1)} %copy-done.2, bf16[128,256]{1,0:T(8,128)(2,1)S(1)} %copy-done, s32[1,256]{1,0:T(1,128)S(1)} %bitcast.1, s32[1,16]{1,0:T(1,128)S(1)} %copy-done.4, ...), custom_call_target="tpu_custom_call" | custom-call | tf_op jit(solution)/shard_map/gather/pallas_call | solution.py:188
  39.1 0.0 copy-start.1
  39.1 16.2 %sample.1.parts = f32[2,4,256,256]{3,2,1,0:T(8,128)S(1)} custom-call(bf16[32,288,128]{2,1,0:T(8,128)(2,1)S(1)} %get-tuple-element.8.blocks, bf16[8,16,256]{2,1,0:T(8,128)(2,1)S(1)} %get-tuple-element.9.row_points, s32[4,8,128]{2,1,0:T(8,128)S(1)} %get-tuple-element.10.lists), custom_call_target="tpu_custom_call" | custom-call | tf_op jit(solution)/shard_map/sample/pallas_call | solution.py:274
  55.3 0.0 copy-done.1
  55.3 55.3 %collect.1 = (f32[256,256]{1,0:T(8,128)S(1)}, f32[2,4,4,8,8,256]{5,4,3,2,1,0:T(8,128)S(1)}) custom-call(f32[2,4,256,256]{3,2,1,0:T(8,128)S(1)} %sample.1.parts, s32[4,256]{1,0:T(4,128)S(1)} %copy-done.1, f32[8,256]{1,0:T(8,128)S(1)} %get-tuple-element.11.tree_points), custom_call_target="tpu_custom_call" | custom-call | tf_op jit(solution)/shard_map/collect/pallas_call | solution.py:464
  110.7 16.1 %finish.1 = (f32[256,256]{1,0:T(8,128)}, f32[2,256,256]{2,1,0:T(8,128)}) custom-call(f32[2,4,4,8,8,256]{5,4,3,2,1,0:T(8,128)S(1)} %get-tuple-element.12.full, f32[256,256]{1,0:T(8,128)S(1)} %get-tuple-element.13.samples), custom_call_target="tpu_custom_call" | custom-call | tf_op jit(solution)/shard_map/finish/pallas_call | solution.py:632
Async XLA Ops:
  0.6 0.8 copy-start
  1.5 0.7 copy-start.2
  2.2 0.7 copy-start.3
  2.8 0.7 copy-start.4
  3.5 0.7 copy-start.5
  39.1 16.3 %copy-start.1 = (s32[4,256]{1,0:T(4,128)S(1)}, s32[4,256]{1,0:T(4,128)}, u32[]{:S(2)}) copy-start(s32[4,256]{1,0:T(4,128)} %skeleton.1) | copy-start | bytes 12292

commit v3 on v2

v3 whole, which is shorter than its diff:
```python
import functools
import math

import jax
import jax.numpy as jnp
from jax import lax
from jax.experimental import pallas as pl
from jax.experimental.pallas import tpu as pltpu
from jax.sharding import PartitionSpec as P

MESH = pl.DeviceIdType.MESH
HIGH = lax.Precision.HIGH
HIGHEST = lax.Precision.HIGHEST
F32 = jnp.float32
BF16 = jnp.bfloat16
VMEM = pl.BlockSpec(memory_space=pltpu.VMEM)
SMEM = pl.BlockSpec(memory_space=pltpu.SMEM)
HBM = pl.BlockSpec(memory_space=pltpu.HBM)

ROWS = 256
FEATS = 8
SAMPLES = 128
RANK = 256
SPAN = 288
LINK = BF16


def place():
    leaf = lax.axis_index("leaf")
    core = lax.axis_index("sub")
    return leaf % 4, (leaf // 4) % 4, leaf // 16, core


def device(x, y, z, core):
    return (z * 16 + y * 4 + x, core)


def greet(partners):
    barrier = pltpu.get_barrier_semaphore()
    for partner in partners:
        pl.semaphore_signal(barrier, inc=1, device_id=partner, device_id_type=MESH)
    pl.semaphore_wait(barrier, len(partners))


def send(src, dst, send_sem, recv_sem, target):
    copy = pltpu.make_async_remote_copy(
        src_ref=src,
        dst_ref=dst,
        send_sem=send_sem,
        recv_sem=recv_sem,
        device_id=target,
        device_id_type=MESH,
    )
    copy.start()
    return copy


def features(coordinates, scale, ones_first):
    norm = -2.0 * jnp.sum(coordinates * coordinates, axis=0, keepdims=True)
    first = norm.astype(BF16).astype(F32)
    second = (norm - first).astype(BF16).astype(F32)
    third = norm - first - second
    row = lax.broadcasted_iota(jnp.int32, coordinates.shape, 0)
    start = 3 if ones_first else 0
    other = 0 if ones_first else 3
    tail = jnp.where((row >= other) & (row < other + 3), 1.0, 0.0)
    tail = jnp.where(row == start, first, tail)
    tail = jnp.where(row == start + 1, second, tail)
    tail = jnp.where(row == start + 2, third, tail)
    return jnp.concatenate([scale * coordinates, tail], axis=0)


def plane_kind(dz):
    return jnp.where((dz == 2) | (dz == 4) | (dz == 5), 0, 1)


def pick_slots(lists, x, y, z):
    lane = lax.broadcasted_iota(jnp.int32, (8, 128), 1)
    kind = lax.broadcasted_iota(jnp.int32, (8, 128), 0) // 4
    along, dz = lane // 8, lane % 8
    plane = ((z + dz) % 8) * 16
    block = jnp.where(
        kind == 0, plane + ((y + along) % 4) * 4 + x, plane + y * 4 + (x + along) % 4
    )
    named = jnp.where((lane < 32) & (plane_kind(dz) == kind), block, -1).astype(F32)
    hit = jnp.zeros((8, 128), F32)
    for side, length in ((0, 16), (1, 32)):
        entries = jnp.concatenate(
            [lists[k, at, side : side + 1, :] for k in range(2) for at in range(4)], axis=0
        ).astype(F32)
        for e in range(length):
            hit = jnp.where(named == jnp.broadcast_to(entries[:, e : e + 1], (8, 128)), 1.0, hit)
    place_of = lane.astype(F32)
    count = jnp.zeros((8, 128), F32)
    found = jnp.zeros((8, 128), F32)
    for slot in range(32):
        if slot % 8:
            here = jnp.broadcast_to(hit[:, slot : slot + 1], (8, 128))
            found = jnp.where((place_of == count) & (here > 0.5), float(slot), found)
            count = count + here
    return jnp.where(lane == 127, count, found).astype(jnp.int32)


def gather_kernel(
    points_in, omega_in, order_in, siblings_in, cousins_in,
    blocks, row_points, picks, tree_points,
    points, omega, order, siblings, cousins, load_sems, own, own_rows, own_lists, lists,
    z_send, z_recv, out_send, out_recv, far_send, far_recv,
    rows_send, rows_recv, list_send, list_recv,
):
    loads = [
        pltpu.make_async_copy(source, target, load_sems.at[k])
        for k, (source, target) in enumerate(
            [
                (omega_in, omega),
                (points_in, points),
                (order_in, order),
                (siblings_in, siblings),
                (cousins_in, cousins),
            ]
        )
    ]
    for copy in loads:
        copy.start()
    x, y, z, core = place()
    mate = 7 - 6 * (z % 2)
    upward, downward = device(x, y, (z + 1) % 8, core), device(x, y, (z + 7) % 8, core)
    plus = [device(x, (y + 1) % 4, z, core), device((x + 1) % 4, y, z, core)]
    minus = [device(x, (y + 3) % 4, z, core), device((x + 3) % 4, y, z, core)]
    along_x = [(d, c, device((x + d) % 4, y, z, (core + c) % 2)) for d in range(4) for c in range(2) if d or c]
    along_y = [(d, c, device(x, (y + d) % 4, z, (core + c) % 2)) for d in range(4) for c in range(2) if d or c]
    greet([upward, downward] + [who for _, _, who in along_x] + [who for _, _, who in along_y[1:]])

    loads[0].wait()
    own[0:ROWS, :] = omega[...].astype(F32).T.astype(BF16)
    loads[1].wait()
    columns = features(points[...].astype(F32), 1.0, False).astype(BF16)
    own[256:272, :] = columns[:, :128]
    own[272:288, :] = columns[:, 128:]
    halves = (pl.ds(0, SPAN // 2), pl.ds(SPAN // 2, SPAN // 2))

    def hop(k, src, dst, who):
        return send(src, dst, z_send.at[k], z_recv.at[k], who)

    hops = [hop(0, own, blocks.at[7], upward), hop(1, own, blocks.at[1], downward)]

    for copy in loads[2:]:
        copy.wait()
    local = order[...] % ROWS
    lane = lax.broadcasted_iota(jnp.int32, (ROWS, ROWS), 0)
    pick = jnp.where(lane == local, 1.0, 0.0).astype(BF16)
    mine = jnp.dot(points[...], pick, preferred_element_type=F32)
    tree_points[...] = mine
    own_rows[...] = features(mine, 4.0, True).astype(BF16)
    own_lists[...] = jnp.zeros_like(own_lists)
    own_lists[0:1, 0:16] = siblings[...]
    own_lists[1:2, 0:32] = cousins[...]
    small = []
    for kind, (at, partners) in enumerate(((x, along_x), (y, along_y))):
        row_points[kind, at * 2 + core] = own_rows[...]
        lists[kind, at] = own_lists[...]
        for k, (d, c, who) in enumerate(partners):
            target = row_points.at[kind, at * 2 + core]
            small.append(send(own_rows, target, rows_send.at[kind, k], rows_recv.at[kind, k], who))
            if not c:
                target = lists.at[kind, at]
                small.append(send(own_lists, target, list_send.at[kind, d], list_recv.at[kind, d], who))

    outs, fars = {}, []

    def fan_out(k, kind, dz):
        block = blocks.at[dz]
        outs[k] = (
            send(block, blocks.at[24 + dz], out_send.at[2 * k], out_recv.at[2 * k], plus[kind]),
            send(block, blocks.at[8 + dz], out_send.at[2 * k + 1], out_recv.at[2 * k + 1], minus[kind]),
        )

    def relay(k, kind, dz):
        for side, (at, half, who) in enumerate(((24, halves[0], plus[kind]), (8, halves[1], minus[kind]))):
            outs[k][side].wait_recv()
            fars.append(
                send(
                    blocks.at[at + dz, half], blocks.at[16 + dz, half],
                    far_send.at[2 * k + side], far_recv.at[2 * k + side], who,
                )
            )

    hops[0].wait_recv()
    hops.append(hop(2, blocks.at[7], blocks.at[6], upward))
    hops[1].wait_recv()
    hops.append(hop(3, blocks.at[1], blocks.at[2], downward))
    fan_out(0, 1, mate)
    hops[2].wait_recv()
    hops.append(hop(4, blocks.at[6], blocks.at[5], upward))
    fan_out(1, 1, 6)
    hops[3].wait_recv()
    hops.append(hop(5, blocks.at[2], blocks.at[3], downward))
    fan_out(2, 0, 2)
    relay(0, 1, mate)
    hops[4].wait_recv()
    hops.append(hop(6, blocks.at[5, halves[0]], blocks.at[4, halves[0]], upward))
    fan_out(3, 0, 5)
    hops[5].wait_recv()
    hops.append(hop(7, blocks.at[3, halves[1]], blocks.at[4, halves[1]], downward))
    fan_out(4, 1, 3)
    relay(1, 1, 6)
    relay(2, 0, 2)
    hops[6].wait_recv()
    hops[7].wait_recv()
    fan_out(5, 0, 4)
    relay(3, 0, 5)
    relay(4, 1, 3)
    relay(5, 0, 4)
    for copy in small:
        copy.wait()
    picks[...] = pick_slots(lists, x, y, z)
    for copy in fars:
        copy.wait()
    for copy in hops:
        copy.wait_send()
    for pair in outs.values():
        for copy in pair:
            copy.wait_send()


def gather(points, omega, order, siblings, cousins):
    dma = pltpu.SemaphoreType.DMA
    return pl.pallas_call(
        gather_kernel,
        out_shape=(
            jax.ShapeDtypeStruct((32, SPAN, 128), BF16),
            jax.ShapeDtypeStruct((2, 8, 16, ROWS), BF16),
            jax.ShapeDtypeStruct((8, 128), jnp.int32),
            jax.ShapeDtypeStruct((FEATS, ROWS), F32),
        ),
        in_specs=[HBM] * 5,
        out_specs=(VMEM,) * 4,
        scratch_shapes=[
            pltpu.VMEM((FEATS, ROWS), BF16),
            pltpu.VMEM((SAMPLES, ROWS), BF16),
            pltpu.VMEM((1, ROWS), jnp.int32),
            pltpu.VMEM((1, 16), jnp.int32),
            pltpu.VMEM((1, 32), jnp.int32),
            dma((5,)),
            pltpu.VMEM((SPAN, 128), BF16),
            pltpu.VMEM((16, ROWS), BF16),
            pltpu.VMEM((8, 128), jnp.int32),
            pltpu.VMEM((2, 4, 8, 128), jnp.int32),
            dma((8,)), dma((8,)), dma((12,)), dma((12,)), dma((12,)), dma((12,)),
            dma((2, 7)), dma((2, 7)), dma((2, 4)), dma((2, 4)),
        ],
        compiler_params=pltpu.CompilerParams(
            collective_id=0, has_side_effects=True, vmem_limit_bytes=32 << 20
        ),
        name="gather",
    )(points, omega, order, siblings, cousins)


def sample_kernel(blocks, row_points, picks, out, rows, even_tile, odd_tile, items):
    _, _, z, _ = place()

    total = 0
    for row in range(8):
        count = picks[row, 127]

        def note(step, at, row=row, count=count):
            items[at, 0] = row
            items[at, 1] = picks[row, 2 * step]
            paired = 2 * step + 1 < count
            items[at, 2] = jnp.where(paired, picks[row, 2 * step + 1], picks[row, 2 * step])
            items[at, 3] = jnp.where(paired, 2, 1)
            return at + 1

        total = lax.fori_loop(0, (count + 1) // 2, note, total)
    for extra in range(2):
        items[total + extra, 0] = 0
        items[total + extra, 1] = jnp.where(total > 0, items[0, 1], 6)
        items[total + extra, 2] = items[total + extra, 1]
        items[total + extra, 3] = 0

    out[...] = jnp.zeros_like(out)
    for row in range(8):
        for half in range(2):
            rows[row, half * ROWS : (half + 1) * ROWS, :] = (
                row_points[row // 4, 2 * (row % 4) + half].astype(F32).T.astype(BF16)
            )

    def kernel_tile(item, tile):
        columns = jnp.concatenate(
            [blocks[items[item, k], at : at + 16, :] for k in (1, 2) for at in (256, 272)], axis=1
        )
        exponent = jnp.dot(rows[items[item, 0]], columns, preferred_element_type=F32)
        tile[...] = jnp.exp(exponent).astype(BF16)

    def add(item, tile):
        weights = []
        for k in (1, 2):
            slot = items[item, k]
            sibling = ((z + slot % 8) % 8) // 4 == z // 4
            use = items[item, 3] >= k
            values = blocks[slot, 0:ROWS, :]
            near = jnp.where(use & sibling, 1.0, 0.0).astype(BF16)
            far = jnp.where(use & jnp.logical_not(sibling), 1.0, 0.0).astype(BF16)
            weights.append(jnp.concatenate([values * near, values * far], axis=1))
        terms = jnp.dot(tile[...], jnp.concatenate(weights, axis=0), preferred_element_type=F32)
        kind, at = items[item, 0] // 4, items[item, 0] % 4
        out[0, kind, at] += terms[0:ROWS]
        out[1, kind, at] += terms[ROWS:]

    kernel_tile(0, even_tile)

    def two_items(step, carry):
        kernel_tile(2 * step + 1, odd_tile)
        add(2 * step, even_tile)
        kernel_tile(2 * step + 2, even_tile)
        add(2 * step + 1, odd_tile)
        return carry

    lax.fori_loop(0, (total + 1) // 2, two_items, 0)


def sample(blocks, row_points, picks):
    return pl.pallas_call(
        sample_kernel,
        out_shape=jax.ShapeDtypeStruct((2, 2, 4, ROWS, RANK), F32),
        in_specs=[VMEM, VMEM, SMEM],
        out_specs=VMEM,
        scratch_shapes=[
            pltpu.VMEM((8, 2 * ROWS, 16), BF16),
            pltpu.VMEM((2 * ROWS, 2 * ROWS), BF16),
            pltpu.VMEM((2 * ROWS, 2 * ROWS), BF16),
            pltpu.SMEM((64, 4), jnp.int32),
        ],
        compiler_params=pltpu.CompilerParams(vmem_limit_bytes=32 << 20),
        name="sample",
    )(blocks, row_points, picks)


def collect_kernel(
    parts, skeleton, tree_points,
    samples, full_a, full_b,
    other_core, relay_out, relay_in, near_out, near_in, table, other_table, piece, pieces,
    core_send, core_recv, relay_sems, near_sems, table_sems, piece_send, piece_recv,
    z_send, z_recv, y_sems, x_sems, swap_sems,
):
    x, y, z, core = place()
    leaf = z * 16 + y * 4 + x
    node = z // 2
    other = device(x, y, z, 1 - core)
    mates = []
    for dz in range(2):
        for dy in range(4):
            for dx in range(4):
                if dz or dy or dx:
                    where = ((x + dx) % 4, (y + dy) % 4, node * 2 + (z + dz) % 2)
                    mates.append((dz * 16 + dy * 4 + dx, where, device(*where, core)))
    column = [device(x, y, (z + dz) % 8, core) for dz in range(1, 8)]
    strangers = [device(x, y, ((node + dn) % 4) * 2 + dz, core) for dn in range(1, 4) for dz in range(2)]
    greet([other] + [who for _, _, who in mates] + strangers)
    right, left = device((x + 1) % 4, y, z, core), device((x + 3) % 4, y, z, core)
    above, below = device(x, (y + 1) % 4, z, core), device(x, (y + 3) % 4, z, core)

    ahead, behind, across = (x + 1) % 4, (x + 3) % 4, (x + 2) % 4
    next_y, last_y = (y + 1) % 4, (y + 3) % 4
    order = [(across, (y + 2) % 4), (ahead, next_y), (behind, last_y), (x, y)]
    swap = {}
    for step, places in enumerate(order):
        for kind in range(2):
            at = places[kind]
            swap[step, kind] = send(
                parts.at[1 - core, kind, at], other_core.at[kind, at],
                core_send.at[kind, step], core_recv.at[kind, step], other,
            )

    def partial(step, kind):
        swap[step, kind].wait_recv()
        at = order[step][kind]
        return parts[core, kind, at] + other_core[kind, at]

    plus, minus = (right, above), (left, below)
    lower, upper = pl.ds(0, 128), pl.ds(128, 128)
    relays, nears = [], []
    for kind in range(2):
        relay_out[kind] = partial(0, kind).astype(LINK)
        for side, (rows_of, who) in enumerate(((lower, plus[kind]), (upper, minus[kind]))):
            relays.append(
                send(
                    relay_out.at[kind, rows_of], relay_in.at[kind, side],
                    relay_sems.at[0, kind, side], relay_sems.at[1, kind, side], who,
                )
            )

    def pass_on(kind, side, first, rows_of, who):
        ref = near_out.at[kind, side, rows_of]
        landing = near_in.at[kind, side, rows_of]
        nears.append(send(ref, landing, near_sems.at[0, kind, side, first], near_sems.at[1, kind, side, first], who))

    waiting = {}
    for kind in range(2):
        to_plus, to_minus = partial(1, kind), partial(2, kind)
        near_out[kind, 0, 128:256, :] = to_plus[128:256].astype(LINK)
        near_out[kind, 1, 0:128, :] = to_minus[0:128].astype(LINK)
        pass_on(kind, 0, 0, upper, plus[kind])
        pass_on(kind, 1, 0, lower, minus[kind])
        waiting[kind] = (to_plus[0:128], to_minus[128:256])
    for kind in range(2):
        relays[2 * kind].wait_recv()
        near_out[kind, 0, 0:128, :] = (waiting[kind][0] + relay_in[kind, 0].astype(F32)).astype(LINK)
        pass_on(kind, 0, 1, lower, plus[kind])
        relays[2 * kind + 1].wait_recv()
        near_out[kind, 1, 128:256, :] = (waiting[kind][1] + relay_in[kind, 1].astype(F32)).astype(LINK)
        pass_on(kind, 1, 1, upper, minus[kind])
    mine = partial(3, 0) + partial(3, 1)
    first_row = (leaf * 2 + core) * ROWS
    row = lax.broadcasted_iota(jnp.int32, (ROWS, RANK), 0) + first_row
    chosen = jnp.where(row == skeleton[pl.ds(node, 1), :], 1.0, 0.0)
    skeleton_points = jnp.dot(
        tree_points[...].astype(BF16), chosen.astype(BF16), preferred_element_type=F32
    )
    for copy in nears:
        copy.wait_recv()
    for kind in range(2):
        for side in range(2):
            mine = mine + near_in[kind, side].astype(F32)
    rows = mine
    samples[...] = rows

    table[0:256, :] = lax.dot_general(
        rows, rows, (((0,), (0,)), ((), ())), precision=HIGHEST, preferred_element_type=F32
    )
    table[128:256, 0:128] = jnp.zeros((128, 128), F32)
    table[128:136, 0:128] = skeleton_points[:, 0:128]
    table[136:144, 0:128] = skeleton_points[:, 128:256]
    table[256:512, :] = lax.dot_general(
        chosen, rows, (((0,), (0,)), ((), ())), precision=HIGHEST, preferred_element_type=F32
    )
    start = pl.multiple_of((1 - core) * 256, 256)
    swap_table = send(
        table.at[pl.ds(start, 256)], other_table, table_sems.at[0], table_sems.at[1], other
    )
    swap_table.wait()
    keep = pl.multiple_of(core * 256, 256)
    other_table[...] += table[pl.ds(keep, 256), :]

    def chunk(where):
        first = (where[0] * 8 + where[1] * 2 + where[2] % 2) * 8
        return other_table.at[pl.ds(pl.multiple_of(first, 8), 8)]

    spreads = []
    for slot, where, who in mates:
        spreads.append(
            send(chunk(where), pieces.at[slot], piece_send.at[slot], piece_recv.at[slot], who)
        )
    sums = chunk((x, y, z))[...]
    for copy in spreads:
        copy.wait_recv()
    for slot, _, _ in mates:
        sums = sums + pieces[slot]
    piece[0] = sums[:, 0:128]
    piece[1] = sums[:, 128:256]
    full_a[core, x, y, z] = sums[:, 0:128]
    full_b[core, y, x, z] = sums[:, 128:256]
    for copy in spreads:
        copy.wait_send()

    stages = []
    for k, who in enumerate(column):
        stages.append(send(piece.at[0], full_a.at[core, x, y, z], z_send.at[2 * k], z_recv.at[2 * k], who))
        stages.append(
            send(piece.at[1], full_b.at[core, y, x, z], z_send.at[2 * k + 1], z_recv.at[2 * k + 1], who)
        )
    for copy in stages:
        copy.wait()

    cuts8, cuts4 = (pl.ds(0, 4), pl.ds(4, 4)), (pl.ds(0, 2), pl.ds(2, 2))
    half_a, half_b = full_a.at[core], full_b.at[core]

    def push(ref, sems, k, who):
        return send(ref, ref, sems.at[2 * k], sems.at[2 * k + 1], who)

    first = [push(half_a.at[x, y], y_sems, 0, above), push(half_a.at[x, y], y_sems, 1, below)]
    second = [push(half_b.at[y, x], x_sems, 0, right), push(half_b.at[y, x], x_sems, 1, left)]
    first[0].wait_recv()
    first.append(push(half_a.at[x, last_y, cuts8[0]], y_sems, 2, above))
    second[0].wait_recv()
    second.append(push(half_b.at[y, behind, cuts8[0]], x_sems, 2, right))
    first[1].wait_recv()
    first.append(push(half_a.at[x, next_y, cuts8[1]], y_sems, 3, below))
    second[1].wait_recv()
    second.append(push(half_b.at[y, ahead, cuts8[1]], x_sems, 3, left))
    for copy in first[2:]:
        copy.wait_recv()
    first.append(push(half_a.at[x], x_sems, 4, right))
    first.append(push(half_a.at[x], x_sems, 5, left))
    for copy in second[2:]:
        copy.wait_recv()
    second.append(push(half_b.at[y], y_sems, 4, above))
    second.append(push(half_b.at[y], y_sems, 5, below))
    swaps = []

    def hand(ref):
        swaps.append(push(ref, swap_sems, len(swaps), other))

    hand(half_a.at[x])
    hand(half_b.at[y])
    first[4].wait_recv()
    first.append(push(half_a.at[behind, cuts4[0]], x_sems, 6, right))
    second[4].wait_recv()
    second.append(push(half_b.at[last_y, cuts4[0]], y_sems, 6, above))
    first[5].wait_recv()
    first.append(push(half_a.at[ahead, cuts4[1]], x_sems, 7, left))
    second[5].wait_recv()
    second.append(push(half_b.at[next_y, cuts4[1]], y_sems, 7, below))
    hand(half_a.at[behind])
    hand(half_b.at[last_y])
    hand(half_a.at[ahead])
    hand(half_b.at[next_y])
    for copy in first[6:]:
        copy.wait_recv()
    hand(half_a.at[across])
    for copy in second[6:]:
        copy.wait_recv()
    hand(half_b.at[(y + 2) % 4])
    for copy in first + second:
        copy.wait_send()
    for copy in swaps:
        copy.wait()
    for copy in relays + nears + list(swap.values()):
        copy.wait_send()


def collect(parts, skeleton, tree_points):
    dma = pltpu.SemaphoreType.DMA
    return pl.pallas_call(
        collect_kernel,
        out_shape=(
            jax.ShapeDtypeStruct((ROWS, RANK), F32),
            jax.ShapeDtypeStruct((2, 4, 4, 8, 8, 128), F32),
            jax.ShapeDtypeStruct((2, 4, 4, 8, 8, 128), F32),
        ),
        in_specs=[VMEM] * 3,
        out_specs=(VMEM,) * 3,
        scratch_shapes=[
            pltpu.VMEM((2, 4, ROWS, RANK), F32),
            pltpu.VMEM((2, ROWS, RANK), LINK),
            pltpu.VMEM((2, 2, 128, RANK), LINK),
            pltpu.VMEM((2, 2, ROWS, RANK), LINK),
            pltpu.VMEM((2, 2, ROWS, RANK), LINK),
            pltpu.VMEM((512, RANK), F32),
            pltpu.VMEM((256, RANK), F32),
            pltpu.VMEM((2, 8, 128), F32),
            pltpu.VMEM((32, 8, RANK), F32),
            dma((2, 4)), dma((2, 4)), dma((2, 2, 2)), dma((2, 2, 2, 2)), dma((2,)), dma((32,)), dma((32,)),
            dma((14,)), dma((14,)), dma((16,)), dma((16,)), dma((16,)),
        ],
        compiler_params=pltpu.CompilerParams(
            collective_id=1, has_side_effects=True, vmem_limit_bytes=32 << 20
        ),
        name="collect",
    )(parts, skeleton, tree_points)


def fold(factors, lines):
    a, b, c, d = (factor * values for factor, values in zip(factors, lines, strict=True))
    return (a + b) + (c + d)


def pivots(entry):
    def pair(a, b, c):
        scale = lax.rsqrt(a)
        return scale, b * scale, a * lax.rsqrt(a * (a * c - b * b))

    r0, l10, r1 = pair(entry(0, 0), entry(1, 0), entry(1, 1))
    l20, l30 = entry(2, 0) * r0, entry(3, 0) * r0
    l21, l31 = (entry(2, 1) - l20 * l10) * r1, (entry(3, 1) - l30 * l10) * r1
    r2, l32, r3 = pair(
        entry(2, 2) - (l20 * l20 + l21 * l21),
        entry(3, 2) - (l30 * l20 + l31 * l21),
        entry(3, 3) - (l30 * l30 + l31 * l31),
    )

    def solve(values):
        v0 = values[0] * r0
        v1 = (values[1] - v0 * l10) * r1
        v2 = (values[2] - (v0 * l20 + v1 * l21)) * r2
        v3 = ((values[3] - (v0 * l30 + v1 * l31)) - v2 * l32) * r3
        return [v0, v1, v2, v3]

    return solve


def finish_kernel(full_a, full_b, samples, basis, coupling, work, chosen):
    node = lax.axis_index("leaf") // 32
    row = lax.broadcasted_iota(jnp.int32, (RANK, RANK), 0)
    col = lax.broadcasted_iota(jnp.int32, (RANK, RANK), 1)
    skeleton_points, sizes = [], []
    for n in range(4):
        for at_x in range(4):
            for at_y in range(4):
                span = pl.ds(at_x * 64 + at_y * 16, 16)
                for kind, target in enumerate((work, chosen)):
                    planes = pl.ds(2 * n, 2)
                    target[n, span, 0:128] = full_a[kind, at_x, at_y, planes].reshape(16, 128)
                    target[n, span, 128:256] = full_b[kind, at_y, at_x, planes].reshape(16, 128)
        skeleton_points.append(
            jnp.concatenate([work[n, 128:136, 0:128], work[n, 136:144, 0:128]], axis=1)
        )
        gram = work[n]
        on_diagonal = jnp.where(row == col, gram, 0.0)
        trace = jnp.sum(jnp.sum(on_diagonal, axis=0, keepdims=True), axis=1, keepdims=True)
        work[n] = gram * (1.0 / trace) + jnp.where(row == col, 0.01, 0.0)
        sizes.append(lax.rsqrt(trace))

    middles = []
    for k in range(2):
        row_side = features(skeleton_points[2 * k], 4.0, True).T.astype(BF16)
        col_side = features(skeleton_points[2 * k + 1], 1.0, False).astype(BF16)
        kernel_skel = jnp.exp(jnp.dot(row_side, col_side, preferred_element_type=F32))
        right = jnp.dot(kernel_skel, chosen[2 * k + 1], precision=HIGH, preferred_element_type=F32)
        middles.append(
            lax.dot_general(
                chosen[2 * k], right, (((0,), (0,)), ((), ())),
                precision=HIGH, preferred_element_type=F32,
            )
        )

    lane8 = lax.broadcasted_iota(jnp.int32, (8, 128), 1)
    row8 = lax.broadcasted_iota(jnp.int32, (8, 128), 0)
    group8 = (lane8 // 32) * 32
    lane = lax.broadcasted_iota(jnp.int32, (32, 128), 1)
    for p in range(8):
        top = 32 * p
        aligned = (top // 128) * 128
        packed = jnp.zeros((32, 128), F32)
        for n in range(4):
            block = work[n, top : top + 32, aligned : aligned + 128]
            turn = (32 * n - (top - aligned)) % 128
            if turn:
                block = pltpu.roll(block, turn, 1)
            packed = jnp.where(lane // 32 == n, block, packed)
        left = [packed[8 * g : 8 * g + 8] for g in range(4)]
        inverse = [jnp.where(lane8 - group8 == row8 + 8 * g, 1.0, 0.0) for g in range(4)]
        for j in range(0, 32, 4):
            own, inner = j // 8, j % 8
            spread = {
                g: [
                    jnp.take_along_axis(left[g], group8 + (j + t), axis=1, mode="promise_in_bounds")
                    for t in range(4)
                ]
                for g in range(own, 4)
            }

            def line(tile, t, inner=inner):
                return jnp.broadcast_to(tile[inner + t : inner + t + 1, :], (8, 128))

            solve = pivots(lambda t, u: line(spread[own][u], t))
            left_rows = solve([line(left[own], t) for t in range(4)])
            inverse_rows = solve([line(inverse[own], t) for t in range(4)])
            for g in range(own, 4):
                if g == own and inner == 4:
                    continue
                factors = solve(spread[g])
                if g == own:
                    factors = [jnp.where(row8 > 3, factor, 0.0) for factor in factors]
                left[g] = left[g] - fold(factors, left_rows)
                inverse[g] = inverse[g] - fold(factors, inverse_rows)
            for t in range(4):
                inverse[own] = jnp.where(row8 == inner + t, inverse_rows[t], inverse[own])
        packed = jnp.concatenate(inverse, axis=0)
        diagonal = jnp.concatenate([jnp.where(lane // 32 == n, packed, 0.0) for n in range(4)], axis=0)
        stacked = jnp.concatenate([work[n, top : top + 32, :] for n in range(4)], axis=0)
        srow = lax.broadcasted_iota(jnp.int32, (128, RANK), 0)
        scol = lax.broadcasted_iota(jnp.int32, (128, RANK), 1)
        identity = jnp.where(srow % 32 == scol % 32, 1.0, 0.0)
        stacked = jnp.where(scol // 32 == p, identity, stacked)
        solved = jnp.dot(diagonal, stacked, precision=HIGHEST, preferred_element_type=F32)
        done = jnp.where(scol < top + 32, solved, 0.0)
        for n in range(4):
            work[n, top : top + 32, :] = done[32 * n : 32 * n + 32]
        rest = RANK - top - 32
        if rest:
            turned = solved.T[top + 32 :, :]
            tlane = lax.broadcasted_iota(jnp.int32, (rest, 128), 1)
            tcol = lax.broadcasted_iota(jnp.int32, (rest, RANK), 1)
            for n in range(4):
                update = jnp.dot(
                    jnp.where(tlane // 32 == n, turned, 0.0), solved,
                    precision=HIGHEST, preferred_element_type=F32,
                )
                work[n, top + 32 :, :] = jnp.where(tcol // 32 == p, 0.0, work[n, top + 32 :, :]) - update

    last = (((1,), (1,)), ((), ()))
    size = sum(jnp.where(node == n, sizes[n], 0.0) for n in range(4))
    basis[...] = (128.0 * size) * lax.dot_general(
        samples[...], work[node], last, precision=HIGH, preferred_element_type=F32
    )
    for k in range(2):
        half = jnp.dot(work[2 * k], middles[k], precision=HIGH, preferred_element_type=F32)
        coupling[k] = ((16384.0 / math.sqrt(RANK)) * sizes[2 * k] * sizes[2 * k + 1]) * lax.dot_general(
            half, work[2 * k + 1], last, precision=HIGH, preferred_element_type=F32
        )


def finish(full_a, full_b, samples):
    return pl.pallas_call(
        finish_kernel,
        out_shape=(
            jax.ShapeDtypeStruct((ROWS, RANK), F32),
            jax.ShapeDtypeStruct((2, RANK, RANK), F32),
        ),
        in_specs=[VMEM] * 3,
        out_specs=(VMEM,) * 2,
        scratch_shapes=[pltpu.VMEM((4, RANK, RANK), F32), pltpu.VMEM((4, RANK, RANK), F32)],
        compiler_params=pltpu.CompilerParams(vmem_limit_bytes=32 << 20),
        name="finish",
    )(full_a, full_b, samples)


def body(points, omega, tree_order, sibling_blocks, cousin_blocks, skeleton):
    blocks, row_points, picks, tree_points = gather(
        points, omega, tree_order.reshape(1, ROWS), sibling_blocks, cousin_blocks
    )
    parts = sample(blocks, row_points, picks)
    samples, full_a, full_b = collect(parts, skeleton, tree_points)
    return finish(full_a, full_b, samples)


def solution(mesh):
    return jax.shard_map(
        body,
        mesh=mesh,
        in_specs=(
            P(None, ("leaf", "sub")),
            P(None, ("leaf", "sub")),
            P(("leaf", "sub")),
            P("leaf", None),
            P("leaf", None),
            P(),
        ),
        out_specs=(P(("leaf", "sub"), None), P()),
        check_vma=False,
    )
```

time: 127 us -> 112 us (0.88)
  Pallas kernels: 123 us -> 108 us
    pallas_call x1, Pallas kernels: 34.9 us -> 28.6 us  [gather(): pl.pallas_call(gather_kernel, out_shape=(jax.ShapeDtypeStruct((32, SPAN,...]
    pallas_call x1, Pallas kernels: 16.2 us -> 11.8 us  [sample(): pl.pallas_call(sample_kernel, out_shape=jax.ShapeDtypeStruct((2, 2, 4, RO...]
    pallas_call x1, Pallas kernels: 55.3 us -> 51 us  [collect(): pl.pallas_call(collect_kernel, out_shape=(jax.ShapeDtypeStruct((ROWS, RAN...]
where the time goes in v3:
time: 112 us
  Pallas kernels  108 us (96%)
  local copies, waits for them, and re-layouts  3.51 us (3%)
    pallas_call x1, Pallas kernels, collect(): pl.pallas_call(collect_kernel, out_shape=(jax.ShapeDtypeStruct((ROWS, RAN...  51 us
    pallas_call x1, Pallas kernels, gather(): pl.pallas_call(gather_kernel, out_shape=(jax.ShapeDtypeStruct((32, SPAN,...  28.6 us
    pallas_call x1, Pallas kernels, finish(): pl.pallas_call(finish_kernel, out_shape=(jax.ShapeDtypeStruct((ROWS, RANK...  16.1 us
    pallas_call x1, Pallas kernels, sample(): pl.pallas_call(sample_kernel, out_shape=jax.ShapeDtypeStruct((2, 2, 4, RO...  11.8 us
    unnamed x12, local copies, waits for them, and re-layouts  3.51 us

profile of v3, /device:TPU:1, one launch (start us, length us, event | category | flops | bytes accessed | tf_op | source)
XLA Modules:
  0.0 111.8 jit_solution(1198316483904870155)
XLA Ops:
  0.6 0.0 copy-start
  0.6 0.8 copy-done
  1.5 0.0 copy-start.2
  1.5 0.7 copy-done.2
  2.2 0.0 copy-start.3
  2.2 0.7 copy-done.3
  2.8 0.0 copy-start.4
  2.8 0.7 copy-done.4
  3.5 0.0 copy-start.5
  3.5 0.7 copy-done.5
  4.2 0.0 copy-start.1
  4.2 28.6 %gather.1 = (bf16[32,288,128]{2,1,0:T(8,128)(2,1)S(1)}, bf16[2,8,16,256]{3,2,1,0:T(8,128)(2,1)S(1)}, s32[8,128]{1,0:T(8,128)S(1)}, f32[8,256]{1,0:T(8,128)S(1)}) custom-call(bf16[8,256]{1,0:T(8,128)(2,1)S(1)} %copy-done.2, bf16[128,256]{1,0:T(8,128)(2,1)S(1)} %copy-done, s32[1,256]{1,0:T(1,128)S(1)} %bitcast.1, s32[1,16]{1,0:T(1,128)S(1)} %copy-done.4, ...), custom_call_target="tpu_custom_call" | custom-call | tf_op jit(solution)/shard_map/gather/pallas_call | solution.py:228
  32.8 11.8 %sample.1.parts = f32[2,2,4,256,256]{4,3,2,1,0:T(8,128)S(1)} custom-call(bf16[32,288,128]{2,1,0:T(8,128)(2,1)S(1)} %get-tuple-element.9.blocks, bf16[2,8,16,256]{3,2,1,0:T(8,128)(2,1)S(1)} %get-tuple-element.10.row_points, s32[8,128]{1,0:T(8,128)S(1)} %get-tuple-element.11.picks), custom_call_target="tpu_custom_call" | custom-call | tf_op jit(solution)/shard_map/sample/pallas_call | solution.py:323
  44.6 0.0 copy-done.1
  44.7 51.0 %collect.1 = (f32[256,256]{1,0:T(8,128)S(1)}, f32[2,4,4,8,8,128]{5,4,3,2,1,0:T(8,128)S(1)}, f32[2,4,4,8,8,128]{5,4,3,2,1,0:T(8,128)S(1)}) custom-call(f32[2,2,4,256,256]{4,3,2,1,0:T(8,128)S(1)} %sample.1.parts, s32[4,256]{1,0:T(4,128)S(1)} %copy-done.1, f32[8,256]{1,0:T(8,128)S(1)} %get-tuple-element.12.tree_points), custom_call_target="tpu_custom_call" | custom-call | tf_op jit(solution)/shard_map/collect/pallas_call | solution.py:534
  95.7 16.1 %finish.1 = (f32[256,256]{1,0:T(8,128)}, f32[2,256,256]{2,1,0:T(8,128)}) custom-call(f32[2,4,4,8,8,128]{5,4,3,2,1,0:T(8,128)S(1)} %get-tuple-element.13.full_a, f32[2,4,4,8,8,128]{5,4,3,2,1,0:T(8,128)S(1)} %get-tuple-element.14.full_b, f32[256,256]{1,0:T(8,128)S(1)} %get-tuple-element.15.samples), custom_call_target="tpu_custom_call" | custom-call | tf_op jit(solution)/shard_map/finish/pallas_call | solution.py:705
Async XLA Ops:
  0.6 0.8 copy-start
  1.5 0.7 copy-start.2
  2.2 0.7 copy-start.3
  2.8 0.7 copy-start.4
  3.5 0.7 copy-start.5
  4.2 40.5 %copy-start.1 = (s32[4,256]{1,0:T(4,128)S(1)}, s32[4,256]{1,0:T(4,128)}, u32[]{:S(2)}) copy-start(s32[4,256]{1,0:T(4,128)} %skeleton.1) | copy-start | bytes 12292

commit v4 on v3

--- a/solution.py
+++ b/solution.py
@@ -139,10 +139,18 @@
     own[272:288, :] = columns[:, 128:]
     halves = (pl.ds(0, SPAN // 2), pl.ds(SPAN // 2, SPAN // 2))
 
-    def hop(k, src, dst, who):
-        return send(src, dst, z_send.at[k], z_recv.at[k], who)
-
-    hops = [hop(0, own, blocks.at[7], upward), hop(1, own, blocks.at[1], downward)]
+    hops = {}
+
+    def hop(source, source_dz, dz, half, who):
+        ref = source if source_dz is None else source.at[source_dz]
+        hops[dz, half] = send(
+            ref.at[halves[half]], blocks.at[dz, halves[half]],
+            z_send.at[dz, half], z_recv.at[dz, half], who,
+        )
+
+    for step in range(2):
+        hop(own, None, 7, step, upward)
+        hop(own, None, 1, 1 - step, downward)
 
     for copy in loads[2:]:
         copy.wait()
@@ -168,59 +176,67 @@
 
     outs, fars = {}, []
 
-    def fan_out(k, kind, dz):
-        block = blocks.at[dz]
-        outs[k] = (
-            send(block, blocks.at[24 + dz], out_send.at[2 * k], out_recv.at[2 * k], plus[kind]),
-            send(block, blocks.at[8 + dz], out_send.at[2 * k + 1], out_recv.at[2 * k + 1], minus[kind]),
-        )
+    def fan_out(k, kind, dz, half):
+        block = blocks.at[dz, halves[half]]
+        for side, (at, who) in enumerate(((24, plus[kind]), (8, minus[kind]))):
+            outs[k, side, half] = send(
+                block, blocks.at[at + dz, halves[half]],
+                out_send.at[k, side, half], out_recv.at[k, side, half], who,
+            )
 
     def relay(k, kind, dz):
-        for side, (at, half, who) in enumerate(((24, halves[0], plus[kind]), (8, halves[1], minus[kind]))):
-            outs[k][side].wait_recv()
+        for side, (at, who) in enumerate(((24, plus[kind]), (8, minus[kind]))):
+            outs[k, side, side].wait_recv()
             fars.append(
                 send(
-                    blocks.at[at + dz, half], blocks.at[16 + dz, half],
-                    far_send.at[2 * k + side], far_recv.at[2 * k + side], who,
+                    blocks.at[at + dz, halves[side]], blocks.at[16 + dz, halves[side]],
+                    far_send.at[k, side], far_recv.at[k, side], who,
                 )
             )
 
-    hops[0].wait_recv()
-    hops.append(hop(2, blocks.at[7], blocks.at[6], upward))
-    hops[1].wait_recv()
-    hops.append(hop(3, blocks.at[1], blocks.at[2], downward))
-    fan_out(0, 1, mate)
-    hops[2].wait_recv()
-    hops.append(hop(4, blocks.at[6], blocks.at[5], upward))
-    fan_out(1, 1, 6)
-    hops[3].wait_recv()
-    hops.append(hop(5, blocks.at[2], blocks.at[3], downward))
-    fan_out(2, 0, 2)
+    for step in range(2):
+        hops[7, step].wait_recv()
+        hop(blocks, 7, 6, step, upward)
+        hops[1, 1 - step].wait_recv()
+        hop(blocks, 1, 2, 1 - step, downward)
+    for half in range(2):
+        fan_out(0, 1, mate, half)
+    for step in range(2):
+        hops[6, step].wait_recv()
+        hop(blocks, 6, 5, step, upward)
+        fan_out(1, 1, 6, step)
+        hops[2, 1 - step].wait_recv()
+        hop(blocks, 2, 3, 1 - step, downward)
+        fan_out(2, 0, 2, 1 - step)
     relay(0, 1, mate)
-    hops[4].wait_recv()
-    hops.append(hop(6, blocks.at[5, halves[0]], blocks.at[4, halves[0]], upward))
-    fan_out(3, 0, 5)
-    hops[5].wait_recv()
-    hops.append(hop(7, blocks.at[3, halves[1]], blocks.at[4, halves[1]], downward))
-    fan_out(4, 1, 3)
+    hops[5, 0].wait_recv()
+    hop(blocks, 5, 4, 0, upward)
+    fan_out(3, 0, 5, 0)
+    hops[3, 1].wait_recv()
+    hop(blocks, 3, 4, 1, downward)
+    fan_out(4, 1, 3, 1)
+    hops[5, 1].wait_recv()
+    fan_out(3, 0, 5, 1)
+    hops[3, 0].wait_recv()
+    fan_out(4, 1, 3, 0)
     relay(1, 1, 6)
     relay(2, 0, 2)
-    hops[6].wait_recv()
-    hops[7].wait_recv()
-    fan_out(5, 0, 4)
+    for half in range(2):
+        hops[4, half].wait_recv()
+        fan_out(5, 0, 4, half)
     relay(3, 0, 5)
     relay(4, 1, 3)
     relay(5, 0, 4)
+    for k in range(6):
+        for side in range(2):
+            outs[k, side, 1 - side].wait_recv()
     for copy in small:
         copy.wait()
     picks[...] = pick_slots(lists, x, y, z)
     for copy in fars:
         copy.wait()
-    for copy in hops:
+    for copy in list(hops.values()) + list(outs.values()):
         copy.wait_send()
-    for pair in outs.values():
-        for copy in pair:
-            copy.wait_send()
 
 
 def gather(points, omega, order, siblings, cousins):
@@ -246,7 +262,7 @@
             pltpu.VMEM((16, ROWS), BF16),
             pltpu.VMEM((8, 128), jnp.int32),
             pltpu.VMEM((2, 4, 8, 128), jnp.int32),
-            dma((8,)), dma((8,)), dma((12,)), dma((12,)), dma((12,)), dma((12,)),
+            dma((8, 2)), dma((8, 2)), dma((6, 2, 2)), dma((6, 2, 2)), dma((6, 2)), dma((6, 2)),
             dma((2, 7)), dma((2, 7)), dma((2, 4)), dma((2, 4)),
         ],
         compiler_params=pltpu.CompilerParams(
@@ -341,7 +357,7 @@
     samples, full_a, full_b,
     other_core, relay_out, relay_in, near_out, near_in, table, other_table, piece, pieces,
     core_send, core_recv, relay_sems, near_sems, table_sems, piece_send, piece_recv,
-    z_send, z_recv, y_sems, x_sems, swap_sems,
+    z_send, z_recv, y_sems, x_sems,
 ):
     x, y, z, core = place()
     leaf = z * 16 + y * 4 + x
@@ -354,8 +370,12 @@
                 if dz or dy or dx:
                     where = ((x + dx) % 4, (y + dy) % 4, node * 2 + (z + dz) % 2)
                     mates.append((dz * 16 + dy * 4 + dx, where, device(*where, core)))
-    column = [device(x, y, (z + dz) % 8, core) for dz in range(1, 8)]
-    strangers = [device(x, y, ((node + dn) % 4) * 2 + dz, core) for dn in range(1, 4) for dz in range(2)]
+    pair = z // 4
+    column = [device(x, y, (z + dz) % 8, pair) for dz in range(8)]
+    strangers = [
+        device(x, y, ((node + dn) % 4) * 2 + dz, c) for dn in range(1, 4) for dz in range(2) for c in range(2)
+    ]
+    strangers.append(device(x, y, node * 2 + (z + 1) % 2, 1 - core))
     greet([other] + [who for _, _, who in mates] + strangers)
     right, left = device((x + 1) % 4, y, z, core), device((x + 3) % 4, y, z, core)
     above, below = device(x, (y + 1) % 4, z, core), device(x, (y + 3) % 4, z, core)
@@ -458,73 +478,98 @@
         sums = sums + pieces[slot]
     piece[0] = sums[:, 0:128]
     piece[1] = sums[:, 128:256]
-    full_a[core, x, y, z] = sums[:, 0:128]
-    full_b[core, y, x, z] = sums[:, 128:256]
     for copy in spreads:
         copy.wait_send()
 
-    stages = []
-    for k, who in enumerate(column):
-        stages.append(send(piece.at[0], full_a.at[core, x, y, z], z_send.at[2 * k], z_recv.at[2 * k], who))
-        stages.append(
-            send(piece.at[1], full_b.at[core, y, x, z], z_send.at[2 * k + 1], z_recv.at[2 * k + 1], who)
+    home_a, home_b = full_a.at[x, y, z % 4, core], full_b.at[y, x, z % 4, core]
+
+    def drop(dz, half):
+        return pltpu.make_async_remote_copy(
+            src_ref=piece.at[half],
+            dst_ref=(home_a, home_b)[half],
+            send_sem=z_send.at[dz, half],
+            recv_sem=z_recv.at[z % 4, core, half],
+            device_id=column[dz],
+            device_id_type=MESH,
         )
-    for copy in stages:
-        copy.wait()
-
-    cuts8, cuts4 = (pl.ds(0, 4), pl.ds(4, 4)), (pl.ds(0, 2), pl.ds(2, 2))
-    half_a, half_b = full_a.at[core], full_b.at[core]
+
+    def arrival(plane, c, half):
+        landing = (full_a.at[x, y, plane, c], full_b.at[y, x, plane, c])[half]
+        return pltpu.make_async_remote_copy(
+            src_ref=piece.at[half],
+            dst_ref=landing,
+            send_sem=z_send.at[0, half],
+            recv_sem=z_recv.at[plane, c, half],
+            device_id=other,
+            device_id_type=MESH,
+        )
+
+    for dz in (4, 3, 5, 2, 6, 1, 7):
+        for half in range(2):
+            drop(dz, half).start()
+
+    @pl.when(pair == core)
+    def _():
+        home_a[...] = piece[0]
+        home_b[...] = piece[1]
+
+    @pl.when(pair != core)
+    def _():
+        for half in range(2):
+            drop(0, half).start()
+
+    for plane in range(4):
+        for c in range(2):
+
+            @pl.when((core * 4 + plane != z) | (core != c))
+            def _(plane=plane, c=c):
+                for half in range(2):
+                    arrival(plane, c, half).wait_recv()
+
+    cuts = (pl.ds(0, 2), pl.ds(2, 2))
 
     def push(ref, sems, k, who):
         return send(ref, ref, sems.at[2 * k], sems.at[2 * k + 1], who)
 
-    first = [push(half_a.at[x, y], y_sems, 0, above), push(half_a.at[x, y], y_sems, 1, below)]
-    second = [push(half_b.at[y, x], x_sems, 0, right), push(half_b.at[y, x], x_sems, 1, left)]
-    first[0].wait_recv()
-    first.append(push(half_a.at[x, last_y, cuts8[0]], y_sems, 2, above))
-    second[0].wait_recv()
-    second.append(push(half_b.at[y, behind, cuts8[0]], x_sems, 2, right))
-    first[1].wait_recv()
-    first.append(push(half_a.at[x, next_y, cuts8[1]], y_sems, 3, below))
-    second[1].wait_recv()
-    second.append(push(half_b.at[y, ahead, cuts8[1]], x_sems, 3, left))
-    for copy in first[2:]:
+    def ring(at, sems, first_k, forward, backward):
+        return [
+            push(at.at[cuts[0]], sems, first_k, forward),
+            push(at.at[cuts[1]], sems, first_k + 1, backward),
+            push(at.at[cuts[1]], sems, first_k + 2, forward),
+            push(at.at[cuts[0]], sems, first_k + 3, backward),
+        ]
+
+    def pass_along(copies, sems, first_k, before, after, forward, backward):
+        copies[0].wait_recv()
+        copies.append(push(before.at[cuts[0]], sems, first_k + 4, forward))
+        copies[1].wait_recv()
+        copies.append(push(after.at[cuts[1]], sems, first_k + 5, backward))
+
+    first = ring(full_a.at[x, y], y_sems, 0, above, below)
+    second = ring(full_b.at[y, x], x_sems, 0, right, left)
+    pass_along(first, y_sems, 0, full_a.at[x, last_y], full_a.at[x, next_y], above, below)
+    pass_along(second, x_sems, 0, full_b.at[y, behind], full_b.at[y, ahead], right, left)
+    for copy in first[2:6]:
         copy.wait_recv()
-    first.append(push(half_a.at[x], x_sems, 4, right))
-    first.append(push(half_a.at[x], x_sems, 5, left))
-    for copy in second[2:]:
+    third = ring(full_a.at[x], x_sems, 6, right, left)
+    for copy in second[2:6]:
         copy.wait_recv()
-    second.append(push(half_b.at[y], y_sems, 4, above))
-    second.append(push(half_b.at[y], y_sems, 5, below))
-    swaps = []
-
-    def hand(ref):
-        swaps.append(push(ref, swap_sems, len(swaps), other))
-
-    hand(half_a.at[x])
-    hand(half_b.at[y])
-    first[4].wait_recv()
-    first.append(push(half_a.at[behind, cuts4[0]], x_sems, 6, right))
-    second[4].wait_recv()
-    second.append(push(half_b.at[last_y, cuts4[0]], y_sems, 6, above))
-    first[5].wait_recv()
-    first.append(push(half_a.at[ahead, cuts4[1]], x_sems, 7, left))
-    second[5].wait_recv()
-    second.append(push(half_b.at[next_y, cuts4[1]], y_sems, 7, below))
-    hand(half_a.at[behind])
-    hand(half_b.at[last_y])
-    hand(half_a.at[ahead])
-    hand(half_b.at[next_y])
-    for copy in first[6:]:
+    fourth = ring(full_b.at[y], y_sems, 6, above, below)
+    pass_along(third, x_sems, 6, full_a.at[behind], full_a.at[ahead], right, left)
+    pass_along(fourth, y_sems, 6, full_b.at[last_y], full_b.at[next_y], above, below)
+    for copy in third[2:] + fourth[2:]:
         copy.wait_recv()
-    hand(half_a.at[across])
-    for copy in second[6:]:
-        copy.wait_recv()
-    hand(half_b.at[(y + 2) % 4])
-    for copy in first + second:
+    for copy in first + second + third + fourth:
         copy.wait_send()
-    for copy in swaps:
-        copy.wait()
+    for dz in range(1, 8):
+        for half in range(2):
+            drop(dz, half).wait_send()
+
+    @pl.when(pair != core)
+    def _():
+        for half in range(2):
+            drop(0, half).wait_send()
+
     for copy in relays + nears + list(swap.values()):
         copy.wait_send()
 
@@ -535,8 +580,8 @@
         collect_kernel,
         out_shape=(
             jax.ShapeDtypeStruct((ROWS, RANK), F32),
-            jax.ShapeDtypeStruct((2, 4, 4, 8, 8, 128), F32),
-            jax.ShapeDtypeStruct((2, 4, 4, 8, 8, 128), F32),
+            jax.ShapeDtypeStruct((4, 4, 4, 2, 8, 128), F32),
+            jax.ShapeDtypeStruct((4, 4, 4, 2, 8, 128), F32),
         ),
         in_specs=[VMEM] * 3,
         out_specs=(VMEM,) * 3,
@@ -551,7 +596,7 @@
             pltpu.VMEM((2, 8, 128), F32),
             pltpu.VMEM((32, 8, RANK), F32),
             dma((2, 4)), dma((2, 4)), dma((2, 2, 2)), dma((2, 2, 2, 2)), dma((2,)), dma((32,)), dma((32,)),
-            dma((14,)), dma((14,)), dma((16,)), dma((16,)), dma((16,)),
+            dma((8, 2)), dma((4, 2, 2)), dma((24,)), dma((24,)),
         ],
         compiler_params=pltpu.CompilerParams(
             collective_id=1, has_side_effects=True, vmem_limit_bytes=32 << 20
@@ -589,19 +634,24 @@
     return solve
 
 
-def finish_kernel(full_a, full_b, samples, basis, coupling, work, chosen):
-    node = lax.axis_index("leaf") // 32
+def finish_kernel(
+    full_a, full_b, samples, basis, coupling, work, chosen, factor_out, factor_in, factor_sems, coupling_sems
+):
+    x, y, z, core = place()
+    other = device(x, y, z, 1 - core)
+    greet([other])
+    node = z // 2
     row = lax.broadcasted_iota(jnp.int32, (RANK, RANK), 0)
     col = lax.broadcasted_iota(jnp.int32, (RANK, RANK), 1)
     skeleton_points, sizes = [], []
-    for n in range(4):
+    for n in range(2):
         for at_x in range(4):
             for at_y in range(4):
                 span = pl.ds(at_x * 64 + at_y * 16, 16)
+                planes = pl.ds(2 * n, 2)
                 for kind, target in enumerate((work, chosen)):
-                    planes = pl.ds(2 * n, 2)
-                    target[n, span, 0:128] = full_a[kind, at_x, at_y, planes].reshape(16, 128)
-                    target[n, span, 128:256] = full_b[kind, at_y, at_x, planes].reshape(16, 128)
+                    target[n, span, 0:128] = full_a[at_x, at_y, planes, kind].reshape(16, 128)
+                    target[n, span, 128:256] = full_b[at_y, at_x, planes, kind].reshape(16, 128)
         skeleton_points.append(
             jnp.concatenate([work[n, 128:136, 0:128], work[n, 136:144, 0:128]], axis=1)
         )
@@ -611,43 +661,36 @@
         work[n] = gram * (1.0 / trace) + jnp.where(row == col, 0.01, 0.0)
         sizes.append(lax.rsqrt(trace))
 
-    middles = []
-    for k in range(2):
-        row_side = features(skeleton_points[2 * k], 4.0, True).T.astype(BF16)
-        col_side = features(skeleton_points[2 * k + 1], 1.0, False).astype(BF16)
-        kernel_skel = jnp.exp(jnp.dot(row_side, col_side, preferred_element_type=F32))
-        right = jnp.dot(kernel_skel, chosen[2 * k + 1], precision=HIGH, preferred_element_type=F32)
-        middles.append(
-            lax.dot_general(
-                chosen[2 * k], right, (((0,), (0,)), ((), ())),
-                precision=HIGH, preferred_element_type=F32,
-            )
-        )
+    row_side = features(skeleton_points[0], 4.0, True).T.astype(BF16)
+    col_side = features(skeleton_points[1], 1.0, False).astype(BF16)
+    kernel_skel = jnp.exp(jnp.dot(row_side, col_side, preferred_element_type=F32))
+    right = jnp.dot(kernel_skel, chosen[1], precision=HIGH, preferred_element_type=F32)
+    middle = lax.dot_general(
+        chosen[0], right, (((0,), (0,)), ((), ())), precision=HIGH, preferred_element_type=F32
+    )
 
     lane8 = lax.broadcasted_iota(jnp.int32, (8, 128), 1)
     row8 = lax.broadcasted_iota(jnp.int32, (8, 128), 0)
-    group8 = (lane8 // 32) * 32
-    lane = lax.broadcasted_iota(jnp.int32, (32, 128), 1)
-    for p in range(8):
-        top = 32 * p
+    group8 = (lane8 // 64) * 64
+    lane = lax.broadcasted_iota(jnp.int32, (64, 128), 1)
+    for p in range(4):
+        top = 64 * p
         aligned = (top // 128) * 128
-        packed = jnp.zeros((32, 128), F32)
-        for n in range(4):
-            block = work[n, top : top + 32, aligned : aligned + 128]
-            turn = (32 * n - (top - aligned)) % 128
-            if turn:
-                block = pltpu.roll(block, turn, 1)
-            packed = jnp.where(lane // 32 == n, block, packed)
-        left = [packed[8 * g : 8 * g + 8] for g in range(4)]
-        inverse = [jnp.where(lane8 - group8 == row8 + 8 * g, 1.0, 0.0) for g in range(4)]
-        for j in range(0, 32, 4):
+        packed = []
+        for n in range(2):
+            block = work[n, top : top + 64, aligned : aligned + 128]
+            packed.append(pltpu.roll(block, 64, 1) if (64 * n - top) % 128 else block)
+        packed = jnp.where(lane < 64, packed[0], packed[1])
+        left = [packed[8 * g : 8 * g + 8] for g in range(8)]
+        inverse = [jnp.where(lane8 - group8 == row8 + 8 * g, 1.0, 0.0) for g in range(8)]
+        for j in range(0, 64, 4):
             own, inner = j // 8, j % 8
             spread = {
                 g: [
                     jnp.take_along_axis(left[g], group8 + (j + t), axis=1, mode="promise_in_bounds")
                     for t in range(4)
                 ]
-                for g in range(own, 4)
+                for g in range(own, 8)
             }
 
             def line(tile, t, inner=inner):
@@ -656,7 +699,7 @@
             solve = pivots(lambda t, u: line(spread[own][u], t))
             left_rows = solve([line(left[own], t) for t in range(4)])
             inverse_rows = solve([line(inverse[own], t) for t in range(4)])
-            for g in range(own, 4):
+            for g in range(own, 8):
                 if g == own and inner == 4:
                     continue
                 factors = solve(spread[g])
@@ -667,41 +710,51 @@
             for t in range(4):
                 inverse[own] = jnp.where(row8 == inner + t, inverse_rows[t], inverse[own])
         packed = jnp.concatenate(inverse, axis=0)
-        diagonal = jnp.concatenate([jnp.where(lane // 32 == n, packed, 0.0) for n in range(4)], axis=0)
-        stacked = jnp.concatenate([work[n, top : top + 32, :] for n in range(4)], axis=0)
+        diagonal = jnp.concatenate([jnp.where(lane < 64, packed, 0.0), jnp.where(lane < 64, 0.0, packed)], axis=0)
+        stacked = jnp.concatenate([work[n, top : top + 64, :] for n in range(2)], axis=0)
         srow = lax.broadcasted_iota(jnp.int32, (128, RANK), 0)
         scol = lax.broadcasted_iota(jnp.int32, (128, RANK), 1)
-        identity = jnp.where(srow % 32 == scol % 32, 1.0, 0.0)
-        stacked = jnp.where(scol // 32 == p, identity, stacked)
-        solved = jnp.dot(diagonal, stacked, precision=HIGHEST, preferred_element_type=F32)
-        done = jnp.where(scol < top + 32, solved, 0.0)
-        for n in range(4):
-            work[n, top : top + 32, :] = done[32 * n : 32 * n + 32]
-        rest = RANK - top - 32
+        identity = jnp.where(srow % 64 == scol % 64, 1.0, 0.0)
+        stacked = jnp.where(scol // 64 == p, identity, stacked)
+        solved = jnp.dot(diagonal, stacked, precision=HIGH, preferred_element_type=F32)
+        done = jnp.where(scol < top + 64, solved, 0.0)
+        for n in range(2):
+            work[n, top : top + 64, :] = done[64 * n : 64 * n + 64]
+        rest = RANK - top - 64
         if rest:
-            turned = solved.T[top + 32 :, :]
+            turned = solved.T[top + 64 :, :]
             tlane = lax.broadcasted_iota(jnp.int32, (rest, 128), 1)
             tcol = lax.broadcasted_iota(jnp.int32, (rest, RANK), 1)
-            for n in range(4):
+            for n in range(2):
                 update = jnp.dot(
-                    jnp.where(tlane // 32 == n, turned, 0.0), solved,
-                    precision=HIGHEST, preferred_element_type=F32,
+                    jnp.where(tlane // 64 == n, turned, 0.0), solved,
+                    precision=HIGH, preferred_element_type=F32,
                 )
-                work[n, top + 32 :, :] = jnp.where(tcol // 32 == p, 0.0, work[n, top + 32 :, :]) - update
-
+                work[n, top + 64 :, :] = jnp.where(tcol // 64 == p, 0.0, work[n, top + 64 :, :]) - update
+
+    size = jnp.where(node % 2 == 0, sizes[0], sizes[1])
+    factor_out[...] = work[node % 2] * size
+    factor_copy = send(factor_out, factor_in, factor_sems.at[0], factor_sems.at[1], other)
     last = (((1,), (1,)), ((), ()))
-    size = sum(jnp.where(node == n, sizes[n], 0.0) for n in range(4))
-    basis[...] = (128.0 * size) * lax.dot_general(
-        samples[...], work[node], last, precision=HIGH, preferred_element_type=F32
-    )
-    for k in range(2):
-        half = jnp.dot(work[2 * k], middles[k], precision=HIGH, preferred_element_type=F32)
-        coupling[k] = ((16384.0 / math.sqrt(RANK)) * sizes[2 * k] * sizes[2 * k + 1]) * lax.dot_general(
-            half, work[2 * k + 1], last, precision=HIGH, preferred_element_type=F32
-        )
+    half = jnp.dot(work[0], middle, precision=HIGH, preferred_element_type=F32)
+    coupling[core] = ((16384.0 / math.sqrt(RANK)) * sizes[0] * sizes[1]) * lax.dot_general(
+        half, work[1], last, precision=HIGH, preferred_element_type=F32
+    )
+    coupling_copy = send(
+        coupling.at[core], coupling.at[core], coupling_sems.at[0], coupling_sems.at[1], other
+    )
+    factor_copy.wait_recv()
+    factor = jnp.where(node // 2 == core, factor_out[...], factor_in[...])
+    basis[...] = 128.0 * lax.dot_general(
+        samples[...], factor, last, precision=HIGH, preferred_element_type=F32
+    )
+    factor_copy.wait_send()
+    coupling_copy.wait()
 
 
 def finish(full_a, full_b, samples):
+    matrix = pltpu.VMEM((RANK, RANK), F32)
+    dma = pltpu.SemaphoreType.DMA
     return pl.pallas_call(
         finish_kernel,
         out_shape=(
@@ -710,8 +763,17 @@
         ),
         in_specs=[VMEM] * 3,
         out_specs=(VMEM,) * 2,
-        scratch_shapes=[pltpu.VMEM((4, RANK, RANK), F32), pltpu.VMEM((4, RANK, RANK), F32)],
-        compiler_params=pltpu.CompilerParams(vmem_limit_bytes=32 << 20),
+        scratch_shapes=[
+            pltpu.VMEM((2, RANK, RANK), F32),
+            pltpu.VMEM((2, RANK, RANK), F32),
+            matrix,
+            matrix,
+            dma((2,)),
+            dma((2,)),
+        ],
+        compiler_params=pltpu.CompilerParams(
+            collective_id=2, has_side_effects=True, vmem_limit_bytes=32 << 20
+        ),
         name="finish",
     )(full_a, full_b, samples)
 

time: 112 us -> 104 us (0.929)
  Pallas kernels: 108 us -> 98 us
  local copies, waits for them, and re-layouts: 3.51 us -> 5.01 us
    pallas_call x1, Pallas kernels: 51 us -> 43.8 us  [collect(): pl.pallas_call(collect_kernel, out_shape=(jax.ShapeDtypeStruct((ROWS, RAN...]
    pallas_call x1, Pallas kernels: 16.1 us -> 14.2 us  [finish(): pl.pallas_call(finish_kernel, out_shape=(jax.ShapeDtypeStruct((ROWS, RANK...]
    pallas_call x1, Pallas kernels: 28.6 us -> 26.7 us  [gather(): pl.pallas_call(gather_kernel, out_shape=(jax.ShapeDtypeStruct((32, SPAN,...]
    unnamed x12 -> x14, local copies, waits for them, and re-layouts: 3.51 us -> 5.01 us
    pallas_call x1, Pallas kernels: 11.8 us -> 13.2 us  [sample(): pl.pallas_call(sample_kernel, out_shape=jax.ShapeDtypeStruct((2, 2, 4, RO...]
where the time goes in v4:
time: 104 us
  Pallas kernels  98 us (94%)
  local copies, waits for them, and re-layouts  5.01 us (5%)
    pallas_call x1, Pallas kernels, collect(): pl.pallas_call(collect_kernel, out_shape=(jax.ShapeDtypeStruct((ROWS, RAN...  43.8 us
    pallas_call x1, Pallas kernels, gather(): pl.pallas_call(gather_kernel, out_shape=(jax.ShapeDtypeStruct((32, SPAN,...  26.7 us
    pallas_call x1, Pallas kernels, finish(): pl.pallas_call(finish_kernel, out_shape=(jax.ShapeDtypeStruct((ROWS, RANK...  14.2 us
    pallas_call x1, Pallas kernels, sample(): pl.pallas_call(sample_kernel, out_shape=jax.ShapeDtypeStruct((2, 2, 4, RO...  13.2 us
    unnamed x14, local copies, waits for them, and re-layouts  5.01 us

profile of v4, /device:TPU:1, one launch (start us, length us, event | category | flops | bytes accessed | tf_op | source)
XLA Modules:
  0.0 103.7 jit_solution(11332842084721736020)
XLA Ops:
  0.6 0.0 copy-start
  0.6 0.8 copy-done
  1.5 0.0 copy-start.2
  1.5 0.7 copy-done.2
  2.2 0.0 copy-start.3
  2.2 0.7 copy-done.3
  2.8 0.0 copy-start.4
  2.8 0.7 copy-done.4
  3.5 0.0 copy-start.5
  3.5 0.7 copy-done.5
  4.2 0.0 copy-start.1
  4.2 26.7 %gather.1 = (bf16[32,288,128]{2,1,0:T(8,128)(2,1)S(1)}, bf16[2,8,16,256]{3,2,1,0:T(8,128)(2,1)S(1)}, s32[8,128]{1,0:T(8,128)S(1)}, f32[8,256]{1,0:T(8,128)S(1)}) custom-call(bf16[8,256]{1,0:T(8,128)(2,1)S(1)} %copy-done.2, bf16[128,256]{1,0:T(8,128)(2,1)S(1)} %copy-done, s32[1,256]{1,0:T(1,128)S(1)} %bitcast.1, s32[1,16]{1,0:T(1,128)S(1)} %copy-done.4, ...), custom_call_target="tpu_custom_call" | custom-call | tf_op jit(solution)/shard_map/gather/pallas_call | solution.py:244
  30.9 13.2 %sample.1.parts = f32[2,2,4,256,256]{4,3,2,1,0:T(8,128)S(1)} custom-call(bf16[32,288,128]{2,1,0:T(8,128)(2,1)S(1)} %get-tuple-element.9.blocks, bf16[2,8,16,256]{3,2,1,0:T(8,128)(2,1)S(1)} %get-tuple-element.10.row_points, s32[8,128]{1,0:T(8,128)S(1)} %get-tuple-element.11.picks), custom_call_target="tpu_custom_call" | custom-call | tf_op jit(solution)/shard_map/sample/pallas_call | solution.py:339
  44.2 0.0 copy-done.1
  44.2 43.8 %collect.1 = (f32[256,256]{1,0:T(8,128)S(1)}, f32[4,4,4,2,8,128]{5,4,3,2,1,0:T(8,128)S(1)}, f32[4,4,4,2,8,128]{5,4,3,2,1,0:T(8,128)S(1)}) custom-call(f32[2,2,4,256,256]{4,3,2,1,0:T(8,128)S(1)} %sample.1.parts, s32[4,256]{1,0:T(4,128)S(1)} %copy-done.1, f32[8,256]{1,0:T(8,128)S(1)} %get-tuple-element.12.tree_points), custom_call_target="tpu_custom_call" | custom-call | tf_op jit(solution)/shard_map/collect/pallas_call | solution.py:579
  87.9 14.2 %finish.1 = (f32[256,256]{1,0:T(8,128)S(1)}, f32[2,256,256]{2,1,0:T(8,128)S(1)}) custom-call(f32[4,4,4,2,8,128]{5,4,3,2,1,0:T(8,128)S(1)} %get-tuple-element.13.full_a, f32[4,4,4,2,8,128]{5,4,3,2,1,0:T(8,128)S(1)} %get-tuple-element.14.full_b, f32[256,256]{1,0:T(8,128)S(1)} %get-tuple-element.15.samples), custom_call_target="tpu_custom_call" | custom-call | tf_op jit(solution)/shard_map/finish/pallas_call | solution.py:758
  102.2 0.7 copy.10
  102.9 0.8 copy.11
Async XLA Ops:
  0.6 0.8 copy-start
  1.5 0.7 copy-start.2
  2.2 0.7 copy-start.3
  2.8 0.7 copy-start.4
  3.5 0.7 copy-start.5
  4.2 40.0 %copy-start.1 = (s32[4,256]{1,0:T(4,128)S(1)}, s32[4,256]{1,0:T(4,128)}, u32[]{:S(2)}) copy-start(s32[4,256]{1,0:T(4,128)} %skeleton.1) | copy-start | bytes 12292

commit v5 on v4

v5 whole, which is shorter than its diff:
```python
import math

import jax
import jax.numpy as jnp
from jax import lax
from jax.experimental import pallas as pl
from jax.experimental.pallas import tpu as pltpu
from jax.sharding import PartitionSpec as P

MESH = pl.DeviceIdType.MESH
HIGH = lax.Precision.HIGH
HIGHEST = lax.Precision.HIGHEST
F32 = jnp.float32
BF16 = jnp.bfloat16
VMEM = pl.BlockSpec(memory_space=pltpu.VMEM)
HBM = pl.BlockSpec(memory_space=pltpu.HBM)

ROWS = 256
FEATS = 8
SAMPLES = 128
RANK = 256
SPAN = 288
LINK = BF16
VMEM_LIMIT = 60 << 20


def place():
    leaf = lax.axis_index("leaf")
    core = lax.axis_index("sub")
    return leaf % 4, (leaf // 4) % 4, leaf // 16, core


def device(x, y, z, core):
    return (z * 16 + y * 4 + x, core)


def send(src, dst, send_sem, recv_sem, target):
    copy = pltpu.make_async_remote_copy(
        src_ref=src,
        dst_ref=dst,
        send_sem=send_sem,
        recv_sem=recv_sem,
        device_id=target,
        device_id_type=MESH,
    )
    copy.start()
    return copy


def features(coordinates, scale, ones_first):
    norm = -2.0 * jnp.sum(coordinates * coordinates, axis=0, keepdims=True)
    first = norm.astype(BF16).astype(F32)
    second = (norm - first).astype(BF16).astype(F32)
    third = norm - first - second
    row = lax.broadcasted_iota(jnp.int32, coordinates.shape, 0)
    start = 3 if ones_first else 0
    other = 0 if ones_first else 3
    tail = jnp.where((row >= other) & (row < other + 3), 1.0, 0.0)
    tail = jnp.where(row == start, first, tail)
    tail = jnp.where(row == start + 1, second, tail)
    tail = jnp.where(row == start + 2, third, tail)
    return jnp.concatenate([scale * coordinates, tail], axis=0)


def fold(factors, lines):
    a, b, c, d = (factor * values for factor, values in zip(factors, lines, strict=True))
    return (a + b) + (c + d)


def pivots(entry):
    def pair(a, b, c):
        scale = lax.rsqrt(a)
        return scale, b * scale, a * lax.rsqrt(a * (a * c - b * b))

    r0, l10, r1 = pair(entry(0, 0), entry(1, 0), entry(1, 1))
    l20, l30 = entry(2, 0) * r0, entry(3, 0) * r0
    l21, l31 = (entry(2, 1) - l20 * l10) * r1, (entry(3, 1) - l30 * l10) * r1
    r2, l32, r3 = pair(
        entry(2, 2) - (l20 * l20 + l21 * l21),
        entry(3, 2) - (l30 * l20 + l31 * l21),
        entry(3, 3) - (l30 * l30 + l31 * l31),
    )

    def solve(values):
        v0 = values[0] * r0
        v1 = (values[1] - v0 * l10) * r1
        v2 = (values[2] - (v0 * l20 + v1 * l21)) * r2
        v3 = ((values[3] - (v0 * l30 + v1 * l31)) - v2 * l32) * r3
        return [v0, v1, v2, v3]

    return solve


MATE = 0
USE = [
    (MATE, 0), (6, 0), (2, 0), (5, 0), (MATE, 1), (MATE, 3), (6, 1), (6, 3),
    (3, 0), (3, 1), (MATE, 2), (6, 2), (3, 3), (3, 2), (2, 1), (2, 3),
    (5, 1), (5, 3), (2, 2), (5, 2), (4, 0), (4, 1), (4, 3), (4, 2),
]
SLOT = {block: slot for slot, block in enumerate(USE)}
KIND = {MATE: 1, 6: 1, 3: 1, 2: 0, 5: 0, 4: 0}


def make_masks(lists, near_mask, far_mask, x, y, z):
    lane = lax.broadcasted_iota(jnp.int32, (8, 128), 1)
    group = lax.broadcasted_iota(jnp.int32, (8, 128), 0) // 4
    named = jnp.full((8, 128), -1, jnp.int32)
    near = jnp.zeros((8, 128), F32)
    for slot, (dz, along) in enumerate(USE):
        plane = (z + (dz or 7 - 6 * (z % 2))) % 8
        if KIND[dz]:
            block = plane * 16 + y * 4 + (x + along) % 4
        else:
            block = plane * 16 + ((y + along) % 4) * 4 + x
        named = jnp.where((lane == slot) & (group == KIND[dz]), block, named)
        near = jnp.where(lane == slot, jnp.where(plane // 4 == z // 4, 1.0, 0.0), near)
    named = named.astype(F32)
    hit = jnp.zeros((8, 128), F32)
    for side, length in ((0, 16), (1, 32)):
        entries = jnp.concatenate(
            [lists[k, at, side : side + 1, :] for k in range(2) for at in range(4)], axis=0
        ).astype(F32)
        for e in range(length):
            hit = jnp.where(named == jnp.broadcast_to(entries[:, e : e + 1], (8, 128)), 1.0, hit)
    near_hit, far_hit = (hit * near).T, (hit * (1.0 - near)).T
    for r in range(8):
        near_mask[r] = jnp.broadcast_to(near_hit[0:32, r : r + 1], (32, 128))
        far_mask[r] = jnp.broadcast_to(far_hit[0:32, r : r + 1], (32, 128))


def whole_kernel(
    points_in, omega_in, order_in, siblings_in, cousins_in, skeleton_in,
    basis, coupling,
    points, omega, tree_order, siblings, cousins, skeleton, load_sems,
    blocks, row_points, lists, own, own_rows, own_lists, near_mask, far_mask, rows, even_tile, odd_tile, parts,
    hop_send, hop_recv, out_send, out_recv, far_send, far_recv, rows_send, rows_recv, list_send, list_recv,
    other_core, relay_out, relay_in, near_out, near_in, table, other_table, piece, pieces, full_a, full_b,
    core_send, core_recv, relay_sems, near_sems, table_sems, piece_send, piece_recv,
    z_send, z_recv, y_sems, x_sems,
    work, chosen, factor_out, factor_in, factor_sems, coupling_sems,
):
    loads = [
        pltpu.make_async_copy(source, target, load_sems.at[k])
        for k, (source, target) in enumerate(
            [
                (omega_in, omega),
                (points_in, points),
                (order_in, tree_order),
                (siblings_in, siblings),
                (cousins_in, cousins),
                (skeleton_in, skeleton),
            ]
        )
    ]
    for copy in loads:
        copy.start()
    x, y, z, core = place()
    leaf = z * 16 + y * 4 + x
    node, pair = z // 2, z // 4
    other = device(x, y, z, 1 - core)
    right, left_side = device((x + 1) % 4, y, z, core), device((x + 3) % 4, y, z, core)
    above, below = device(x, (y + 1) % 4, z, core), device(x, (y + 3) % 4, z, core)
    upward, downward = device(x, y, (z + 1) % 8, core), device(x, y, (z + 7) % 8, core)
    mates = []
    for dz in range(2):
        for dy in range(4):
            for dx in range(4):
                if dz or dy or dx:
                    where = ((x + dx) % 4, (y + dy) % 4, node * 2 + (z + dz) % 2)
                    mates.append((dz * 16 + dy * 4 + dx, where, device(*where, core)))
    column = [device(x, y, (z + dz) % 8, pair) for dz in range(8)]
    along_x = [device((x + d) % 4, y, z, core) for d in range(4)]
    along_y = [device(x, (y + d) % 4, z, core) for d in range(4)]
    partners = [who for _, _, who in mates] + [other]
    partners += [
        device(x, y, ((node + dn) % 4) * 2 + dz, c) for dn in range(1, 4) for dz in range(2) for c in range(2)
    ]
    partners.append(device(x, y, node * 2 + (z + 1) % 2, 1 - core))
    barrier = pltpu.get_barrier_semaphore()
    for partner in partners:
        pl.semaphore_signal(barrier, inc=1, device_id=partner, device_id_type=MESH)

    loads[0].wait()
    own[0:ROWS, :] = omega[...].astype(F32).T.astype(BF16)
    loads[1].wait()
    columns = features(points[...].astype(F32), 1.0, False).astype(BF16)
    own[256:272, :] = columns[:, :128]
    own[272:288, :] = columns[:, 128:]
    halves = (pl.ds(0, SPAN // 2), pl.ds(SPAN // 2, SPAN // 2))
    pl.semaphore_wait(barrier, len(partners))

    from_below, from_above = 24 * (z % 2), 24 * ((z + 1) % 2)
    hops = {}

    def hop(ref, slot, key, half, who):
        hops[key, half] = send(
            ref.at[halves[half]], blocks.at[slot, halves[half]],
            hop_send.at[key, half], hop_recv.at[key, half], who,
        )

    for step in range(2):
        hop(own, from_above, 7, step, upward)
        hop(own, from_below, 1, 1 - step, downward)

    for copy in loads[2:]:
        copy.wait()
    local = tree_order[...] % ROWS
    lane = lax.broadcasted_iota(jnp.int32, (ROWS, ROWS), 0)
    pick = jnp.where(lane == local, 1.0, 0.0).astype(BF16)
    mine = jnp.dot(points[...], pick, preferred_element_type=F32)
    own_rows[...] = features(mine, 4.0, True).astype(BF16)
    own_lists[...] = jnp.zeros_like(own_lists)
    own_lists[0:1, 0:16] = siblings[...]
    own_lists[1:2, 0:32] = cousins[...]
    small = []
    for kind, (at, line) in enumerate(((x, along_x), (y, along_y))):
        row_points[kind, at, core] = own_rows[...]
        lists[kind, at] = own_lists[...]
        for d in range(1, 4):
            target = row_points.at[kind, at, core]
            small.append(send(own_rows, target, rows_send.at[kind, d], rows_recv.at[kind, d], line[d]))
            target = lists.at[kind, at]
            small.append(send(own_lists, target, list_send.at[kind, d], list_recv.at[kind, d], line[d]))
    parts[...] = jnp.zeros_like(parts)

    plus, minus = (above, right), (below, left_side)
    outs, fars = {}, {}

    def fan_out(k, dz, half):
        kind = KIND[dz]
        block = blocks.at[SLOT[dz, 0], halves[half]]
        for side, (at, who) in enumerate(((SLOT[dz, 3], plus[kind]), (SLOT[dz, 1], minus[kind]))):
            outs[k, side, half] = send(
                block, blocks.at[at, halves[half]], out_send.at[k, side, half], out_recv.at[k, side, half], who
            )

    def relay(k, dz):
        kind = KIND[dz]
        for side, (at, who) in enumerate(((SLOT[dz, 3], plus[kind]), (SLOT[dz, 1], minus[kind]))):
            outs[k, side, side].wait_recv()
            fars[k, side] = send(
                blocks.at[at, halves[side]], blocks.at[SLOT[dz, 2], halves[side]],
                far_send.at[k, side], far_recv.at[k, side], who,
            )

    def landed(*ks):
        for k in ks:
            for side in range(2):
                outs[k, side, 1 - side].wait_recv()

    def passed(*ks):
        for k in ks:
            for side in range(2):
                fars[k, side].wait_recv()

    for step in range(2):
        hops[7, step].wait_recv()
        hop(blocks.at[from_below], SLOT[6, 0], 6, step, upward)
        hops[1, 1 - step].wait_recv()
        hop(blocks.at[from_above], SLOT[2, 0], 2, 1 - step, downward)
    for half in range(2):
        fan_out(0, MATE, half)
    for copy in small:
        copy.wait_recv()
    swap_rows = send(row_points.at[:, :, core], row_points.at[:, :, core], rows_send.at[0, 0], rows_recv.at[0, 0], other)
    make_masks(lists, near_mask, far_mask, x, y, z)
    for step in range(2):
        hops[6, step].wait_recv()
        hop(blocks.at[SLOT[6, 0]], SLOT[5, 0], 5, step, upward)
        fan_out(1, 6, step)
        hops[2, 1 - step].wait_recv()
        hop(blocks.at[SLOT[2, 0]], SLOT[3, 0], 3, 1 - step, downward)
        fan_out(2, 2, 1 - step)
    swap_rows.wait()
    for r in range(8):
        for half in range(2):
            rows[r, half * ROWS : (half + 1) * ROWS, :] = row_points[r // 4, r % 4, half].astype(F32).T.astype(BF16)

    def kernel_tile(r, use, tile):
        columns = jnp.concatenate(
            [blocks[2 * use + k, at : at + 16, :] for k in range(2) for at in (256, 272)], axis=1
        )
        exponent = jnp.dot(rows[r], columns, preferred_element_type=F32)
        tile[...] = jnp.exp(exponent).astype(BF16)

    def add(kind, at, use, tile):
        r = kind * 4 + at
        weights = []
        for k in range(2):
            slot = 2 * use + k
            values = blocks[slot, 0:ROWS, :]
            near = near_mask[r, pl.ds(slot, 1), :].astype(BF16)
            far = far_mask[r, pl.ds(slot, 1), :].astype(BF16)
            weights.append(jnp.concatenate([values * near, values * far], axis=1))
        terms = jnp.dot(tile[...], jnp.concatenate(weights, axis=0), preferred_element_type=F32)
        parts[0, kind, at] += terms[0:ROWS]
        parts[1, kind, at] += terms[ROWS:]

    def batch(kind, count, item):
        at, use = item(0)
        kernel_tile(kind * 4 + at, use, even_tile)

        def two_steps(step, carry):
            at0, use0 = item(2 * step)
            at1, use1 = item(2 * step + 1)
            at2, use2 = item((2 * step + 2) % count)
            kernel_tile(kind * 4 + at1, use1, odd_tile)
            add(kind, at0, use0, even_tile)
            kernel_tile(kind * 4 + at2, use2, even_tile)
            add(kind, at1, use1, odd_tile)
            return carry

        lax.fori_loop(0, count // 2, two_steps, 0)

    batch(1, 4, lambda i: (i, 0))
    relay(0, MATE)
    hops[5, 0].wait_recv()
    hop(blocks.at[SLOT[5, 0]], SLOT[4, 0], 4, 0, upward)
    fan_out(3, 5, 0)
    hops[3, 1].wait_recv()
    hop(blocks.at[SLOT[3, 0]], SLOT[4, 0], 4, 1, downward)
    fan_out(4, 3, 1)
    hops[5, 1].wait_recv()
    fan_out(3, 5, 1)
    hops[3, 0].wait_recv()
    fan_out(4, 3, 0)
    batch(0, 4, lambda i: (i, 1))
    relay(1, 6)
    relay(2, 2)
    for half in range(2):
        hops[4, half].wait_recv()
        fan_out(5, 4, half)
    landed(0, 1)
    batch(1, 8, lambda i: (i % 4, 2 + i // 4))
    relay(3, 5)
    relay(4, 3)
    relay(5, 4)
    landed(4)
    passed(0, 1)
    batch(1, 8, lambda i: (i % 4, 4 + i // 4))
    passed(4)
    batch(1, 4, lambda i: (i, 6))

    ahead, behind, across = (x + 1) % 4, (x + 3) % 4, (x + 2) % 4
    next_y, last_y = (y + 1) % 4, (y + 3) % 4
    order = [(across, (y + 2) % 4), (ahead, next_y), (behind, last_y), (x, y)]
    swap = {}

    def give(step, kind):
        at = order[step][kind]
        swap[step, kind] = send(
            parts.at[1 - core, kind, at], other_core.at[kind, at],
            core_send.at[kind, step], core_recv.at[kind, step], other,
        )


    def partial(step, kind):
        swap[step, kind].wait_recv()
        at = order[step][kind]
        return parts[core, kind, at] + other_core[kind, at]

    forward, backward = (right, above), (left_side, below)
    lower, upper = pl.ds(0, 128), pl.ds(128, 128)
    relays, nears = {}, []

    def pass_on(kind, side, first, rows_of, who):
        ref = near_out.at[kind, side, rows_of]
        landing = near_in.at[kind, side, rows_of]
        nears.append(send(ref, landing, near_sems.at[0, kind, side, first], near_sems.at[1, kind, side, first], who))

    def start_sum(kind):
        relay_out[kind] = partial(0, kind).astype(LINK)
        for side, (rows_of, who) in enumerate(((lower, forward[kind]), (upper, backward[kind]))):
            relays[kind, side] = send(
                relay_out.at[kind, rows_of], relay_in.at[kind, side],
                relay_sems.at[0, kind, side], relay_sems.at[1, kind, side], who,
            )

    def middle_sum(kind):
        near_out[kind, 0] = partial(1, kind).astype(LINK)
        pass_on(kind, 0, 0, upper, forward[kind])
        near_out[kind, 1] = partial(2, kind).astype(LINK)
        pass_on(kind, 1, 0, lower, backward[kind])

    def end_sum(kind):
        relays[kind, 0].wait_recv()
        near_out[kind, 0, 0:128, :] = (
            parts[core, kind, order[1][kind], 0:128, :]
            + other_core[kind, order[1][kind], 0:128, :]
            + relay_in[kind, 0].astype(F32)
        ).astype(LINK)
        pass_on(kind, 0, 1, lower, forward[kind])
        relays[kind, 1].wait_recv()
        near_out[kind, 1, 128:256, :] = (
            parts[core, kind, order[2][kind], 128:256, :]
            + other_core[kind, order[2][kind], 128:256, :]
            + relay_in[kind, 1].astype(F32)
        ).astype(LINK)
        pass_on(kind, 1, 1, upper, backward[kind])

    for step in range(4):
        give(step, 1)
    landed(2, 3, 5)
    passed(2, 3, 5)
    batch(0, 10, lambda i: ((x + 2 + 3 * (i // 5)) % 4, 7 + i % 5))
    give(0, 0)
    give(1, 0)
    start_sum(1)
    middle_sum(1)
    batch(0, 10, lambda i: ((x + 3 + i // 5) % 4, 7 + i % 5))
    give(2, 0)
    give(3, 0)
    start_sum(0)
    end_sum(1)
    middle_sum(0)
    end_sum(0)
    total = partial(3, 1) + partial(3, 0)
    first_row = (leaf * 2 + core) * ROWS
    row = lax.broadcasted_iota(jnp.int32, (ROWS, RANK), 0) + first_row
    picked = jnp.where(row == skeleton[pl.ds(node, 1), :], 1.0, 0.0)
    own_skeleton = jnp.dot(
        mine.astype(BF16), picked.astype(BF16), preferred_element_type=F32
    )
    for copy in nears:
        copy.wait_recv()
    for kind in range(2):
        for side in range(2):
            total = total + near_in[kind, side].astype(F32)
    rows_here = total

    table[0:256, :] = lax.dot_general(
        rows_here, rows_here, (((0,), (0,)), ((), ())), precision=HIGHEST, preferred_element_type=F32
    )
    table[128:256, 0:128] = jnp.zeros((128, 128), F32)
    table[128:136, 0:128] = own_skeleton[:, 0:128]
    table[136:144, 0:128] = own_skeleton[:, 128:256]
    table[256:512, :] = lax.dot_general(
        picked, rows_here, (((0,), (0,)), ((), ())), precision=HIGHEST, preferred_element_type=F32
    )
    start = pl.multiple_of((1 - core) * 256, 256)
    swap_table = send(
        table.at[pl.ds(start, 256)], other_table, table_sems.at[0], table_sems.at[1], other
    )
    swap_table.wait()
    keep = pl.multiple_of(core * 256, 256)
    other_table[...] += table[pl.ds(keep, 256), :]

    def chunk(where):
        first = (where[0] * 8 + where[1] * 2 + where[2] % 2) * 8
        return other_table.at[pl.ds(pl.multiple_of(first, 8), 8)]

    spreads = []
    for slot, where, who in mates:
        spreads.append(
            send(chunk(where), pieces.at[slot], piece_send.at[slot], piece_recv.at[slot], who)
        )
    sums = chunk((x, y, z))[...]
    for copy in spreads:
        copy.wait_recv()
    for slot, _, _ in mates:
        sums = sums + pieces[slot]
    piece[0] = sums[:, 0:128]
    piece[1] = sums[:, 128:256]
    for copy in spreads:
        copy.wait_send()

    home_a, home_b = full_a.at[x, y, z % 4, core], full_b.at[y, x, z % 4, core]

    def drop(dz, half):
        return pltpu.make_async_remote_copy(
            src_ref=piece.at[half],
            dst_ref=(home_a, home_b)[half],
            send_sem=z_send.at[dz, half],
            recv_sem=z_recv.at[z % 4, core, half],
            device_id=column[dz],
            device_id_type=MESH,
        )

    def arrival(plane, c, half):
        landing = (full_a.at[x, y, plane, c], full_b.at[y, x, plane, c])[half]
        return pltpu.make_async_remote_copy(
            src_ref=piece.at[half],
            dst_ref=landing,
            send_sem=z_send.at[0, half],
            recv_sem=z_recv.at[plane, c, half],
            device_id=other,
            device_id_type=MESH,
        )

    for dz in (4, 3, 5, 2, 6, 1, 7):
        for half in range(2):
            drop(dz, half).start()

    @pl.when(pair == core)
    def _():
        home_a[...] = piece[0]
        home_b[...] = piece[1]

    @pl.when(pair != core)
    def _():
        for half in range(2):
            drop(0, half).start()

    for plane in range(4):
        for c in range(2):

            @pl.when((core * 4 + plane != z) | (core != c))
            def _(plane=plane, c=c):
                for half in range(2):
                    arrival(plane, c, half).wait_recv()

    cuts = (pl.ds(0, 2), pl.ds(2, 2))

    def push(ref, sems, k, who):
        return send(ref, ref, sems.at[2 * k], sems.at[2 * k + 1], who)

    def ring(at, sems, first_k, forward, backward):
        return [
            push(at.at[cuts[0]], sems, first_k, forward),
            push(at.at[cuts[1]], sems, first_k + 1, backward),
            push(at.at[cuts[1]], sems, first_k + 2, forward),
            push(at.at[cuts[0]], sems, first_k + 3, backward),
        ]

    def pass_along(copies, sems, first_k, before, after, forward, backward):
        copies[0].wait_recv()
        copies.append(push(before.at[cuts[0]], sems, first_k + 4, forward))
        copies[1].wait_recv()
        copies.append(push(after.at[cuts[1]], sems, first_k + 5, backward))

    first = ring(full_a.at[x, y], y_sems, 0, above, below)
    second = ring(full_b.at[y, x], x_sems, 0, right, left_side)
    pass_along(first, y_sems, 0, full_a.at[x, last_y], full_a.at[x, next_y], above, below)
    pass_along(second, x_sems, 0, full_b.at[y, behind], full_b.at[y, ahead], right, left_side)
    for copy in first[2:6]:
        copy.wait_recv()
    third = ring(full_a.at[x], x_sems, 6, right, left_side)
    for copy in second[2:6]:
        copy.wait_recv()
    fourth = ring(full_b.at[y], y_sems, 6, above, below)
    pass_along(third, x_sems, 6, full_a.at[behind], full_a.at[ahead], right, left_side)
    pass_along(fourth, y_sems, 6, full_b.at[last_y], full_b.at[next_y], above, below)
    for copy in third[2:] + fourth[2:]:
        copy.wait_recv()
    for copy in first + second + third + fourth:
        copy.wait_send()
    for dz in range(1, 8):
        for half in range(2):
            drop(dz, half).wait_send()

    @pl.when(pair != core)
    def _():
        for half in range(2):
            drop(0, half).wait_send()

    row = lax.broadcasted_iota(jnp.int32, (RANK, RANK), 0)
    col = lax.broadcasted_iota(jnp.int32, (RANK, RANK), 1)
    skeleton_points, sizes = [], []
    for n in range(2):
        for at_x in range(4):
            for at_y in range(4):
                span = pl.ds(at_x * 64 + at_y * 16, 16)
                planes = pl.ds(2 * n, 2)
                for kind, target in enumerate((work, chosen)):
                    target[n, span, 0:128] = full_a[at_x, at_y, planes, kind].reshape(16, 128)
                    target[n, span, 128:256] = full_b[at_y, at_x, planes, kind].reshape(16, 128)
        skeleton_points.append(
            jnp.concatenate([work[n, 128:136, 0:128], work[n, 136:144, 0:128]], axis=1)
        )
        gram = work[n]
        on_diagonal = jnp.where(row == col, gram, 0.0)
        trace = jnp.sum(jnp.sum(on_diagonal, axis=0, keepdims=True), axis=1, keepdims=True)
        work[n] = gram * (1.0 / trace) + jnp.where(row == col, 0.01, 0.0)
        sizes.append(lax.rsqrt(trace))

    row_side = features(skeleton_points[0], 4.0, True).T.astype(BF16)
    col_side = features(skeleton_points[1], 1.0, False).astype(BF16)
    kernel_skel = jnp.exp(jnp.dot(row_side, col_side, preferred_element_type=F32))
    right = jnp.dot(kernel_skel, chosen[1], precision=HIGH, preferred_element_type=F32)
    middle = lax.dot_general(
        chosen[0], right, (((0,), (0,)), ((), ())), precision=HIGH, preferred_element_type=F32
    )

    lane8 = lax.broadcasted_iota(jnp.int32, (8, 128), 1)
    row8 = lax.broadcasted_iota(jnp.int32, (8, 128), 0)
    group8 = (lane8 // 64) * 64
    lane = lax.broadcasted_iota(jnp.int32, (64, 128), 1)
    for p in range(4):
        top = 64 * p
        aligned = (top // 128) * 128
        packed = []
        for n in range(2):
            block = work[n, top : top + 64, aligned : aligned + 128]
            packed.append(pltpu.roll(block, 64, 1) if (64 * n - top) % 128 else block)
        packed = jnp.where(lane < 64, packed[0], packed[1])
        left = [packed[8 * g : 8 * g + 8] for g in range(8)]
        inverse = [jnp.where(lane8 - group8 == row8 + 8 * g, 1.0, 0.0) for g in range(8)]
        for j in range(0, 64, 4):
            own, inner = j // 8, j % 8
            spread = {
                g: [
                    jnp.take_along_axis(left[g], group8 + (j + t), axis=1, mode="promise_in_bounds")
                    for t in range(4)
                ]
                for g in range(own, 8)
            }

            def line(tile, t, inner=inner):
                return jnp.broadcast_to(tile[inner + t : inner + t + 1, :], (8, 128))

            solve = pivots(lambda t, u: line(spread[own][u], t))
            left_rows = solve([line(left[own], t) for t in range(4)])
            inverse_rows = solve([line(inverse[own], t) for t in range(4)])
            for g in range(own, 8):
                if g == own and inner == 4:
                    continue
                factors = solve(spread[g])
                if g == own:
                    factors = [jnp.where(row8 > 3, factor, 0.0) for factor in factors]
                left[g] = left[g] - fold(factors, left_rows)
                inverse[g] = inverse[g] - fold(factors, inverse_rows)
            for t in range(4):
                inverse[own] = jnp.where(row8 == inner + t, inverse_rows[t], inverse[own])
        packed = jnp.concatenate(inverse, axis=0)
        diagonal = jnp.concatenate([jnp.where(lane < 64, packed, 0.0), jnp.where(lane < 64, 0.0, packed)], axis=0)
        stacked = jnp.concatenate([work[n, top : top + 64, :] for n in range(2)], axis=0)
        srow = lax.broadcasted_iota(jnp.int32, (128, RANK), 0)
        scol = lax.broadcasted_iota(jnp.int32, (128, RANK), 1)
        identity = jnp.where(srow % 64 == scol % 64, 1.0, 0.0)
        stacked = jnp.where(scol // 64 == p, identity, stacked)
        solved = jnp.dot(diagonal, stacked, precision=HIGH, preferred_element_type=F32)
        done = jnp.where(scol < top + 64, solved, 0.0)
        for n in range(2):
            work[n, top : top + 64, :] = done[64 * n : 64 * n + 64]
        rest = RANK - top - 64
        if rest:
            turned = solved.T[top + 64 :, :]
            tlane = lax.broadcasted_iota(jnp.int32, (rest, 128), 1)
            tcol = lax.broadcasted_iota(jnp.int32, (rest, RANK), 1)
            for n in range(2):
                update = jnp.dot(
                    jnp.where(tlane // 64 == n, turned, 0.0), solved,
                    precision=HIGH, preferred_element_type=F32,
                )
                work[n, top + 64 :, :] = jnp.where(tcol // 64 == p, 0.0, work[n, top + 64 :, :]) - update

    size = jnp.where(node % 2 == 0, sizes[0], sizes[1])
    factor_out[...] = work[node % 2] * size
    factor_copy = send(factor_out, factor_in, factor_sems.at[0], factor_sems.at[1], other)
    last = (((1,), (1,)), ((), ()))
    half = jnp.dot(work[0], middle, precision=HIGH, preferred_element_type=F32)
    coupling[core] = ((16384.0 / math.sqrt(RANK)) * sizes[0] * sizes[1]) * lax.dot_general(
        half, work[1], last, precision=HIGH, preferred_element_type=F32
    )
    coupling_copy = send(
        coupling.at[core], coupling.at[core], coupling_sems.at[0], coupling_sems.at[1], other
    )
    factor_copy.wait_recv()
    factor = jnp.where(node // 2 == core, factor_out[...], factor_in[...])
    basis[...] = 128.0 * lax.dot_general(
        rows_here, factor, last, precision=HIGH, preferred_element_type=F32
    )
    factor_copy.wait_send()
    coupling_copy.wait()


    for copy in list(relays.values()) + nears + list(swap.values()) + small:
        copy.wait_send()
    for copy in list(hops.values()) + list(outs.values()) + list(fars.values()):
        copy.wait_send()


def whole(*arguments):
    dma = pltpu.SemaphoreType.DMA

    def block(*shape, kind=F32):
        return pltpu.VMEM(shape, kind)

    i32 = jnp.int32
    return pl.pallas_call(
        whole_kernel,
        out_shape=(
            jax.ShapeDtypeStruct((ROWS, RANK), F32),
            jax.ShapeDtypeStruct((2, RANK, RANK), F32),
        ),
        in_specs=[HBM] * 6,
        out_specs=(VMEM,) * 2,
        scratch_shapes=[
            block(FEATS, ROWS, kind=BF16), block(SAMPLES, ROWS, kind=BF16), block(1, ROWS, kind=i32),
            block(1, 16, kind=i32), block(1, 32, kind=i32), block(4, RANK, kind=i32), dma((6,)),
            block(25, SPAN, 128, kind=BF16), block(2, 4, 2, 16, ROWS, kind=BF16), block(2, 4, 8, 128, kind=i32),
            block(SPAN, 128, kind=BF16), block(16, ROWS, kind=BF16), block(8, 128, kind=i32),
            block(8, 32, 128), block(8, 32, 128), block(8, 2 * ROWS, 16, kind=BF16),
            block(2 * ROWS, 2 * ROWS, kind=BF16), block(2 * ROWS, 2 * ROWS, kind=BF16), block(2, 2, 4, ROWS, RANK),
            dma((8, 2)), dma((8, 2)), dma((6, 2, 2)), dma((6, 2, 2)), dma((6, 2)), dma((6, 2)),
            dma((2, 4)), dma((2, 4)), dma((2, 4)), dma((2, 4)),
            block(2, 4, ROWS, RANK), block(2, ROWS, RANK, kind=LINK), block(2, 2, 128, RANK, kind=LINK),
            block(2, 2, ROWS, RANK, kind=LINK), block(2, 2, ROWS, RANK, kind=LINK),
            block(512, RANK), block(256, RANK), block(2, 8, 128), block(32, 8, RANK),
            block(4, 4, 4, 2, 8, 128), block(4, 4, 4, 2, 8, 128),
            dma((2, 4)), dma((2, 4)), dma((2, 2, 2)), dma((2, 2, 2, 2)), dma((2,)), dma((32,)), dma((32,)),
            dma((8, 2)), dma((4, 2, 2)), dma((24,)), dma((24,)),
            block(2, RANK, RANK), block(2, RANK, RANK), block(RANK, RANK), block(RANK, RANK), dma((2,)), dma((2,)),
        ],
        compiler_params=pltpu.CompilerParams(
            collective_id=0, has_side_effects=True, vmem_limit_bytes=VMEM_LIMIT
        ),
        name="whole",
    )(*arguments)


def body(points, omega, tree_order, sibling_blocks, cousin_blocks, skeleton):
    return whole(points, omega, tree_order.reshape(1, ROWS), sibling_blocks, cousin_blocks, skeleton)


def solution(mesh):
    return jax.shard_map(
        body,
        mesh=mesh,
        in_specs=(
            P(None, ("leaf", "sub")),
            P(None, ("leaf", "sub")),
            P(("leaf", "sub")),
            P("leaf", None),
            P("leaf", None),
            P(),
        ),
        out_specs=(P(("leaf", "sub"), None), P()),
        check_vma=False,
    )
```

time: 104 us -> 94.5 us (0.909)
  Pallas kernels: 98 us -> 91.2 us
  local copies, waits for them, and re-layouts: 5.01 us -> 2.52 us
    pallas_call x4 -> x1, Pallas kernels: 98 us -> 91.2 us  [whole(): pl.pallas_call(whole_kernel, out_shape=(jax.ShapeDtypeStruct((ROWS, RANK)...]
    unnamed x14 -> x4, local copies, waits for them, and re-layouts: 5.01 us -> 2.52 us
where the time goes in v5:
time: 94.5 us; the launch traced here: 94.3 us
  Pallas kernels  91.2 us (97%)
  local copies, waits for them, and re-layouts  2.52 us (3%)
    pallas_call x1, Pallas kernels, whole(): pl.pallas_call(whole_kernel, out_shape=(jax.ShapeDtypeStruct((ROWS, RANK)...  91.2 us
    unnamed x4, local copies, waits for them, and re-layouts  2.52 us

profile of v5, /device:TPU:1, one launch (start us, length us, event | category | flops | bytes accessed | tf_op | source)
XLA Modules:
  0.0 94.3 jit_solution(1589792724782643248)
XLA Ops:
  0.6 91.2 %whole.1 = (f32[256,256]{1,0:T(8,128)}, f32[2,256,256]{2,1,0:T(8,128)}) custom-call(bf16[8,256]{1,0:T(8,128)(2,1)} %points_in.1, bf16[128,256]{1,0:T(8,128)(2,1)} %omega_in.1, s32[1,256]{1,0:T(1,128)} %bitcast.1, s32[1,16]{1,0:T(1,128)} %siblings_in.1, s32[1,32]{1,0:T(1,128)} %cousins_in.1, s32[4,256]{1,0:T(4,128)} %skeleton_in.1), custom_call_target="tpu_custom_call" | custom-call | tf_op jit(solution)/shard_map/whole/pallas_call | solution.py:680
  91.8 0.0 copy-start
  91.8 1.7 %copy.10 = f32[256,256]{1,0:T(8,128)} copy(f32[256,256]{1,0:T(8,128)} %get-tuple-element.4) | data formatting | bytes 524288
  93.5 0.0 copy-done
  93.5 0.8 copy.11
Async XLA Ops:
  91.8 1.7 %copy-start = (f32[2,256,256]{2,1,0:T(8,128)S(1)}, f32[2,256,256]{2,1,0:T(8,128)}, u32[]{:S(2)}) copy-start(f32[2,256,256]{2,1,0:T(8,128)} %get-tuple-element.5) | copy-start | bytes 1572868

commit v6 on v5

--- a/solution.py
+++ b/solution.py
@@ -134,7 +134,7 @@
     points, omega, tree_order, siblings, cousins, skeleton, load_sems,
     blocks, row_points, lists, own, own_rows, own_lists, near_mask, far_mask, rows, even_tile, odd_tile, parts,
     hop_send, hop_recv, out_send, out_recv, far_send, far_recv, rows_send, rows_recv, list_send, list_recv,
-    other_core, relay_out, relay_in, near_out, near_in, table, other_table, piece, pieces, full_a, full_b,
+    other_core, relay_out, relay_in, near_out, near_in, table, other_table, piece, pieces, landing, full_a, full_b,
     core_send, core_recv, relay_sems, near_sems, table_sems, piece_send, piece_recv,
     z_send, z_recv, y_sems, x_sems,
     work, chosen, factor_out, factor_in, factor_sems, coupling_sems,
@@ -303,14 +303,21 @@
         def two_steps(step, carry):
             at0, use0 = item(2 * step)
             at1, use1 = item(2 * step + 1)
-            at2, use2 = item((2 * step + 2) % count)
+            at2, use2 = item(2 * step + 2)
             kernel_tile(kind * 4 + at1, use1, odd_tile)
             add(kind, at0, use0, even_tile)
             kernel_tile(kind * 4 + at2, use2, even_tile)
             add(kind, at1, use1, odd_tile)
             return carry
 
-        lax.fori_loop(0, count // 2, two_steps, 0)
+        lax.fori_loop(0, (count - 1) // 2, two_steps, 0)
+        if count % 2:
+            add(kind, *item(count - 1), even_tile)
+        else:
+            at, use = item(count - 1)
+            kernel_tile(kind * 4 + at, use, odd_tile)
+            add(kind, *item(count - 2), even_tile)
+            add(kind, at, use, odd_tile)
 
     batch(1, 4, lambda i: (i, 0))
     relay(0, MATE)
@@ -365,8 +372,8 @@
 
     def pass_on(kind, side, first, rows_of, who):
         ref = near_out.at[kind, side, rows_of]
-        landing = near_in.at[kind, side, rows_of]
-        nears.append(send(ref, landing, near_sems.at[0, kind, side, first], near_sems.at[1, kind, side, first], who))
+        target = near_in.at[kind, side, rows_of]
+        nears.append(send(ref, target, near_sems.at[0, kind, side, first], near_sems.at[1, kind, side, first], who))
 
     def start_sum(kind):
         relay_out[kind] = partial(0, kind).astype(LINK)
@@ -376,11 +383,9 @@
                 relay_sems.at[0, kind, side], relay_sems.at[1, kind, side], who,
             )
 
-    def middle_sum(kind):
-        near_out[kind, 0] = partial(1, kind).astype(LINK)
-        pass_on(kind, 0, 0, upper, forward[kind])
-        near_out[kind, 1] = partial(2, kind).astype(LINK)
-        pass_on(kind, 1, 0, lower, backward[kind])
+    def middle_sum(kind, side):
+        near_out[kind, side] = partial(1 + side, kind).astype(LINK)
+        pass_on(kind, side, 0, (upper, lower)[side], (forward, backward)[side][kind])
 
     def end_sum(kind):
         relays[kind, 0].wait_recv()
@@ -402,17 +407,23 @@
         give(step, 1)
     landed(2, 3, 5)
     passed(2, 3, 5)
-    batch(0, 10, lambda i: ((x + 2 + 3 * (i // 5)) % 4, 7 + i % 5))
-    give(0, 0)
-    give(1, 0)
+
+    def last_batch(step):
+        at = order[step][0]
+        batch(0, 5, lambda i: (at, 7 + i))
+        give(step, 0)
+
+    last_batch(0)
     start_sum(1)
-    middle_sum(1)
-    batch(0, 10, lambda i: ((x + 3 + i // 5) % 4, 7 + i % 5))
-    give(2, 0)
-    give(3, 0)
+    middle_sum(1, 0)
+    middle_sum(1, 1)
+    last_batch(1)
     start_sum(0)
+    last_batch(2)
     end_sum(1)
-    middle_sum(0)
+    middle_sum(0, 0)
+    last_batch(3)
+    middle_sum(0, 1)
     end_sum(0)
     total = partial(3, 1) + partial(3, 0)
     first_row = (leaf * 2 + core) * ROWS
@@ -450,7 +461,7 @@
         return other_table.at[pl.ds(pl.multiple_of(first, 8), 8)]
 
     spreads = []
-    for slot, where, who in mates:
+    for slot, where, who in sorted(mates, key=lambda mate: -sum(min(d, 4 - d) for d in (mate[0] // 16, mate[0] // 4 % 4, mate[0] % 4))):
         spreads.append(
             send(chunk(where), pieces.at[slot], piece_send.at[slot], piece_recv.at[slot], who)
         )
@@ -464,94 +475,60 @@
     for copy in spreads:
         copy.wait_send()
 
-    home_a, home_b = full_a.at[x, y, z % 4, core], full_b.at[y, x, z % 4, core]
-
-    def drop(dz, half):
+    def drop(dz):
         return pltpu.make_async_remote_copy(
-            src_ref=piece.at[half],
-            dst_ref=(home_a, home_b)[half],
-            send_sem=z_send.at[dz, half],
-            recv_sem=z_recv.at[z % 4, core, half],
+            src_ref=piece,
+            dst_ref=landing.at[z % 4, core],
+            send_sem=z_send.at[dz],
+            recv_sem=z_recv.at[z % 4, core],
             device_id=column[dz],
             device_id_type=MESH,
         )
 
-    def arrival(plane, c, half):
-        landing = (full_a.at[x, y, plane, c], full_b.at[y, x, plane, c])[half]
-        return pltpu.make_async_remote_copy(
-            src_ref=piece.at[half],
-            dst_ref=landing,
-            send_sem=z_send.at[0, half],
-            recv_sem=z_recv.at[plane, c, half],
-            device_id=other,
-            device_id_type=MESH,
-        )
-
     for dz in (4, 3, 5, 2, 6, 1, 7):
-        for half in range(2):
-            drop(dz, half).start()
+        drop(dz).start()
 
     @pl.when(pair == core)
     def _():
-        home_a[...] = piece[0]
-        home_b[...] = piece[1]
+        landing[z % 4, core] = piece[...]
 
     @pl.when(pair != core)
     def _():
-        for half in range(2):
-            drop(0, half).start()
-
-    for plane in range(4):
-        for c in range(2):
+        drop(0).start()
+
+    def fan(ref, sems, first, line):
+        return [
+            send(ref, ref, sems.at[0, first + d - 1], sems.at[1, first + d - 1], line[d]) for d in (2, 1, 3)
+        ]
+
+    def first_leg(c):
+        for plane in range(4):
 
             @pl.when((core * 4 + plane != z) | (core != c))
-            def _(plane=plane, c=c):
-                for half in range(2):
-                    arrival(plane, c, half).wait_recv()
-
-    cuts = (pl.ds(0, 2), pl.ds(2, 2))
-
-    def push(ref, sems, k, who):
-        return send(ref, ref, sems.at[2 * k], sems.at[2 * k + 1], who)
-
-    def ring(at, sems, first_k, forward, backward):
-        return [
-            push(at.at[cuts[0]], sems, first_k, forward),
-            push(at.at[cuts[1]], sems, first_k + 1, backward),
-            push(at.at[cuts[1]], sems, first_k + 2, forward),
-            push(at.at[cuts[0]], sems, first_k + 3, backward),
-        ]
-
-    def pass_along(copies, sems, first_k, before, after, forward, backward):
-        copies[0].wait_recv()
-        copies.append(push(before.at[cuts[0]], sems, first_k + 4, forward))
-        copies[1].wait_recv()
-        copies.append(push(after.at[cuts[1]], sems, first_k + 5, backward))
-
-    first = ring(full_a.at[x, y], y_sems, 0, above, below)
-    second = ring(full_b.at[y, x], x_sems, 0, right, left_side)
-    pass_along(first, y_sems, 0, full_a.at[x, last_y], full_a.at[x, next_y], above, below)
-    pass_along(second, x_sems, 0, full_b.at[y, behind], full_b.at[y, ahead], right, left_side)
-    for copy in first[2:6]:
+            def _(plane=plane):
+                pltpu.make_async_remote_copy(
+                    src_ref=piece,
+                    dst_ref=landing.at[plane, c],
+                    send_sem=z_send.at[0],
+                    recv_sem=z_recv.at[plane, c],
+                    device_id=other,
+                    device_id_type=MESH,
+                ).wait_recv()
+
+        full_a[c, x, y] = landing[:, c, 0]
+        full_b[c, y, x] = landing[:, c, 1]
+        return fan(full_a.at[c, x, y], y_sems, 6 * c, along_y) + fan(full_b.at[c, y, x], x_sems, 6 * c, along_x)
+
+    def second_leg(c, copies):
+        for copy in copies:
+            copy.wait_recv()
+        return fan(full_a.at[c, x], x_sems, 6 * c + 3, along_x) + fan(full_b.at[c, y], y_sems, 6 * c + 3, along_y)
+
+    legs = [first_leg(0)]
+    legs.append(second_leg(0, legs[0]))
+    legs.append(first_leg(1))
+    for copy in legs[1]:
         copy.wait_recv()
-    third = ring(full_a.at[x], x_sems, 6, right, left_side)
-    for copy in second[2:6]:
-        copy.wait_recv()
-    fourth = ring(full_b.at[y], y_sems, 6, above, below)
-    pass_along(third, x_sems, 6, full_a.at[behind], full_a.at[ahead], right, left_side)
-    pass_along(fourth, y_sems, 6, full_b.at[last_y], full_b.at[next_y], above, below)
-    for copy in third[2:] + fourth[2:]:
-        copy.wait_recv()
-    for copy in first + second + third + fourth:
-        copy.wait_send()
-    for dz in range(1, 8):
-        for half in range(2):
-            drop(dz, half).wait_send()
-
-    @pl.when(pair != core)
-    def _():
-        for half in range(2):
-            drop(0, half).wait_send()
 
     row = lax.broadcasted_iota(jnp.int32, (RANK, RANK), 0)
     col = lax.broadcasted_iota(jnp.int32, (RANK, RANK), 1)
@@ -561,9 +538,8 @@
             for at_y in range(4):
                 span = pl.ds(at_x * 64 + at_y * 16, 16)
                 planes = pl.ds(2 * n, 2)
-                for kind, target in enumerate((work, chosen)):
-                    target[n, span, 0:128] = full_a[at_x, at_y, planes, kind].reshape(16, 128)
-                    target[n, span, 128:256] = full_b[at_y, at_x, planes, kind].reshape(16, 128)
+                work[n, span, 0:128] = full_a[0, at_x, at_y, planes].reshape(16, 128)
+                work[n, span, 128:256] = full_b[0, at_y, at_x, planes].reshape(16, 128)
         skeleton_points.append(
             jnp.concatenate([work[n, 128:136, 0:128], work[n, 136:144, 0:128]], axis=1)
         )
@@ -576,10 +552,6 @@
     row_side = features(skeleton_points[0], 4.0, True).T.astype(BF16)
     col_side = features(skeleton_points[1], 1.0, False).astype(BF16)
     kernel_skel = jnp.exp(jnp.dot(row_side, col_side, preferred_element_type=F32))
-    right = jnp.dot(kernel_skel, chosen[1], precision=HIGH, preferred_element_type=F32)
-    middle = lax.dot_general(
-        chosen[0], right, (((0,), (0,)), ((), ())), precision=HIGH, preferred_element_type=F32
-    )
 
     lane8 = lax.broadcasted_iota(jnp.int32, (8, 128), 1)
     row8 = lax.broadcasted_iota(jnp.int32, (8, 128), 0)
@@ -643,6 +615,22 @@
                     precision=HIGH, preferred_element_type=F32,
                 )
                 work[n, top + 64 :, :] = jnp.where(tcol // 64 == p, 0.0, work[n, top + 64 :, :]) - update
+        if p == 0:
+            legs.append(second_leg(1, legs[2]))
+        if p == 1:
+            for copy in legs[3]:
+                copy.wait_recv()
+            for n in range(2):
+                for at_x in range(4):
+                    for at_y in range(4):
+                        span = pl.ds(at_x * 64 + at_y * 16, 16)
+                        planes = pl.ds(2 * n, 2)
+                        chosen[n, span, 0:128] = full_a[1, at_x, at_y, planes].reshape(16, 128)
+                        chosen[n, span, 128:256] = full_b[1, at_y, at_x, planes].reshape(16, 128)
+            right_part = jnp.dot(kernel_skel, chosen[1], precision=HIGH, preferred_element_type=F32)
+            middle = lax.dot_general(
+                chosen[0], right_part, (((0,), (0,)), ((), ())), precision=HIGH, preferred_element_type=F32
+            )
 
     size = jnp.where(node % 2 == 0, sizes[0], sizes[1])
     factor_out[...] = work[node % 2] * size
@@ -664,8 +652,15 @@
     coupling_copy.wait()
 
 
-    for copy in list(relays.values()) + nears + list(swap.values()) + small:
+    for copy in list(relays.values()) + nears + list(swap.values()) + small + sum(legs, []):
         copy.wait_send()
+    for dz in range(1, 8):
+        drop(dz).wait_send()
+
+    @pl.when(pair != core)
+    def _():
+        drop(0).wait_send()
+
     for copy in list(hops.values()) + list(outs.values()) + list(fars.values()):
         copy.wait_send()
 
@@ -697,9 +692,9 @@
             block(2, 4, ROWS, RANK), block(2, ROWS, RANK, kind=LINK), block(2, 2, 128, RANK, kind=LINK),
             block(2, 2, ROWS, RANK, kind=LINK), block(2, 2, ROWS, RANK, kind=LINK),
             block(512, RANK), block(256, RANK), block(2, 8, 128), block(32, 8, RANK),
-            block(4, 4, 4, 2, 8, 128), block(4, 4, 4, 2, 8, 128),
+            block(4, 2, 2, 8, 128), block(2, 4, 4, 4, 8, 128), block(2, 4, 4, 4, 8, 128),
             dma((2, 4)), dma((2, 4)), dma((2, 2, 2)), dma((2, 2, 2, 2)), dma((2,)), dma((32,)), dma((32,)),
-            dma((8, 2)), dma((4, 2, 2)), dma((24,)), dma((24,)),
+            dma((8,)), dma((4, 2)), dma((2, 12)), dma((2, 12)),
             block(2, RANK, RANK), block(2, RANK, RANK), block(RANK, RANK), block(RANK, RANK), dma((2,)), dma((2,)),
         ],
         compiler_params=pltpu.CompilerParams(

time: 94.5 us -> 89.3 us (0.945)
  Pallas kernels: 91.2 us -> 86 us
    pallas_call x1, Pallas kernels: 91.2 us -> 86 us  [whole(): pl.pallas_call(whole_kernel, out_shape=(jax.ShapeDtypeStruct((ROWS, RANK)...]
where the time goes in v6:
time: 89.3 us; the launch traced here: 89.2 us
  Pallas kernels  86 us (96%)
  local copies, waits for them, and re-layouts  2.52 us (3%)
    pallas_call x1, Pallas kernels, whole(): pl.pallas_call(whole_kernel, out_shape=(jax.ShapeDtypeStruct((ROWS, RANK)...  86 us
    unnamed x4, local copies, waits for them, and re-layouts  2.52 us

profile of v6, /device:TPU:1, one launch (start us, length us, event | category | flops | bytes accessed | tf_op | source)
XLA Modules:
  0.0 89.2 jit_solution(6290831199543553184)
XLA Ops:
  0.6 86.0 %whole.1 = (f32[256,256]{1,0:T(8,128)}, f32[2,256,256]{2,1,0:T(8,128)}) custom-call(bf16[8,256]{1,0:T(8,128)(2,1)} %points_in.1, bf16[128,256]{1,0:T(8,128)(2,1)} %omega_in.1, s32[1,256]{1,0:T(1,128)} %bitcast.1, s32[1,16]{1,0:T(1,128)} %siblings_in.1, s32[1,32]{1,0:T(1,128)} %cousins_in.1, s32[4,256]{1,0:T(4,128)} %skeleton_in.1), custom_call_target="tpu_custom_call" | custom-call | tf_op jit(solution)/shard_map/whole/pallas_call | solution.py:675
  86.7 0.0 copy-start
  86.7 1.7 %copy.10 = f32[256,256]{1,0:T(8,128)} copy(f32[256,256]{1,0:T(8,128)} %get-tuple-element.4) | data formatting | bytes 524288
  88.4 0.0 copy-done
  88.4 0.8 copy.11
Async XLA Ops:
  86.7 1.7 %copy-start = (f32[2,256,256]{2,1,0:T(8,128)S(1)}, f32[2,256,256]{2,1,0:T(8,128)}, u32[]{:S(2)}) copy-start(f32[2,256,256]{2,1,0:T(8,128)} %get-tuple-element.5) | copy-start | bytes 1572868

commit v7 on v6

--- a/solution.py
+++ b/solution.py
@@ -12,7 +12,6 @@
 HIGHEST = lax.Precision.HIGHEST
 F32 = jnp.float32
 BF16 = jnp.bfloat16
-VMEM = pl.BlockSpec(memory_space=pltpu.VMEM)
 HBM = pl.BlockSpec(memory_space=pltpu.HBM)
 
 ROWS = 256
@@ -134,10 +133,10 @@
     points, omega, tree_order, siblings, cousins, skeleton, load_sems,
     blocks, row_points, lists, own, own_rows, own_lists, near_mask, far_mask, rows, even_tile, odd_tile, parts,
     hop_send, hop_recv, out_send, out_recv, far_send, far_recv, rows_send, rows_recv, list_send, list_recv,
-    other_core, relay_out, relay_in, near_out, near_in, table, other_table, piece, pieces, landing, full_a, full_b,
+    other_core, relay_out, relay_in, near_out, near_in, table, sums, piece, pieces, landing, full_a, full_b,
     core_send, core_recv, relay_sems, near_sems, table_sems, piece_send, piece_recv,
     z_send, z_recv, y_sems, x_sems,
-    work, chosen, factor_out, factor_in, factor_sems, coupling_sems,
+    work, chosen, factor_out, factor_in, coupling_out, basis_out, factor_sems, coupling_sems, result_sems,
 ):
     loads = [
         pltpu.make_async_copy(source, target, load_sems.at[k])
@@ -408,10 +407,11 @@
     landed(2, 3, 5)
     passed(2, 3, 5)
 
-    def last_batch(step):
+    def last_batch(step, first=0, count=5):
         at = order[step][0]
-        batch(0, 5, lambda i: (at, 7 + i))
-        give(step, 0)
+        batch(0, count, lambda i: (at, 7 + first + i))
+        if first + count == 5:
+            give(step, 0)
 
     last_batch(0)
     start_sum(1)
@@ -419,12 +419,13 @@
     middle_sum(1, 1)
     last_batch(1)
     start_sum(0)
+    end_sum(1)
     last_batch(2)
-    end_sum(1)
     middle_sum(0, 0)
-    last_batch(3)
+    last_batch(3, 0, 3)
     middle_sum(0, 1)
     end_sum(0)
+    last_batch(3, 3, 2)
     total = partial(3, 1) + partial(3, 0)
     first_row = (leaf * 2 + core) * ROWS
     row = lax.broadcasted_iota(jnp.int32, (ROWS, RANK), 0) + first_row
@@ -439,62 +440,73 @@
             total = total + near_in[kind, side].astype(F32)
     rows_here = total
 
-    table[0:256, :] = lax.dot_general(
-        rows_here, rows_here, (((0,), (0,)), ((), ())), precision=HIGHEST, preferred_element_type=F32
-    )
-    table[128:256, 0:128] = jnp.zeros((128, 128), F32)
-    table[128:136, 0:128] = own_skeleton[:, 0:128]
-    table[136:144, 0:128] = own_skeleton[:, 128:256]
-    table[256:512, :] = lax.dot_general(
-        picked, rows_here, (((0,), (0,)), ((), ())), precision=HIGHEST, preferred_element_type=F32
-    )
-    start = pl.multiple_of((1 - core) * 256, 256)
-    swap_table = send(
-        table.at[pl.ds(start, 256)], other_table, table_sems.at[0], table_sems.at[1], other
-    )
-    swap_table.wait()
-    keep = pl.multiple_of(core * 256, 256)
-    other_table[...] += table[pl.ds(keep, 256), :]
-
-    def chunk(where):
+    def product(c, first):
+        values = lax.dot_general(
+            first, rows_here, (((0,), (0,)), ((), ())), precision=HIGH, preferred_element_type=F32
+        )
+        table[c, 0] = values[:, 0:128]
+        table[c, 1] = values[:, 128:256]
+
+    def swap_table(c):
+        return send(table.at[c, 1 - core], sums.at[c], table_sems.at[0, c], table_sems.at[1, c], other)
+
+    def spread_table(c):
+        swaps[c].wait_recv()
+        sums[c] += table[c, core]
+        copies = []
+        for slot, where, who in far_first:
+            copies.append(
+                send(chunk(c, where), pieces.at[c, slot], piece_send.at[c, slot], piece_recv.at[c, slot], who)
+            )
+        return copies
+
+    def chunk(c, where):
         first = (where[0] * 8 + where[1] * 2 + where[2] % 2) * 8
-        return other_table.at[pl.ds(pl.multiple_of(first, 8), 8)]
-
-    spreads = []
-    for slot, where, who in sorted(mates, key=lambda mate: -sum(min(d, 4 - d) for d in (mate[0] // 16, mate[0] // 4 % 4, mate[0] % 4))):
-        spreads.append(
-            send(chunk(where), pieces.at[slot], piece_send.at[slot], piece_recv.at[slot], who)
-        )
-    sums = chunk((x, y, z))[...]
-    for copy in spreads:
-        copy.wait_recv()
-    for slot, _, _ in mates:
-        sums = sums + pieces[slot]
-    piece[0] = sums[:, 0:128]
-    piece[1] = sums[:, 128:256]
-    for copy in spreads:
-        copy.wait_send()
-
-    def drop(dz):
+        return sums.at[c, pl.ds(pl.multiple_of(first, 8), 8)]
+
+    def reach(mate):
+        return sum(min(d, 4 - d) for d in (mate[0] // 16, mate[0] // 4 % 4, mate[0] % 4))
+
+    def drop(c, dz):
         return pltpu.make_async_remote_copy(
-            src_ref=piece,
-            dst_ref=landing.at[z % 4, core],
-            send_sem=z_send.at[dz],
-            recv_sem=z_recv.at[z % 4, core],
+            src_ref=piece.at[c],
+            dst_ref=landing.at[c, z % 4, core],
+            send_sem=z_send.at[c, dz],
+            recv_sem=z_recv.at[c, z % 4, core],
             device_id=column[dz],
             device_id_type=MESH,
         )
 
-    for dz in (4, 3, 5, 2, 6, 1, 7):
-        drop(dz).start()
-
-    @pl.when(pair == core)
-    def _():
-        landing[z % 4, core] = piece[...]
-
-    @pl.when(pair != core)
-    def _():
-        drop(0).start()
+    def collect_chunk(c):
+        result = chunk(c, (x, y, z))[...]
+        for copy in spreads[c]:
+            copy.wait_recv()
+        for slot, _, _ in mates:
+            result = result + pieces[c, slot]
+        piece[c] = result
+        for dz in (4, 3, 5, 2, 6, 1, 7):
+            drop(c, dz).start()
+
+        @pl.when(pair == core)
+        def _():
+            landing[c, z % 4, core] = piece[c]
+
+        @pl.when(pair != core)
+        def _():
+            drop(c, 0).start()
+
+    far_first = sorted(mates, key=reach, reverse=True)
+    product(0, rows_here)
+    table[0, 0, 128:256, :] = jnp.zeros((128, 128), F32)
+    table[0, 0, 128:136, :] = own_skeleton[:, 0:128]
+    table[0, 0, 136:144, :] = own_skeleton[:, 128:256]
+    swaps = [swap_table(0)]
+    product(1, picked)
+    swaps.append(swap_table(1))
+    spreads = [spread_table(0)]
+    spreads.append(spread_table(1))
+    collect_chunk(0)
+    collect_chunk(1)
 
     def fan(ref, sems, first, line):
         return [
@@ -503,20 +515,21 @@
 
     def first_leg(c):
         for plane in range(4):
-
-            @pl.when((core * 4 + plane != z) | (core != c))
-            def _(plane=plane):
-                pltpu.make_async_remote_copy(
-                    src_ref=piece,
-                    dst_ref=landing.at[plane, c],
-                    send_sem=z_send.at[0],
-                    recv_sem=z_recv.at[plane, c],
-                    device_id=other,
-                    device_id_type=MESH,
-                ).wait_recv()
-
-        full_a[c, x, y] = landing[:, c, 0]
-        full_b[c, y, x] = landing[:, c, 1]
+            for half in range(2):
+
+                @pl.when((core * 4 + plane != z) | (core != half))
+                def _(plane=plane, half=half):
+                    pltpu.make_async_remote_copy(
+                        src_ref=piece.at[c],
+                        dst_ref=landing.at[c, plane, half],
+                        send_sem=z_send.at[c, 0],
+                        recv_sem=z_recv.at[c, plane, half],
+                        device_id=other,
+                        device_id_type=MESH,
+                    ).wait_recv()
+
+        full_a[c, x, y] = landing[c, :, 0]
+        full_b[c, y, x] = landing[c, :, 1]
         return fan(full_a.at[c, x, y], y_sems, 6 * c, along_y) + fan(full_b.at[c, y, x], x_sems, 6 * c, along_x)
 
     def second_leg(c, copies):
@@ -617,7 +630,7 @@
                 work[n, top + 64 :, :] = jnp.where(tcol // 64 == p, 0.0, work[n, top + 64 :, :]) - update
         if p == 0:
             legs.append(second_leg(1, legs[2]))
-        if p == 1:
+        if p == 2:
             for copy in legs[3]:
                 copy.wait_recv()
             for n in range(2):
@@ -637,29 +650,38 @@
     factor_copy = send(factor_out, factor_in, factor_sems.at[0], factor_sems.at[1], other)
     last = (((1,), (1,)), ((), ()))
     half = jnp.dot(work[0], middle, precision=HIGH, preferred_element_type=F32)
-    coupling[core] = ((16384.0 / math.sqrt(RANK)) * sizes[0] * sizes[1]) * lax.dot_general(
+    coupling_out[...] = ((16384.0 / math.sqrt(RANK)) * sizes[0] * sizes[1]) * lax.dot_general(
         half, work[1], last, precision=HIGH, preferred_element_type=F32
     )
     coupling_copy = send(
-        coupling.at[core], coupling.at[core], coupling_sems.at[0], coupling_sems.at[1], other
+        coupling_out, coupling.at[core], coupling_sems.at[0], coupling_sems.at[1], other
     )
+    results = [pltpu.make_async_copy(coupling_out, coupling.at[core], result_sems.at[0])]
+    results[0].start()
     factor_copy.wait_recv()
     factor = jnp.where(node // 2 == core, factor_out[...], factor_in[...])
-    basis[...] = 128.0 * lax.dot_general(
+    basis_out[...] = 128.0 * lax.dot_general(
         rows_here, factor, last, precision=HIGH, preferred_element_type=F32
     )
+    results.append(pltpu.make_async_copy(basis_out, basis, result_sems.at[1]))
+    results[1].start()
     factor_copy.wait_send()
     coupling_copy.wait()
-
+    for copy in results:
+        copy.wait()
 
     for copy in list(relays.values()) + nears + list(swap.values()) + small + sum(legs, []):
         copy.wait_send()
-    for dz in range(1, 8):
-        drop(dz).wait_send()
-
-    @pl.when(pair != core)
-    def _():
-        drop(0).wait_send()
+    for c in range(2):
+        swaps[c].wait_send()
+        for copy in spreads[c]:
+            copy.wait_send()
+        for dz in range(1, 8):
+            drop(c, dz).wait_send()
+
+        @pl.when(pair != core)
+        def _(c=c):
+            drop(c, 0).wait_send()
 
     for copy in list(hops.values()) + list(outs.values()) + list(fars.values()):
         copy.wait_send()
@@ -679,7 +701,7 @@
             jax.ShapeDtypeStruct((2, RANK, RANK), F32),
         ),
         in_specs=[HBM] * 6,
-        out_specs=(VMEM,) * 2,
+        out_specs=(HBM,) * 2,
         scratch_shapes=[
             block(FEATS, ROWS, kind=BF16), block(SAMPLES, ROWS, kind=BF16), block(1, ROWS, kind=i32),
             block(1, 16, kind=i32), block(1, 32, kind=i32), block(4, RANK, kind=i32), dma((6,)),
@@ -691,11 +713,12 @@
             dma((2, 4)), dma((2, 4)), dma((2, 4)), dma((2, 4)),
             block(2, 4, ROWS, RANK), block(2, ROWS, RANK, kind=LINK), block(2, 2, 128, RANK, kind=LINK),
             block(2, 2, ROWS, RANK, kind=LINK), block(2, 2, ROWS, RANK, kind=LINK),
-            block(512, RANK), block(256, RANK), block(2, 8, 128), block(32, 8, RANK),
-            block(4, 2, 2, 8, 128), block(2, 4, 4, 4, 8, 128), block(2, 4, 4, 4, 8, 128),
-            dma((2, 4)), dma((2, 4)), dma((2, 2, 2)), dma((2, 2, 2, 2)), dma((2,)), dma((32,)), dma((32,)),
-            dma((8,)), dma((4, 2)), dma((2, 12)), dma((2, 12)),
-            block(2, RANK, RANK), block(2, RANK, RANK), block(RANK, RANK), block(RANK, RANK), dma((2,)), dma((2,)),
+            block(2, 2, RANK, 128), block(2, RANK, 128), block(2, 8, 128), block(2, 32, 8, 128),
+            block(2, 4, 2, 8, 128), block(2, 4, 4, 4, 8, 128), block(2, 4, 4, 4, 8, 128),
+            dma((2, 4)), dma((2, 4)), dma((2, 2, 2)), dma((2, 2, 2, 2)), dma((2, 2)), dma((2, 32)), dma((2, 32)),
+            dma((2, 8)), dma((2, 4, 2)), dma((2, 12)), dma((2, 12)),
+            block(2, RANK, RANK), block(2, RANK, RANK), block(RANK, RANK), block(RANK, RANK), block(RANK, RANK),
+            block(ROWS, RANK), dma((2,)), dma((2,)), dma((2,)),
         ],
         compiler_params=pltpu.CompilerParams(
             collective_id=0, has_side_effects=True, vmem_limit_bytes=VMEM_LIMIT

time: 89.3 us -> 86.4 us (0.968)
  Pallas kernels: 86 us -> 83 us
    pallas_call x1, Pallas kernels: 86 us -> 83 us  [whole(): pl.pallas_call(whole_kernel, out_shape=(jax.ShapeDtypeStruct((ROWS, RANK)...]
where the time goes in v7:
time: 86.4 us; the launch traced here: 86.2 us
  Pallas kernels  83 us (96%)
  local copies, waits for them, and re-layouts  2.52 us (3%)
    pallas_call x1, Pallas kernels, whole(): pl.pallas_call(whole_kernel, out_shape=(jax.ShapeDtypeStruct((ROWS, RANK)...  83 us
    unnamed x4, local copies, waits for them, and re-layouts  2.52 us

profile of v7, /device:TPU:1, one launch (start us, length us, event | category | flops | bytes accessed | tf_op | source)
XLA Modules:
  0.0 86.2 jit_solution(1728677978779549091)
XLA Ops:
  0.6 83.0 %whole.1 = (f32[256,256]{1,0:T(8,128)}, f32[2,256,256]{2,1,0:T(8,128)}) custom-call(bf16[8,256]{1,0:T(8,128)(2,1)} %points_in.1, bf16[128,256]{1,0:T(8,128)(2,1)} %omega_in.1, s32[1,256]{1,0:T(1,128)} %bitcast.1, s32[1,16]{1,0:T(1,128)} %siblings_in.1, s32[1,32]{1,0:T(1,128)} %cousins_in.1, s32[4,256]{1,0:T(4,128)} %skeleton_in.1), custom_call_target="tpu_custom_call" | custom-call | tf_op jit(solution)/shard_map/whole/pallas_call | solution.py:697
  83.7 0.0 copy-start
  83.7 1.7 %copy.10 = f32[256,256]{1,0:T(8,128)} copy(f32[256,256]{1,0:T(8,128)} %get-tuple-element.4) | data formatting | bytes 524288
  85.4 0.0 copy-done
  85.4 0.8 copy.11
Async XLA Ops:
  83.7 1.7 %copy-start = (f32[2,256,256]{2,1,0:T(8,128)S(1)}, f32[2,256,256]{2,1,0:T(8,128)}, u32[]{:S(2)}) copy-start(f32[2,256,256]{2,1,0:T(8,128)} %get-tuple-element.5) | copy-start | bytes 1572868

commit v8 on v7

--- a/solution.py
+++ b/solution.py
@@ -13,6 +13,7 @@
 F32 = jnp.float32
 BF16 = jnp.bfloat16
 HBM = pl.BlockSpec(memory_space=pltpu.HBM)
+VMEM = pl.BlockSpec(memory_space=pltpu.VMEM)
 
 ROWS = 256
 FEATS = 8
@@ -20,7 +21,7 @@
 RANK = 256
 SPAN = 288
 LINK = BF16
-VMEM_LIMIT = 60 << 20
+VMEM_LIMIT = 40 << 20
 
 
 def place():
@@ -62,30 +63,35 @@
 
 
 def fold(factors, lines):
-    a, b, c, d = (factor * values for factor, values in zip(factors, lines, strict=True))
-    return (a + b) + (c + d)
+    terms = [factor * values for factor, values in zip(factors, lines, strict=True)]
+    while len(terms) > 1:
+        terms = [a + b for a, b in zip(terms[::2], terms[1::2], strict=True)]
+    return terms[0]
 
 
 def pivots(entry):
-    def pair(a, b, c):
-        scale = lax.rsqrt(a)
-        return scale, b * scale, a * lax.rsqrt(a * (a * c - b * b))
-
-    r0, l10, r1 = pair(entry(0, 0), entry(1, 0), entry(1, 1))
-    l20, l30 = entry(2, 0) * r0, entry(3, 0) * r0
-    l21, l31 = (entry(2, 1) - l20 * l10) * r1, (entry(3, 1) - l30 * l10) * r1
-    r2, l32, r3 = pair(
-        entry(2, 2) - (l20 * l20 + l21 * l21),
-        entry(3, 2) - (l30 * l20 + l31 * l21),
-        entry(3, 3) - (l30 * l30 + l31 * l31),
-    )
+    left = {(t, u): entry(t, u) for t in range(8) for u in range(t + 1)}
+    scale, lower = {}, {}
+    for t in range(0, 8, 2):
+        a, b, c = left[t, t], left[t + 1, t], left[t + 1, t + 1]
+        scale[t] = lax.rsqrt(a)
+        lower[t + 1, t] = b * scale[t]
+        scale[t + 1] = a * lax.rsqrt(a * (a * c - b * b))
+        for i in range(t + 2, 8):
+            lower[i, t] = left[i, t] * scale[t]
+            lower[i, t + 1] = (left[i, t + 1] - lower[i, t] * lower[t + 1, t]) * scale[t + 1]
+        for i in range(t + 2, 8):
+            for k in range(t + 2, i + 1):
+                left[i, k] = left[i, k] - (lower[i, t] * lower[k, t] + lower[i, t + 1] * lower[k, t + 1])
 
     def solve(values):
-        v0 = values[0] * r0
-        v1 = (values[1] - v0 * l10) * r1
-        v2 = (values[2] - (v0 * l20 + v1 * l21)) * r2
-        v3 = ((values[3] - (v0 * l30 + v1 * l31)) - v2 * l32) * r3
-        return [v0, v1, v2, v3]
+        values = list(values)
+        for t in range(0, 8, 2):
+            values[t] = values[t] * scale[t]
+            values[t + 1] = (values[t + 1] - values[t] * lower[t + 1, t]) * scale[t + 1]
+            for i in range(t + 2, 8):
+                values[i] = values[i] - (values[t] * lower[i, t] + values[t + 1] * lower[i, t + 1])
+        return values
 
     return solve
 
@@ -136,7 +142,7 @@
     other_core, relay_out, relay_in, near_out, near_in, table, sums, piece, pieces, landing, full_a, full_b,
     core_send, core_recv, relay_sems, near_sems, table_sems, piece_send, piece_recv,
     z_send, z_recv, y_sems, x_sems,
-    work, chosen, factor_out, factor_in, coupling_out, basis_out, factor_sems, coupling_sems, result_sems,
+    work, chosen, factor_out, factor_in, factor_sems, coupling_sems,
 ):
     loads = [
         pltpu.make_async_copy(source, target, load_sems.at[k])
@@ -580,32 +586,27 @@
         packed = jnp.where(lane < 64, packed[0], packed[1])
         left = [packed[8 * g : 8 * g + 8] for g in range(8)]
         inverse = [jnp.where(lane8 - group8 == row8 + 8 * g, 1.0, 0.0) for g in range(8)]
-        for j in range(0, 64, 4):
-            own, inner = j // 8, j % 8
+        for own in range(8):
             spread = {
                 g: [
-                    jnp.take_along_axis(left[g], group8 + (j + t), axis=1, mode="promise_in_bounds")
-                    for t in range(4)
+                    jnp.take_along_axis(left[g], group8 + (8 * own + t), axis=1, mode="promise_in_bounds")
+                    for t in range(8)
                 ]
                 for g in range(own, 8)
             }
 
-            def line(tile, t, inner=inner):
-                return jnp.broadcast_to(tile[inner + t : inner + t + 1, :], (8, 128))
+            def line(tile, t):
+                return jnp.broadcast_to(tile[t : t + 1, :], (8, 128))
 
             solve = pivots(lambda t, u: line(spread[own][u], t))
-            left_rows = solve([line(left[own], t) for t in range(4)])
-            inverse_rows = solve([line(inverse[own], t) for t in range(4)])
-            for g in range(own, 8):
-                if g == own and inner == 4:
-                    continue
+            left_rows = solve([line(left[own], t) for t in range(8)])
+            inverse_rows = solve([line(inverse[own], t) for t in range(8)])
+            for g in range(own + 1, 8):
                 factors = solve(spread[g])
-                if g == own:
-                    factors = [jnp.where(row8 > 3, factor, 0.0) for factor in factors]
                 left[g] = left[g] - fold(factors, left_rows)
                 inverse[g] = inverse[g] - fold(factors, inverse_rows)
-            for t in range(4):
-                inverse[own] = jnp.where(row8 == inner + t, inverse_rows[t], inverse[own])
+            for t in range(8):
+                inverse[own] = jnp.where(row8 == t, inverse_rows[t], inverse[own])
         packed = jnp.concatenate(inverse, axis=0)
         diagonal = jnp.concatenate([jnp.where(lane < 64, packed, 0.0), jnp.where(lane < 64, 0.0, packed)], axis=0)
         stacked = jnp.concatenate([work[n, top : top + 64, :] for n in range(2)], axis=0)
@@ -650,25 +651,19 @@
     factor_copy = send(factor_out, factor_in, factor_sems.at[0], factor_sems.at[1], other)
     last = (((1,), (1,)), ((), ()))
     half = jnp.dot(work[0], middle, precision=HIGH, preferred_element_type=F32)
-    coupling_out[...] = ((16384.0 / math.sqrt(RANK)) * sizes[0] * sizes[1]) * lax.dot_general(
+    coupling[core] = ((16384.0 / math.sqrt(RANK)) * sizes[0] * sizes[1]) * lax.dot_general(
         half, work[1], last, precision=HIGH, preferred_element_type=F32
     )
     coupling_copy = send(
-        coupling_out, coupling.at[core], coupling_sems.at[0], coupling_sems.at[1], other
+        coupling.at[core], coupling.at[core], coupling_sems.at[0], coupling_sems.at[1], other
     )
-    results = [pltpu.make_async_copy(coupling_out, coupling.at[core], result_sems.at[0])]
-    results[0].start()
     factor_copy.wait_recv()
     factor = jnp.where(node // 2 == core, factor_out[...], factor_in[...])
-    basis_out[...] = 128.0 * lax.dot_general(
+    basis[...] = 128.0 * lax.dot_general(
         rows_here, factor, last, precision=HIGH, preferred_element_type=F32
     )
-    results.append(pltpu.make_async_copy(basis_out, basis, result_sems.at[1]))
-    results[1].start()
     factor_copy.wait_send()
     coupling_copy.wait()
-    for copy in results:
-        copy.wait()
 
     for copy in list(relays.values()) + nears + list(swap.values()) + small + sum(legs, []):
         copy.wait_send()
@@ -701,7 +696,7 @@
             jax.ShapeDtypeStruct((2, RANK, RANK), F32),
         ),
         in_specs=[HBM] * 6,
-        out_specs=(HBM,) * 2,
+        out_specs=(VMEM,) * 2,
         scratch_shapes=[
             block(FEATS, ROWS, kind=BF16), block(SAMPLES, ROWS, kind=BF16), block(1, ROWS, kind=i32),
             block(1, 16, kind=i32), block(1, 32, kind=i32), block(4, RANK, kind=i32), dma((6,)),
@@ -717,8 +712,8 @@
             block(2, 4, 2, 8, 128), block(2, 4, 4, 4, 8, 128), block(2, 4, 4, 4, 8, 128),
             dma((2, 4)), dma((2, 4)), dma((2, 2, 2)), dma((2, 2, 2, 2)), dma((2, 2)), dma((2, 32)), dma((2, 32)),
             dma((2, 8)), dma((2, 4, 2)), dma((2, 12)), dma((2, 12)),
-            block(2, RANK, RANK), block(2, RANK, RANK), block(RANK, RANK), block(RANK, RANK), block(RANK, RANK),
-            block(ROWS, RANK), dma((2,)), dma((2,)), dma((2,)),
+            block(2, RANK, RANK), block(2, RANK, RANK), block(RANK, RANK), block(RANK, RANK),
+            dma((2,)), dma((2,)),
         ],
         compiler_params=pltpu.CompilerParams(
             collective_id=0, has_side_effects=True, vmem_limit_bytes=VMEM_LIMIT
@@ -728,7 +723,8 @@
 
 
 def body(points, omega, tree_order, sibling_blocks, cousin_blocks, skeleton):
-    return whole(points, omega, tree_order.reshape(1, ROWS), sibling_blocks, cousin_blocks, skeleton)
+    arguments = (points, omega, tree_order.reshape(1, ROWS), sibling_blocks, cousin_blocks, skeleton)
+    return whole(*(pltpu.with_memory_space_constraint(argument, pltpu.HBM) for argument in arguments))
 
 
 def solution(mesh):

time: 86.4 us -> 83.9 us (0.971)
  Pallas kernels: 83 us -> 81.6 us
  local copies, waits for them, and re-layouts: 2.52 us -> 1.5 us
    pallas_call x1, Pallas kernels: 83 us -> 81.6 us  [whole(): pl.pallas_call(whole_kernel, out_shape=(jax.ShapeDtypeStruct((ROWS, RANK)...]
    unnamed x4 -> x2, local copies, waits for them, and re-layouts: 2.52 us -> 1.5 us
where the time goes in v8:
time: 83.9 us; the launch traced here: 83.7 us
  Pallas kernels  81.6 us (97%)
  local copies, waits for them, and re-layouts  1.5 us (2%)
    pallas_call x1, Pallas kernels, whole(): pl.pallas_call(whole_kernel, out_shape=(jax.ShapeDtypeStruct((ROWS, RANK)...  81.6 us

profile of v8, /device:TPU:1, one launch (start us, length us, event | category | flops | bytes accessed | tf_op | source)
XLA Modules:
  0.0 83.7 jit_solution(2467807327322850795)
XLA Ops:
  0.6 81.6 %whole.1 = (f32[256,256]{1,0:T(8,128)S(1)}, f32[2,256,256]{2,1,0:T(8,128)S(1)}) custom-call(bf16[8,256]{1,0:T(8,128)(2,1)} %points_in.1, bf16[128,256]{1,0:T(8,128)(2,1)} %omega_in.1, s32[1,256]{1,0:T(1,128)} %bitcast.1, s32[1,16]{1,0:T(1,128)} %siblings_in.1, s32[1,32]{1,0:T(1,128)} %cousins_in.1, s32[4,256]{1,0:T(4,128)} %skeleton_in.1), custom_call_target="tpu_custom_call" | custom-call | tf_op jit(solution)/shard_map/whole/pallas_call | solution.py:692
  82.2 0.7 copy.10
  83.0 0.8 copy.11

commit v9 on v8

--- a/solution.py
+++ b/solution.py
@@ -139,8 +139,8 @@
     points, omega, tree_order, siblings, cousins, skeleton, load_sems,
     blocks, row_points, lists, own, own_rows, own_lists, near_mask, far_mask, rows, even_tile, odd_tile, parts,
     hop_send, hop_recv, out_send, out_recv, far_send, far_recv, rows_send, rows_recv, list_send, list_recv,
-    other_core, relay_out, relay_in, near_out, near_in, table, sums, piece, pieces, landing, full_a, full_b,
-    core_send, core_recv, relay_sems, near_sems, table_sems, piece_send, piece_recv,
+    other_core, shipped, received, table, sums, piece, pieces, landing, full_a, full_b,
+    core_send, core_recv, ship_sems, table_sems, piece_send, piece_recv,
     z_send, z_recv, y_sems, x_sems,
     work, chosen, factor_out, factor_in, factor_sems, coupling_sems,
 ):
@@ -371,42 +371,17 @@
         at = order[step][kind]
         return parts[core, kind, at] + other_core[kind, at]
 
-    forward, backward = (right, above), (left_side, below)
-    lower, upper = pl.ds(0, 128), pl.ds(128, 128)
-    relays, nears = {}, []
-
-    def pass_on(kind, side, first, rows_of, who):
-        ref = near_out.at[kind, side, rows_of]
-        target = near_in.at[kind, side, rows_of]
-        nears.append(send(ref, target, near_sems.at[0, kind, side, first], near_sems.at[1, kind, side, first], who))
-
-    def start_sum(kind):
-        relay_out[kind] = partial(0, kind).astype(LINK)
-        for side, (rows_of, who) in enumerate(((lower, forward[kind]), (upper, backward[kind]))):
-            relays[kind, side] = send(
-                relay_out.at[kind, rows_of], relay_in.at[kind, side],
-                relay_sems.at[0, kind, side], relay_sems.at[1, kind, side], who,
+    ships = []
+
+    def ship(step, kind):
+        shipped[kind, step] = partial(step, kind).astype(LINK)
+        who = (along_x, along_y)[kind][(2, 1, 3)[step]]
+        ships.append(
+            send(
+                shipped.at[kind, step], received.at[kind, step],
+                ship_sems.at[0, kind, step], ship_sems.at[1, kind, step], who,
             )
-
-    def middle_sum(kind, side):
-        near_out[kind, side] = partial(1 + side, kind).astype(LINK)
-        pass_on(kind, side, 0, (upper, lower)[side], (forward, backward)[side][kind])
-
-    def end_sum(kind):
-        relays[kind, 0].wait_recv()
-        near_out[kind, 0, 0:128, :] = (
-            parts[core, kind, order[1][kind], 0:128, :]
-            + other_core[kind, order[1][kind], 0:128, :]
-            + relay_in[kind, 0].astype(F32)
-        ).astype(LINK)
-        pass_on(kind, 0, 1, lower, forward[kind])
-        relays[kind, 1].wait_recv()
-        near_out[kind, 1, 128:256, :] = (
-            parts[core, kind, order[2][kind], 128:256, :]
-            + other_core[kind, order[2][kind], 128:256, :]
-            + relay_in[kind, 1].astype(F32)
-        ).astype(LINK)
-        pass_on(kind, 1, 1, upper, backward[kind])
+        )
 
     for step in range(4):
         give(step, 1)
@@ -420,18 +395,15 @@
             give(step, 0)
 
     last_batch(0)
-    start_sum(1)
-    middle_sum(1, 0)
-    middle_sum(1, 1)
+    for step in range(3):
+        ship(step, 1)
     last_batch(1)
-    start_sum(0)
-    end_sum(1)
+    ship(0, 0)
     last_batch(2)
-    middle_sum(0, 0)
-    last_batch(3, 0, 3)
-    middle_sum(0, 1)
-    end_sum(0)
-    last_batch(3, 3, 2)
+    ship(1, 0)
+    last_batch(3, 0, 2)
+    ship(2, 0)
+    last_batch(3, 2, 3)
     total = partial(3, 1) + partial(3, 0)
     first_row = (leaf * 2 + core) * ROWS
     row = lax.broadcasted_iota(jnp.int32, (ROWS, RANK), 0) + first_row
@@ -439,11 +411,11 @@
     own_skeleton = jnp.dot(
         mine.astype(BF16), picked.astype(BF16), preferred_element_type=F32
     )
-    for copy in nears:
+    for copy in ships:
         copy.wait_recv()
     for kind in range(2):
-        for side in range(2):
-            total = total + near_in[kind, side].astype(F32)
+        for step in range(3):
+            total = total + received[kind, step].astype(F32)
     rows_here = total
 
     def product(c, first):
@@ -546,6 +518,7 @@
     legs = [first_leg(0)]
     legs.append(second_leg(0, legs[0]))
     legs.append(first_leg(1))
+    legs.append(second_leg(1, legs[2]))
     for copy in legs[1]:
         copy.wait_recv()
 
@@ -629,9 +602,7 @@
                     precision=HIGH, preferred_element_type=F32,
                 )
                 work[n, top + 64 :, :] = jnp.where(tcol // 64 == p, 0.0, work[n, top + 64 :, :]) - update
-        if p == 0:
-            legs.append(second_leg(1, legs[2]))
-        if p == 2:
+        if p == 1:
             for copy in legs[3]:
                 copy.wait_recv()
             for n in range(2):
@@ -665,7 +636,7 @@
     factor_copy.wait_send()
     coupling_copy.wait()
 
-    for copy in list(relays.values()) + nears + list(swap.values()) + small + sum(legs, []):
+    for copy in ships + list(swap.values()) + small + sum(legs, []):
         copy.wait_send()
     for c in range(2):
         swaps[c].wait_send()
@@ -706,11 +677,10 @@
             block(2 * ROWS, 2 * ROWS, kind=BF16), block(2 * ROWS, 2 * ROWS, kind=BF16), block(2, 2, 4, ROWS, RANK),
             dma((8, 2)), dma((8, 2)), dma((6, 2, 2)), dma((6, 2, 2)), dma((6, 2)), dma((6, 2)),
             dma((2, 4)), dma((2, 4)), dma((2, 4)), dma((2, 4)),
-            block(2, 4, ROWS, RANK), block(2, ROWS, RANK, kind=LINK), block(2, 2, 128, RANK, kind=LINK),
-            block(2, 2, ROWS, RANK, kind=LINK), block(2, 2, ROWS, RANK, kind=LINK),
+            block(2, 4, ROWS, RANK), block(2, 3, ROWS, RANK, kind=LINK), block(2, 3, ROWS, RANK, kind=LINK),
             block(2, 2, RANK, 128), block(2, RANK, 128), block(2, 8, 128), block(2, 32, 8, 128),
             block(2, 4, 2, 8, 128), block(2, 4, 4, 4, 8, 128), block(2, 4, 4, 4, 8, 128),
-            dma((2, 4)), dma((2, 4)), dma((2, 2, 2)), dma((2, 2, 2, 2)), dma((2, 2)), dma((2, 32)), dma((2, 32)),
+            dma((2, 4)), dma((2, 4)), dma((2, 2, 3)), dma((2, 2)), dma((2, 32)), dma((2, 32)),
             dma((2, 8)), dma((2, 4, 2)), dma((2, 12)), dma((2, 12)),
             block(2, RANK, RANK), block(2, RANK, RANK), block(RANK, RANK), block(RANK, RANK),
             dma((2,)), dma((2,)),

time: 83.9 us -> 82 us (0.977)
  Pallas kernels: 81.6 us -> 79.7 us
    pallas_call x1, Pallas kernels: 81.6 us -> 79.7 us  [whole(): pl.pallas_call(whole_kernel, out_shape=(jax.ShapeDtypeStruct((ROWS, RANK)...]
where the time goes in v9:
time: 82 us; the launch traced here: 81.9 us
  Pallas kernels  79.7 us (97%)
  local copies, waits for them, and re-layouts  1.5 us (2%)
    pallas_call x1, Pallas kernels, whole(): pl.pallas_call(whole_kernel, out_shape=(jax.ShapeDtypeStruct((ROWS, RANK)...  79.7 us

profile of v9, /device:TPU:1, one launch (start us, length us, event | category | flops | bytes accessed | tf_op | source)
XLA Modules:
  0.0 81.9 jit_solution(9425987237817163135)
XLA Ops:
  0.6 79.7 %whole.1 = (f32[256,256]{1,0:T(8,128)S(1)}, f32[2,256,256]{2,1,0:T(8,128)S(1)}) custom-call(bf16[8,256]{1,0:T(8,128)(2,1)} %points_in.1, bf16[128,256]{1,0:T(8,128)(2,1)} %omega_in.1, s32[1,256]{1,0:T(1,128)} %bitcast.1, s32[1,16]{1,0:T(1,128)} %siblings_in.1, s32[1,32]{1,0:T(1,128)} %cousins_in.1, s32[4,256]{1,0:T(4,128)} %skeleton_in.1), custom_call_target="tpu_custom_call" | custom-call | tf_op jit(solution)/shard_map/whole/pallas_call | solution.py:663
  80.4 0.7 copy.10
  81.1 0.8 copy.11

commit v10 on v9

--- a/solution.py
+++ b/solution.py
@@ -301,28 +301,34 @@
         parts[0, kind, at] += terms[0:ROWS]
         parts[1, kind, at] += terms[ROWS:]
 
-    def batch(kind, count, item):
-        at, use = item(0)
-        kernel_tile(kind * 4 + at, use, even_tile)
+    def batch(kind, count, item, tiles=(even_tile, odd_tile), primed=False, following=None):
+        now, later = tiles
+        if not primed:
+            at, use = item(0)
+            kernel_tile(kind * 4 + at, use, now)
 
         def two_steps(step, carry):
             at0, use0 = item(2 * step)
             at1, use1 = item(2 * step + 1)
             at2, use2 = item(2 * step + 2)
-            kernel_tile(kind * 4 + at1, use1, odd_tile)
-            add(kind, at0, use0, even_tile)
-            kernel_tile(kind * 4 + at2, use2, even_tile)
-            add(kind, at1, use1, odd_tile)
+            kernel_tile(kind * 4 + at1, use1, later)
+            add(kind, at0, use0, now)
+            kernel_tile(kind * 4 + at2, use2, now)
+            add(kind, at1, use1, later)
             return carry
 
-        lax.fori_loop(0, (count - 1) // 2, two_steps, 0)
-        if count % 2:
-            add(kind, *item(count - 1), even_tile)
-        else:
+        if count > 2:
+            lax.fori_loop(0, (count - 1) // 2, two_steps, 0)
+        if count % 2 == 0:
             at, use = item(count - 1)
-            kernel_tile(kind * 4 + at, use, odd_tile)
-            add(kind, *item(count - 2), even_tile)
-            add(kind, at, use, odd_tile)
+            kernel_tile(kind * 4 + at, use, later)
+            add(kind, *item(count - 2), now)
+            now, later = later, now
+        if following is not None:
+            at, use = following
+            kernel_tile(kind * 4 + at, use, later)
+        add(kind, *item(count - 1), now)
+        return later, now
 
     batch(1, 4, lambda i: (i, 0))
     relay(0, MATE)
@@ -388,22 +394,23 @@
     landed(2, 3, 5)
     passed(2, 3, 5)
 
-    def last_batch(step, first=0, count=5):
+    def last_batch(step, first, count, tiles, primed, following):
         at = order[step][0]
-        batch(0, count, lambda i: (at, 7 + first + i))
+        tiles = batch(0, count, lambda i: (at, 7 + first + i), tiles, primed, following)
         if first + count == 5:
             give(step, 0)
-
-    last_batch(0)
+        return tiles
+
+    tiles = last_batch(0, 0, 5, (even_tile, odd_tile), False, (order[1][0], 7))
     for step in range(3):
         ship(step, 1)
-    last_batch(1)
+    tiles = last_batch(1, 0, 5, tiles, True, (order[2][0], 7))
     ship(0, 0)
-    last_batch(2)
+    tiles = last_batch(2, 0, 5, tiles, True, (order[3][0], 7))
     ship(1, 0)
-    last_batch(3, 0, 2)
+    tiles = last_batch(3, 0, 2, tiles, True, (order[3][0], 9))
     ship(2, 0)
-    last_batch(3, 2, 3)
+    last_batch(3, 2, 3, tiles, True, None)
     total = partial(3, 1) + partial(3, 0)
     first_row = (leaf * 2 + core) * ROWS
     row = lax.broadcasted_iota(jnp.int32, (ROWS, RANK), 0) + first_row

time: 82 us -> 81.9 us (level)
  no operation moved by 1% of the time
where the time goes in v10:
time: 81.9 us; the launch traced here: 81.7 us
  Pallas kernels  79.6 us (97%)
  local copies, waits for them, and re-layouts  1.5 us (2%)
    pallas_call x1, Pallas kernels, whole(): pl.pallas_call(whole_kernel, out_shape=(jax.ShapeDtypeStruct((ROWS, RANK)...  79.6 us

profile of v10, /device:TPU:1, one launch (start us, length us, event | category | flops | bytes accessed | tf_op | source)
XLA Modules:
  0.0 81.7 jit_solution(8879388020868433325)
XLA Ops:
  0.6 79.6 %whole.1 = (f32[256,256]{1,0:T(8,128)S(1)}, f32[2,256,256]{2,1,0:T(8,128)S(1)}) custom-call(bf16[8,256]{1,0:T(8,128)(2,1)} %points_in.1, bf16[128,256]{1,0:T(8,128)(2,1)} %omega_in.1, s32[1,256]{1,0:T(1,128)} %bitcast.1, s32[1,16]{1,0:T(1,128)} %siblings_in.1, s32[1,32]{1,0:T(1,128)} %cousins_in.1, s32[4,256]{1,0:T(4,128)} %skeleton_in.1), custom_call_target="tpu_custom_call" | custom-call | tf_op jit(solution)/shard_map/whole/pallas_call | solution.py:670
  80.2 0.7 copy.10
  80.9 0.8 copy.11
